TPU v7x, 32 devices: a whole 2x2x4 slice. The times are simulated.
32 devices in a mesh: group: 8 (over z, x), expert: 4 (over y, core).
Axes of the slice: x: 2, y: 2, z: 4, core: 2. Of those that a mesh axis runs over, the one named last changes fastest.
Arguments:
- hidden_in: bfloat16 [8192, 2048], P(('group', 'expert')), may hold values from -54 to 54
- norm_attention: float32 [2048], replicated, may hold values from 0.5 to 1.5
- norm_experts: float32 [2048], replicated, may hold values from 0.5 to 1.5
- query_master: float32 [2048, 4096], P('group', 'expert'), may hold values from -0.125 to 0.125
- trainer_key_value_weight: float32 [2, 2048, 512], P(None, 'group'), may hold values from -0.125 to 0.125
- output_master: float32 [4096, 2048], P('expert', 'group'), may hold values from -0.09375 to 0.09375
- query_gain: float32 [128], replicated, may hold values from 0.5 to 1.5
- key_gain: float32 [128], replicated, may hold values from 0.5 to 1.5
- lengths: int32 [4], replicated, may hold values from 1 to 2048, as said below
- router: bfloat16 [2048, 128], replicated, may hold values from -0.125 to 0.125
- expert_gateup: bfloat16 [4, 2048, 1536], P('expert'), may hold values from -0.125 to 0.125
- expert_down: bfloat16 [4, 768, 2048], P('expert'), may hold values from -0.21875 to 0.21875
- routes: int32 [8192, 8], P(('group', 'expert')), may hold values from 0 to 127, as said below
Outputs:
- hidden: bfloat16 [8192, 2048], P(('group', 'expert'))
- expert_mix: bfloat16 [8192, 2048], P(('group', 'expert'))
Inputs may be any that keep to these rules, and one draw needn't show every extreme that they name: `lengths`: one request has exactly 2048 valid tokens. `routes`: A row's 8 experts are different, and at most one of them is below 4. In the 256 rows of one device, each expert below 4 is named by at most 64 rows; in every such block some expert is named by exactly 64 rows, and one expert is named by exactly 64 rows in every block.
All inputs are finite; a program needn't handle non-finite values.
Results may differ from a plain program's by a relative error of at most 0.02.
Values may be sent and summed in bfloat16 or wider, within the bound.
No kernel may reach another device: no remote copies, remote signals or barrier semaphores. Data moves between devices by JAX's collectives and lax.ppermute only.
A program may use at most 128 MiB of HBM per device.

v0:
```python
import math

import jax
import jax.numpy as jnp
from jax import lax
from jax.sharding import PartitionSpec as P

QUERY_HEADS = 32
KEY_VALUE_HEADS = 4
HEAD_DIMENSION = 128


epsilon = 1e-06
rope_theta = 1000000.0


def from_partner(block, axis, stride):
    count = lax.axis_size(axis)
    route = []
    for low in range(count):
        high = low | 1 << stride
        if high != low and high < count:
            route += [(low, high), (high, low)]
    return lax.ppermute(block, axis, route)


def norm_rows(values, gain_vector):
    widened = values.astype(jnp.float32)
    inverse_rms = lax.rsqrt(jnp.mean(widened * widened, axis=-1, keepdims=True) + epsilon)
    return widened * inverse_rms * gain_vector


def rotate(values, positions):
    half_width = values.shape[-1] // 2
    exponents = jnp.arange(half_width).astype(jnp.float32)
    inverse = jnp.exp(exponents * (-2.0 * math.log(rope_theta) / values.shape[-1]))
    angles = positions[:, None, None] * inverse[None, None, :]
    cosine_values = jnp.cos(angles)
    sine_values = jnp.sin(angles)
    first_half = values[..., :half_width]
    second = values[..., half_width:]
    return jnp.concatenate(
        [
            first_half * cosine_values - second * sine_values,
            second * cosine_values + first_half * sine_values,
        ],
        axis=-1,
    )


def local_positions(parity, row_count):
    indices = jnp.arange(row_count)
    quarter = row_count // 2
    offset = jnp.where(parity == 0, jnp.where(indices < quarter, 0, 2 * quarter), quarter)
    return indices + offset


def per_device(
    hidden_in,
    norm_attention,
    norm_experts,
    query_master,
    trainer_key_value_weight,
    output_master,
    query_gain,
    key_gain,
    lengths,
    router,
    expert_gateup,
    expert_down,
    routes,
):
    experts_axis = lax.axis_size("expert")
    group_member = lax.axis_index("expert")
    group_index = lax.axis_index("group")
    local_head_count = QUERY_HEADS // experts_axis
    width_here = local_head_count * HEAD_DIMENSION
    common_head = group_member * local_head_count // (QUERY_HEADS // KEY_VALUE_HEADS)
    keyvalue_slice = lax.dynamic_slice_in_dim(
        trainer_key_value_weight, common_head * HEAD_DIMENSION, HEAD_DIMENSION, 2
    ).astype(jnp.bfloat16)
    query_full, keyvalue_full, output_part = (
        lax.all_gather(query_master.astype(jnp.bfloat16), "group", axis=0, tiled=True),
        lax.all_gather(keyvalue_slice, "group", axis=1, tiled=True),
        lax.all_gather(output_master.astype(jnp.bfloat16), "group", axis=1, tiled=True),
    )
    joined_weights = jnp.concatenate([query_full, keyvalue_full[0], keyvalue_full[1]], axis=1)
    normed = norm_rows(hidden_in, norm_attention).astype(jnp.bfloat16)
    projected = jnp.dot(
        lax.all_gather(normed, "expert", axis=0, tiled=True),
        joined_weights,
        preferred_element_type=jnp.float32,
    ).astype(jnp.bfloat16)
    local_rows = projected.shape[0]
    query_rows_list = projected[:, :width_here].reshape(
        local_rows, local_head_count, HEAD_DIMENSION
    )
    key_rows = projected[:, width_here : width_here + HEAD_DIMENSION]
    value_rows = projected[:, width_here + HEAD_DIMENSION :]
    parity = group_index % 2
    own_places = local_positions(parity, local_rows)
    partner_places = local_positions(1 - parity, local_rows)
    query_rows_list = rotate(
        norm_rows(query_rows_list, query_gain), own_places.astype(jnp.float32)
    ).astype(jnp.bfloat16)
    key_rows = rotate(norm_rows(key_rows[:, None, :], key_gain), own_places.astype(jnp.float32))[
        :, 0, :
    ].astype(jnp.bfloat16)
    partner = from_partner(jnp.stack([key_rows, value_rows]), "group", 0)
    all_keys = jnp.concatenate([key_rows, partner[0]], axis=0)
    all_values = jnp.concatenate([value_rows, partner[1]], axis=0)
    key_places = jnp.concatenate([own_places, partner_places])
    valid_length = jnp.sum(jnp.where(jnp.arange(lengths.shape[0]) == group_index // 2, lengths, 0))
    block_rows = min(512, local_rows)
    block_count = local_rows // block_rows
    score_scale = HEAD_DIMENSION ** (-0.5)

    def attend(block_index):
        block_start = block_index * block_rows
        query_block = lax.dynamic_slice_in_dim(query_rows_list, block_start, block_rows, 0)
        query_places = lax.dynamic_slice_in_dim(own_places, block_start, block_rows, 0)
        scores = (
            jnp.einsum("qhd,kd->hqk", query_block, all_keys, preferred_element_type=jnp.float32)
            * score_scale
        )
        allowed = (key_places[None, :] <= query_places[:, None]) & (
            key_places[None, :] < valid_length
        )
        weights = jnp.where(allowed[None], jnp.exp(scores), 0.0)
        denominators = jnp.sum(weights, axis=-1)
        weighted = jnp.einsum(
            "hqk,kd->qhd",
            weights.astype(jnp.bfloat16),
            all_values,
            preferred_element_type=jnp.float32,
        )
        return (weighted / jnp.transpose(denominators)[:, :, None]).astype(jnp.bfloat16)

    attended = lax.map(attend, jnp.arange(block_count)).reshape(local_rows, width_here)
    summed = lax.psum_scatter(
        jnp.dot(attended, output_part, preferred_element_type=jnp.float32).astype(jnp.bfloat16),
        "expert",
        scatter_dimension=0,
        tiled=True,
    ).astype(jnp.float32)
    hidden = (hidden_in.astype(jnp.float32) + summed).astype(jnp.bfloat16)
    normed_second = norm_rows(hidden, norm_experts).astype(jnp.bfloat16)
    logits = jnp.dot(normed_second, router, preferred_element_type=jnp.float32)
    route_table = routes[:, :, None] == jnp.arange(logits.shape[1])[None, None, :]
    picked = jnp.sum(jnp.where(route_table, logits[:, None, :], 0.0), axis=-1)
    raised = jnp.exp(picked)
    gate_values = raised / jnp.sum(raised, axis=1, keepdims=True)
    inside = routes < experts_axis
    gate_window = jnp.sum(jnp.where(inside, gate_values, 0.0), axis=1)
    expert_window = jnp.sum(jnp.where(inside, routes, 0), axis=1)
    present = jnp.any(inside, axis=1)
    capacity = local_rows // (experts_axis * experts_axis)
    member_table = (
        present[:, None] & (expert_window[:, None] == jnp.arange(experts_axis)[None, :])
    ).astype(jnp.int32)
    ranking = jnp.sum(jnp.cumsum(member_table, axis=0) * member_table, axis=1) - 1
    slot_index = expert_window * capacity + ranking
    select = (
        (jnp.arange(experts_axis * capacity)[:, None] == slot_index[None, :]) & present[None, :]
    ).astype(jnp.bfloat16)
    model_width = normed_second.shape[1]
    outgoing = (
        jnp.dot(select, normed_second, preferred_element_type=jnp.float32)
        .astype(jnp.bfloat16)
        .reshape(experts_axis, capacity, model_width)
    )
    gateup_here = expert_gateup[0]
    down_here = expert_down[0]
    hidden_units = down_here.shape[0]
    slot_items = lax.all_to_all(outgoing, "expert", split_axis=0, concat_axis=0, tiled=True)
    flattened = slot_items.reshape(-1, slot_items.shape[-1])
    gate_up = jnp.dot(flattened, gateup_here, preferred_element_type=jnp.float32)
    active = (jax.nn.silu(gate_up[:, :hidden_units]) * gate_up[:, hidden_units:]).astype(
        jnp.bfloat16
    )
    result = (
        jnp.dot(active, down_here, preferred_element_type=jnp.float32)
        .astype(jnp.bfloat16)
        .reshape(slot_items.shape)
    )
    returned = lax.all_to_all(result, "expert", split_axis=0, concat_axis=0, tiled=True)
    combined = jnp.dot(
        jnp.transpose(select), returned.reshape(-1, model_width), preferred_element_type=jnp.float32
    )
    expert_mix = (gate_window[:, None] * combined).astype(jnp.bfloat16)
    return (hidden, expert_mix)


def solution(mesh):
    return jax.shard_map(
        per_device,
        mesh=mesh,
        in_specs=(
            P(("group", "expert"), None),
            P(),
            P(),
            P("group", "expert"),
            P(None, "group", None),
            P("expert", "group"),
            P(),
            P(),
            P(),
            P(),
            P("expert", None, None),
            P("expert", None, None),
            P(("group", "expert"), None),
        ),
        out_specs=(P(("group", "expert"), None), P(("group", "expert"), None)),
        check_vma=False,
    )
```

profile of v0, /device:TPU:0, one launch (start us, length us, event | category | flops | bytes accessed | tf_op | source)
XLA Modules:
  0.0 372.8 jit_solution(2640574707530155596)
XLA Ops:
  7.2 1.8 dynamic-slice_convert_fusion
  9.1 1.5 fusion.32
  10.6 2.5 fusion.34
  13.2 2.1 convert_element_type.105
  15.4 2.1 convert_element_type.116
  17.7 3.1 multiply_cosine_fusion.1
  21.4 31.7 %all-gather.9.cloned.1.call-done = bf16[2,2048,128]{2,1,0:T(8,128)(2,1)} async-done(((bf16[2,256,128]{2,1,0:T(8,128)(2,1)}), bf16[2,2048,128]{2,1,0:T(8,128)(2,1)}) %all-gather.9.cloned.1.call-update) | async-done | bytes 1048592 | tf_op jit(solution)/shard_map/all_gather | solution.py:84
  53.1 2.2 slice_bitcast_fusion.1
  55.4 33.2 %all-gather.5.cloned.1.call-done = bf16[1024,2048]{1,0:T(8,128)(2,1)} async-done(((bf16[256,2048]{1,0:T(8,128)(2,1)}), bf16[1024,2048]{1,0:T(8,128)(2,1)}) %all-gather.5.cloned.1.call-update) | async-done | bytes 4194320 | tf_op jit(solution)/shard_map/all_gather | solution.py:90
  88.6 75.6 %all-gather.7.cloned.1.call-done = bf16[2048,1024]{1,0:T(8,128)(2,1)} async-done(((bf16[256,1024]{1,0:T(8,128)(2,1)}), bf16[2048,1024]{1,0:T(8,128)(2,1)}) %all-gather.7.cloned.1.call-update) | async-done | bytes 4194320 | tf_op jit(solution)/shard_map/all_gather | solution.py:83
  164.1 9.4 %fusion.20 = bf16[1024,1280]{1,0:T(8,128)(2,1)S(1)} fusion(bf16[1024,2048]{1,0:T(8,128)(2,1)} %all-gather.5.cloned.1.call-done, bf16[2048,128]{1,0:T(8,128)(2,1)} %get-tuple-element.79, bf16[2048,128]{1,0:T(8,128)(2,1)} %get-tuple-element.78, bf16[2048,1024]{1,0:T(8,128)(2,1)} %all-gather.7.cloned.1.call-done), kind=kOutput, calls=%fused_computation.33 | convolution fusion | flops 5385748480 | bytes 12058624 | tf_op jit(solution)/shard_map/dot_general | solution.py:89
  174.0 2.4 fusion.46
  176.6 0.9 fusion.73
  177.4 2.5 convert_bitcast_fusion.1
  179.9 0.8 pad_maximum_fusion.1
  181.3 1.0 copy.49
  182.3 1.9 multiply_reduce_fusion
  184.3 1.2 copy.38
  185.6 3.9 %fusion.19 = f32[1024,8,128]{2,0,1:T(8,128)S(1)} fusion(f32[128,8,8,128]{3,2,1,0:T(8,128)} %get-tuple-element.77, f32[128]{0:T(128)S(1)} %copy-done.7, f32[1024,8]{0,1:T(8,128)S(1)} %add_rsqrt_fusion), kind=kLoop, calls=%fused_computation.29 | loop fusion | flops 2097152 | bytes 8421888 | tf_op jit(solution)/shard_map/mul | solution.py:30
  189.5 1.5 subtract_convert_fusion
  191.0 2.5 pad_maximum_fusion
  193.6 1.1 slice_bitcast_fusion.2
  194.6 1.1 pad_maximum_fusion.2
  195.7 68.4 %while.10 = (s32[]{:T(128)}, bf16[2,512,8,128]{3,2,1,0:T(8,128)(2,1)}, s32[2048]{0:T(1024)S(1)}, s32[2]{0:T(128)S(1)}, s32[1024]{0:T(1024)S(1)}, /*index=5*/s32[...) while((s32[]{:T(128)}, ...), condition=%wide.region_6.7_spmd, body=%wide.region_4.6_spmd.sunk | while | flops 4348442624 | bytes 77654752 | solution.py:139
  195.7 0.7 dynamic_slice.23
  197.8 0.7 compare_and_fusion.2
  198.5 16.3 %bitcast_reduce_fusion.2 = (f32[8,512]{1,0:T(8,128)S(1)}, f32[512,8,2048]{2,0,1:T(8,128)}) fusion(pred[512,2048]{1,0:T(8,128)(4,1)S(1)} %compare_and_fusion.2, bf16[2048,128]{1,0:T(8,128)(2,1)} %get-tuple-element.182, bf16[1024,8,128]{2,0,1:T(8,128)(2,1)} %get-tuple-element.181, s32[]{:T(128)S(6)} %select_n.127), kind=kOutput, calls=%fused_computation.clone.1 | convolution fusion | flops 2172645376 | bytes 36192260 | tf_op jit(solution)/shard_map/while/body/eval_jaxpr/qhd,kd->hqk/dot_general | solution.py:123
  214.8 13.5 %fusion.82 = bf16[1,512,8,128]{3,1,2,0:T(8,128)(2,1)S(1)} fusion(f32[512,8,2048]{2,0,1:T(8,128)} %get-tuple-element.147, pred[512,2048]{1,0:T(8,128)(4,1)S(1)} %compare_and_fusion.2, f32[512,8]{0,1:T(8,128)S(1)} %bitcast.113, bf16[2048,128]{1,0:T(8,128)(2,1)S(1)} %copy-done.5), kind=kOutput, calls=%fused_computation.8.clone.1 | convolution fusion | flops 2173698048 | bytes 36192256 | tf_op jit(solution)/shard_map/while/body/eval_jaxpr/hqk,kd->qhd/dot_general | solution.py:131
  228.3 1.7 copy_dynamic-update-slice_fusion.2
  230.0 0.7 dynamic_slice.23
  232.1 0.7 compare_and_fusion.2
  232.8 16.2 %bitcast_reduce_fusion.2 = (f32[8,512]{1,0:T(8,128)S(1)}, f32[512,8,2048]{2,0,1:T(8,128)}) fusion(pred[512,2048]{1,0:T(8,128)(4,1)S(1)} %compare_and_fusion.2, bf16[2048,128]{1,0:T(8,128)(2,1)} %get-tuple-element.182, bf16[1024,8,128]{2,0,1:T(8,128)(2,1)} %get-tuple-element.181, s32[]{:T(128)S(6)} %select_n.127), kind=kOutput, calls=%fused_computation.clone.1 | convolution fusion | flops 2172645376 | bytes 36192260 | tf_op jit(solution)/shard_map/while/body/eval_jaxpr/qhd,kd->hqk/dot_general | solution.py:123
  249.1 13.4 %fusion.82 = bf16[1,512,8,128]{3,1,2,0:T(8,128)(2,1)S(1)} fusion(f32[512,8,2048]{2,0,1:T(8,128)} %get-tuple-element.147, pred[512,2048]{1,0:T(8,128)(4,1)S(1)} %compare_and_fusion.2, f32[512,8]{0,1:T(8,128)S(1)} %bitcast.113, bf16[2048,128]{1,0:T(8,128)(2,1)S(1)} %copy-done.5), kind=kOutput, calls=%fused_computation.8.clone.1 | convolution fusion | flops 2173698048 | bytes 36192256 | tf_op jit(solution)/shard_map/while/body/eval_jaxpr/hqk,kd->qhd/dot_general | solution.py:131
  262.5 1.6 copy_dynamic-update-slice_fusion.2
  264.1 9.2 %convolution_convert_fusion = bf16[1024,2048]{1,0:T(8,128)(2,1)} fusion(bf16[1024,2048]{1,0:T(8,128)(2,1)} %all-gather.11.cloned.1.call-done, bf16[128,8,8,128]{3,2,1,0:T(8,128)(2,1)} %bitcast.30), kind=kOutput, calls=%fused_computation.34 | convolution fusion | flops 4297064448 | bytes 10485760 | tf_op jit(solution)/shard_map/dot_general | solution.py:141
  273.4 0.7 copy-done.6
  274.4 1.2 reduce-window.6
  276.1 41.6 %reduce-scatter.2.cloned.1.call-done = bf16[256,2048]{1,0:T(8,128)(2,1)} async-done(((bf16[1024,2048]{1,0:T(8,128)(2,1)}), bf16[256,2048]{1,0:T(8,128)(2,1)}) %reduce-scatter.2.cloned.1.call-update) | async-done | bytes 1048592 | tf_op jit(solution)/shard_map/reduce_scatter | solution.py:140
  317.7 2.0 fusion.29
  319.8 1.0 copy-done.3
  321.3 16.9 %all_to_all.10 = bf16[4,64,2048]{2,1,0:T(8,128)(2,1)S(1)} all-to-all(bf16[4,64,2048]{2,1,0:T(8,128)(2,1)S(1)} %bitcast.109), channel_id=1, replica_groups=mesh['group'=8,'expert'=4] {'expert'}, dimensions={0} | all-to-all | bytes 2097152 | tf_op jit(solution)/shard_map/all_to_all | solution.py:175
  338.2 4.6 %fusion.11 = f32[256,1536]{1,0:T(8,128)S(1)} fusion(bf16[256,2048]{1,0:T(8,128)(2,1)S(1)} %bitcast.108, bf16[1,2048,1536]{2,1,0:T(8,128)(2,1)} %param.25), kind=kOutput, calls=%fused_computation.18 | convolution fusion | flops 1610612736 | bytes 8912896 | tf_op jit(solution)/shard_map/dot_general | solution.py:177
  342.8 2.0 fusion.26
  344.8 4.2 %all-to-all-start.1 = ((bf16[4,64,2048]{2,1,0:T(8,128)(2,1)}), bf16[4,64,2048]{2,1,0:T(8,128)(2,1)}, u32[]{:S(2)}, u32[]{:S(2)}) async-start(bf16[4,64,2048]{2,1,0:T(8,128)(2,1)} %bitcast.107), calls=%async_computation.2 | async-start | bytes 2097152 | tf_op jit(solution)/shard_map/all_to_all | solution.py:186
  349.1 1.9 fusion.51
  350.9 0.9 select_reduce_fusion
  352.1 11.5 %all-to-all-done.1 = bf16[4,64,2048]{2,1,0:T(8,128)(2,1)} async-done(((bf16[4,64,2048]{2,1,0:T(8,128)(2,1)}), bf16[4,64,2048]{2,1,0:T(8,128)(2,1)}, u32[]{:S(2)}, u32[]{:S(2)}) %all-to-all-start.1) | async-done | bytes 1048608 | tf_op jit(solution)/shard_map/all_to_all | solution.py:186
  363.6 2.7 fusion.25
  (69 shorter events, 5.4 us)
Async XLA Ops:
  7.2 335.6 %copy-start = (bf16[1,768,2048]{2,1,0:T(8,128)(2,1)S(1)}, bf16[1,768,2048]{2,1,0:T(8,128)(2,1)}, u32[]{:S(2)}) copy-start(bf16[1,768,2048]{2,1,0:T(8,128)(2,1)} %param.26) | copy-start | bytes 9437188
  7.2 46.0 %all-gather.9.cloned.1.call-start = ((), (), s32[]{:S(2)}) async-start(), calls=%async_computation.5 | async-start | bytes 1179648 | tf_op jit(solution)/shard_map/all_gather | solution.py:84
  9.1 79.5 %all-gather.5.cloned.1.call-start = ((), (), s32[]{:S(2)}) async-start(), calls=%async_computation.3 | async-start | bytes 5242880 | tf_op jit(solution)/shard_map/all_gather | solution.py:90
  10.6 10.1 %copy-start.10 = (s32[4]{0:T(128)S(1)}, s32[4]{0:T(128)}, u32[]{:S(2)}) copy-start(s32[4]{0:T(128)} %param.23) | copy-start | bytes 52
  13.2 150.9 %all-gather.7.cloned.1.call-start = ((), (), s32[]{:S(2)}) async-start(), calls=%async_computation.4 | async-start | bytes 4718592 | tf_op jit(solution)/shard_map/all_gather | solution.py:83
  15.4 248.7 %all-gather.11.cloned.1.call-start = ((), (), s32[]{:S(2)}) async-start(), calls=%async_computation.6 | async-start | bytes 4718592 | tf_op jit(solution)/shard_map/all_gather | solution.py:85
  17.5 300.2 %reduce-scatter.2.cloned.1.call-start = ((), (), s32[]{:S(2)}) async-start(), calls=%async_computation.7 | async-start | bytes 5242880 | tf_op jit(solution)/shard_map/reduce_scatter | solution.py:140
  164.1 9.7 %copy-start.8 = (f32[128]{0:T(128)S(1)}, f32[128]{0:T(128)}, u32[]{:S(2)}) copy-start(f32[128]{0:T(128)} %param.22) | copy-start | bytes 1540
  180.8 12.8 %collective-permute-start = (bf16[2,1024,128]{2,1,0:T(8,128)(2,1)}, bf16[2,1024,128]{2,1,0:T(8,128)(2,1)}, u32[]{:S(2)}, u32[]{:S(2)}) collective-permute-start(bf16[2,1024,128]{2,1,0:T(8,128)(2,1)} %pad_maximum_fusion.1), channel_id=1, source_target_pairs={{0,4},{4,0},{8,12},{12,8},{16,20},{20,16},{24,28},{28,24},{1,5},{5... | collective-permute-start | bytes 1572872 | tf_op jit(solution)/shard_map/ppermute | solution.py:24
  182.3 3.2 copy-start.7
  185.5 3.9 %copy-start.1 = (f32[1024,64]{1,0:T(8,128)S(1)}, f32[1024,64]{1,0:T(8,128)}, u32[]{:S(2)}) copy-start(f32[1024,64]{1,0:T(8,128)} %get-tuple-element.84) | copy-start | bytes 786436
  185.5 3.9 %copy-start.2 = (f32[1024,64]{1,0:T(8,128)S(1)}, f32[1024,64]{1,0:T(8,128)}, u32[]{:S(2)}) copy-start(f32[1024,64]{1,0:T(8,128)} %get-tuple-element.85) | copy-start | bytes 786436
  191.0 3.7 copy-start.4
  198.5 16.3 %copy-start.5 = (bf16[2048,128]{1,0:T(8,128)(2,1)S(1)}, bf16[2048,128]{1,0:T(8,128)(2,1)}, u32[]{:S(2)}) copy-start(bf16[2048,128]{1,0:T(8,128)(2,1)} %get-tuple-element.183) | copy-start | bytes 1572868 | tf_op jit(solution)/shard_map/while
  232.8 16.2 %copy-start.5 = (bf16[2048,128]{1,0:T(8,128)(2,1)S(1)}, bf16[2048,128]{1,0:T(8,128)(2,1)}, u32[]{:S(2)}) copy-start(bf16[2048,128]{1,0:T(8,128)(2,1)} %get-tuple-element.183) | copy-start | bytes 1572868 | tf_op jit(solution)/shard_map/while
  273.4 0.7 copy-start.6
  273.4 47.4 %copy-start.9 = (f32[2048]{0:T(1024)S(1)}, f32[2048]{0:T(1024)}, u32[]{:S(2)}) copy-start(f32[2048]{0:T(1024)} %param.17) | copy-start | bytes 24580
  319.8 1.0 copy-start.3
  344.8 18.8 %all-to-all-start.1 = ((bf16[4,64,2048]{2,1,0:T(8,128)(2,1)}), bf16[4,64,2048]{2,1,0:T(8,128)(2,1)}, u32[]{:S(2)}, u32[]{:S(2)}) async-start(bf16[4,64,2048]{2,1,0:T(8,128)(2,1)} %bitcast.107), calls=%async_computation.2 | async-start | bytes 2097152 | tf_op jit(solution)/shard_map/all_to_all | solution.py:186
Sparse Core Ops, SparseCore 0:
  10.2 42.9 all-gather.8
  55.3 33.2 all-gather.4
  90.7 73.3 all-gather.6
  166.6 73.2 all-gather.10
  273.5 44.1 reduce-scatter.1
where the time goes:
time: 374 us; the launch traced here: 373 us
  waiting for transfers between devices  194 us (52%)
  matrix products  89.7 us (24%)
  other arithmetic  37.6 us (10%)
  blocking collectives  16.9 us (5%)
  local copies, waits for them, and re-layouts  14.2 us (4%)
  between operations  14.1 us (4%)
  starting transfers between devices  5 us (1%)
    all_gather x1, waiting for transfers between devices, per_device(): lax.all_gather(query_master.astype(jnp.bfloat16), 'group', axis=0, tiled=...  75.6 us
    reduce_scatter x1, waiting for transfers between devices, per_device(): lax.psum_scatter(jnp.dot(attended, output_part, preferred_element_type=jn...  41.6 us
    all_gather x1, waiting for transfers between devices, per_device(): lax.all_gather(normed, 'expert', axis=0, tiled=True)  33.2 us
    dot_general x2, matrix products, attend(): jnp.einsum('qhd,kd->hqk', query_block, all_keys, preferred_element_type=j...  32.5 us
    all_gather x1, waiting for transfers between devices, per_device(): lax.all_gather(keyvalue_slice, 'group', axis=1, tiled=True)  31.7 us
    dot_general x2, matrix products, attend(): jnp.einsum('hqk,kd->qhd', weights.astype(jnp.bfloat16), all_values, prefe...  26.9 us
    all_to_all x1, blocking collectives, per_device(): lax.all_to_all(outgoing, 'expert', split_axis=0, concat_axis=0, tiled=True)  16.9 us
    all_to_all x1, waiting for transfers between devices, per_device(): lax.all_to_all(result, 'expert', split_axis=0, concat_axis=0, tiled=True)  11.5 us
  transfers between devices with their start and end apart: 7, of which 6 were waited for; matrix products, arithmetic and copies ran while one was open for 31% of the time, Pallas kernels for 0%

commit v1 on v0

v1 whole, which is shorter than its diff:
```python
import functools
import math

import jax
import jax.numpy as jnp
from jax import lax
from jax.experimental import pallas as pl
from jax.experimental.pallas import tpu as pltpu
from jax.sharding import PartitionSpec as P

QUERY_HEADS = 32
KEY_VALUE_HEADS = 4
HEAD_DIMENSION = 128

epsilon = 1e-06
rope_theta = 1000000.0
VMEM_LIMIT = 56 * 1024 * 1024


def norm_rows(values, gain_vector):
    widened = values.astype(jnp.float32)
    inverse_rms = lax.rsqrt(jnp.mean(widened * widened, axis=-1, keepdims=True) + epsilon)
    return widened * inverse_rms * gain_vector


def local_positions(parity, row_count):
    indices = jnp.arange(row_count)
    quarter = row_count // 2
    offset = jnp.where(parity == 0, jnp.where(indices < quarter, 0, 2 * quarter), quarter)
    return indices + offset


def from_xor(block, axis, mask):
    count = lax.axis_size(axis)
    return lax.ppermute(block, axis, [(i, i ^ mask) for i in range(count)])


def gather_group(block):
    count = lax.axis_size("group")
    places = count // 2
    shards = {(0, 0): block}

    def cross(shard, step):
        route = [(i, i ^ 1) for i in range(count) if 0 <= i // 2 + step < places]
        return lax.ppermute(shard, "group", route)

    shards[1, 0] = cross(block, 0)
    above = below = block
    for step in range(1, places):
        above = lax.ppermute(above, "group", [(i, i - 2) for i in range(2, count)])
        below = lax.ppermute(below, "group", [(i, i + 2) for i in range(count - 2)])
        shards[0, step] = above
        shards[0, -step] = below
        shards[1, step] = cross(above, step)
        shards[1, -step] = cross(below, -step)
    return shards


def doubling_masks(count):
    masks, stride = [0], count // 2
    while stride:
        masks = masks + [mask ^ stride for mask in masks]
        stride //= 2
    return masks


def gather_tokens(rows):
    blocks = rows[None]
    stride = lax.axis_size("expert") // 2
    while stride:
        blocks = jnp.concatenate([blocks, from_xor(blocks, "expert", stride)], axis=0)
        stride //= 2
    return blocks


def scatter_sum(blocks):
    stride = 1
    while blocks.shape[0] > 1:
        half = blocks.shape[0] // 2
        arrived = from_xor(blocks[half:], "expert", stride)
        blocks = blocks[:half].astype(jnp.float32) + arrived.astype(jnp.float32)
        if half > 1:
            blocks = blocks.astype(jnp.bfloat16)
        stride *= 2
    return blocks[0]


def load_shards(place, side, places, keys, shard_refs, target, sem):
    for goal in range(places):
        for here in range(places):
            for offset in range(2):

                @pl.when(place == here)
                def _():
                    ref = shard_refs[keys.index((offset, goal - here))]
                    group = 2 * goal + (side ^ offset)
                    pltpu.make_async_copy(ref, target(group), sem).start()

    for group in range(2 * places):
        pltpu.make_async_copy(shard_refs[0], target(group), sem).wait()


def project_kernel(heads, places, keys, meta, rows, cosine, sine, gains, *rest):
    shard_refs = rest[: len(keys)]
    query_out, key_out, value_out, weights, sem = rest[len(keys) :]
    depth = shard_refs[0].shape[0]
    dim = HEAD_DIMENSION

    @pl.when(pl.program_id(0) == 0)
    def _():
        load_shards(
            meta[0], meta[1], places, keys, shard_refs,
            lambda group: weights.at[pl.ds(pl.multiple_of(group * depth, depth), depth)], sem,
        )

    projected = jnp.dot(rows[0], weights[...], preferred_element_type=jnp.float32)
    cosines, sines = cosine[...], sine[...]

    def turned(head, gain):
        values = projected[:, head * dim : (head + 1) * dim]
        inverse = lax.rsqrt(jnp.mean(values * values, axis=-1, keepdims=True) + epsilon)
        scaled = values * gain
        return ((scaled * cosines + pltpu.roll(scaled, dim // 2, 1) * sines) * inverse).astype(
            jnp.bfloat16
        )

    for head in range(heads):
        query_out[head] = turned(head, gains[0:1, :])
    key_out[...] = turned(heads, gains[1:2, :])
    value_out[...] = projected[:, (heads + 1) * dim :].astype(jnp.bfloat16)


def project(meta, blocks, row_count, shards, cosine, sine, gains, heads):
    count, tile, width = blocks.shape
    keys = list(shards)
    depth, columns = shards[0, 0].shape
    dim = HEAD_DIMENSION
    places = width // depth // 2

    def spot(j, meta):
        return (meta[2 + j], 0)

    return pl.pallas_call(
        functools.partial(project_kernel, heads, places, keys),
        grid_spec=pltpu.PrefetchScalarGridSpec(
            num_scalar_prefetch=1,
            grid=(count,),
            in_specs=[
                pl.BlockSpec((1, tile, width), lambda j, meta: (j, 0, 0)),
                pl.BlockSpec((tile, dim), spot),
                pl.BlockSpec((tile, dim), spot),
                pl.BlockSpec((2, dim), lambda j, meta: (0, 0)),
            ]
            + [pl.BlockSpec(memory_space=pl.ANY)] * len(keys),
            out_specs=[
                pl.BlockSpec((heads, tile, dim), lambda j, meta: (0, meta[2 + j], 0)),
                pl.BlockSpec((tile, dim), spot),
                pl.BlockSpec((tile, dim), spot),
            ],
            scratch_shapes=[
                pltpu.VMEM((width, columns), jnp.bfloat16),
                pltpu.SemaphoreType.DMA,
            ],
        ),
        out_shape=[
            jax.ShapeDtypeStruct((heads, row_count, dim), jnp.bfloat16),
            jax.ShapeDtypeStruct((row_count, dim), jnp.bfloat16),
            jax.ShapeDtypeStruct((row_count, dim), jnp.bfloat16),
        ],
        compiler_params=pltpu.CompilerParams(vmem_limit_bytes=VMEM_LIMIT),
        cost_estimate=pl.CostEstimate(
            flops=2 * row_count * width * columns,
            bytes_accessed=2 * (row_count * width + width * columns + row_count * columns),
            transcendentals=0,
        ),
    )(meta, blocks, cosine, sine, gains, *[shards[key] for key in keys])


def attend_kernel(tile, meta, query, own_key, own_value, far_key, far_value, out, keys, values, total):
    heads, dim = query.shape[0], HEAD_DIMENSION
    row_count = own_key.shape[0]
    half = row_count // 2
    parity, length = meta[0], meta[1]
    step = pl.program_id(0)

    @pl.when(step == 0)
    def _():
        ones = jnp.ones((half, dim), jnp.bfloat16)
        for key_ref, value_ref, whose in ((own_key, own_value, parity), (far_key, far_value, 1 - parity)):
            for part in range(2):
                base = jnp.where(whose == 0, 3 * half * part, half * (1 + part))
                base = pl.multiple_of(base, half)
                source = pl.ds(part * half, half)
                keys[pl.ds(base, half), :] = key_ref[source, :]
                valid = base + lax.broadcasted_iota(jnp.int32, (half, dim), 0) < length
                zero = jnp.zeros((half, dim), jnp.bfloat16)
                values[pl.ds(base, half), :dim] = jnp.where(valid, value_ref[source, :], zero)
                values[pl.ds(base, half), dim:] = jnp.where(valid, ones, zero)

    first = step * tile
    first = first + jnp.where(parity == 0, jnp.where(first < half, 0, 2 * half), half)

    def weigh(head, start, width, masked):
        scores = lax.dot_general(
            query[head], keys[pl.ds(start, width), :], (((1,), (1,)), ((), ())),
            preferred_element_type=jnp.float32,
        )
        weights = jnp.exp2(scores)
        if masked:
            below = lax.broadcasted_iota(jnp.int32, weights.shape, 1) <= lax.broadcasted_iota(
                jnp.int32, weights.shape, 0
            )
            weights = jnp.where(below, weights, 0.0)
        return jnp.dot(
            weights.astype(jnp.bfloat16), values[pl.ds(start, width), :], preferred_element_type=jnp.float32
        )

    diagonal = pl.multiple_of(first, tile)
    for head in range(heads):
        total[head] = weigh(head, diagonal, tile, True)

    def wide(index, _):
        start = pl.multiple_of(index * half, half)
        for head in range(heads):
            total[head] += weigh(head, start, half, False)
        return 0

    lax.fori_loop(0, first // half, wide, 0)

    def narrow(index, _):
        start = pl.multiple_of(index * tile, tile)
        for head in range(heads):
            total[head] += weigh(head, start, tile, False)
        return 0

    lax.fori_loop(first // half * (half // tile), first // tile, narrow, 0)
    for head in range(heads):
        summed = total[head]
        out[:, head * dim : (head + 1) * dim] = (summed[:, :dim] / summed[:, dim:]).astype(jnp.bfloat16)


def attend(meta, query, own_key, own_value, far_key, far_value):
    heads, row_count, dim = query.shape
    tile = min(256, row_count // 2)
    whole = pl.BlockSpec((row_count, dim), lambda i, meta: (0, 0))
    return pl.pallas_call(
        functools.partial(attend_kernel, tile),
        grid_spec=pltpu.PrefetchScalarGridSpec(
            num_scalar_prefetch=1,
            grid=(row_count // tile,),
            in_specs=[pl.BlockSpec((heads, tile, dim), lambda i, meta: (0, i, 0))] + [whole] * 4,
            out_specs=pl.BlockSpec((tile, heads * dim), lambda i, meta: (i, 0)),
            scratch_shapes=[
                pltpu.VMEM((2 * row_count, dim), jnp.bfloat16),
                pltpu.VMEM((2 * row_count, 2 * dim), jnp.bfloat16),
                pltpu.VMEM((heads, tile, 2 * dim), jnp.float32),
            ],
        ),
        out_shape=jax.ShapeDtypeStruct((row_count, heads * dim), jnp.bfloat16),
        compiler_params=pltpu.CompilerParams(vmem_limit_bytes=VMEM_LIMIT),
        cost_estimate=pl.CostEstimate(
            flops=4 * heads * row_count * row_count * dim * 2,
            bytes_accessed=4 * heads * row_count * dim + 8 * row_count * dim,
            transcendentals=heads * row_count * row_count,
        ),
    )(meta, query, own_key, own_value, far_key, far_value)


def output_kernel(places, keys, meta, rows, *rest):
    shard_refs = rest[: len(keys)]
    out, weights, sem = rest[len(keys) :]
    columns = shard_refs[0].shape[1]

    @pl.when(pl.program_id(0) == 0)
    def _():
        load_shards(
            meta[0], meta[1], places, keys, shard_refs,
            lambda group: weights.at[:, pl.ds(pl.multiple_of(group * columns, columns), columns)], sem,
        )

    out[0] = jnp.dot(rows[...], weights[...], preferred_element_type=jnp.float32).astype(jnp.bfloat16)


def output_part(meta, attended, shards, blocks):
    row_count, depth = attended.shape
    keys = list(shards)
    columns = shards[0, 0].shape[1]
    places = (max(key[1] for key in keys)) + 1
    width = columns * 2 * places
    tile = row_count // blocks
    return pl.pallas_call(
        functools.partial(output_kernel, places, keys),
        grid_spec=pltpu.PrefetchScalarGridSpec(
            num_scalar_prefetch=1,
            grid=(blocks,),
            in_specs=[pl.BlockSpec((tile, depth), lambda j, meta: (meta[2 + j], 0))]
            + [pl.BlockSpec(memory_space=pl.ANY)] * len(keys),
            out_specs=pl.BlockSpec((1, tile, width), lambda j, meta: (j, 0, 0)),
            scratch_shapes=[pltpu.VMEM((depth, width), jnp.bfloat16), pltpu.SemaphoreType.DMA],
        ),
        out_shape=jax.ShapeDtypeStruct((blocks, tile, width), jnp.bfloat16),
        compiler_params=pltpu.CompilerParams(vmem_limit_bytes=VMEM_LIMIT),
        cost_estimate=pl.CostEstimate(
            flops=2 * row_count * width * depth,
            bytes_accessed=2 * (row_count * width + width * depth + row_count * depth),
            transcendentals=0,
        ),
    )(meta, attended, *[shards[key] for key in keys])


def per_device(
    hidden_in,
    norm_attention,
    norm_experts,
    query_master,
    trainer_key_value_weight,
    output_master,
    query_gain,
    key_gain,
    lengths,
    router,
    expert_gateup,
    expert_down,
    routes,
):
    experts_axis = lax.axis_size("expert")
    group_member = lax.axis_index("expert")
    group_index = lax.axis_index("group")
    heads = QUERY_HEADS // experts_axis
    dim = HEAD_DIMENSION
    rows_here, model_width = hidden_in.shape
    local_rows = rows_here * experts_axis

    common_head = group_member * heads // (QUERY_HEADS // KEY_VALUE_HEADS)
    pair = lax.dynamic_slice_in_dim(trainer_key_value_weight, common_head * dim, dim, 2)
    joined = jnp.concatenate([query_master, pair[0], pair[1]], axis=1).astype(jnp.bfloat16)
    joined_shards = gather_group(joined)
    blocks = gather_tokens(hidden_in)
    stages = 2 if output_master.shape[1] >= 256 else 1
    stage_width = output_master.shape[1] // stages
    output_shards = [
        gather_group(output_master[:, s * stage_width : (s + 1) * stage_width].astype(jnp.bfloat16))
        for s in range(stages)
    ]

    masks = doubling_masks(experts_axis)
    block_order = jnp.bitwise_xor(group_member, jnp.array(masks, jnp.int32))
    meta = jnp.concatenate([jnp.stack([group_index // 2, group_index % 2]), block_order]).astype(jnp.int32)

    parity = group_index % 2
    own_places = local_positions(parity, local_rows).astype(jnp.float32)
    exponents = jnp.arange(dim // 2).astype(jnp.float32)
    inverse = jnp.exp(exponents * (-2.0 * math.log(rope_theta) / dim))
    angles = own_places[:, None] * inverse[None, :]
    cosine_values, sine_values = jnp.cos(angles), jnp.sin(angles)
    cosine = jnp.concatenate([cosine_values, cosine_values], axis=1)
    sine = jnp.concatenate([-sine_values, sine_values], axis=1)
    gains = jnp.stack([query_gain * (dim**-0.5 * math.log2(math.e)), key_gain])
    normed = norm_rows(blocks, norm_attention).astype(jnp.bfloat16)
    query, key_rows, value_rows = project(
        meta, normed, local_rows, joined_shards, cosine, sine, gains, heads
    )

    partner = from_xor(jnp.stack([key_rows, value_rows]), "group", 1)
    valid_length = jnp.sum(jnp.where(jnp.arange(lengths.shape[0]) == group_index // 2, lengths, 0))
    attend_meta = jnp.stack([parity, valid_length]).astype(jnp.int32)
    attended = attend(attend_meta, query, key_rows, value_rows, partner[0], partner[1])

    sums = [
        scatter_sum(output_part(meta, attended, shards, experts_axis)) for shards in output_shards
    ]
    summed = jnp.stack([part.reshape(rows_here, -1, stage_width) for part in sums], axis=2).reshape(
        rows_here, model_width
    )
    hidden = (hidden_in.astype(jnp.float32) + summed).astype(jnp.bfloat16)

    normed_second = norm_rows(hidden, norm_experts).astype(jnp.bfloat16)
    logits = jnp.dot(normed_second, router, preferred_element_type=jnp.float32)
    route_table = routes[:, :, None] == jnp.arange(logits.shape[1])[None, None, :]
    picked = jnp.sum(jnp.where(route_table, logits[:, None, :], 0.0), axis=-1)
    raised = jnp.exp(picked)
    gate_values = raised / jnp.sum(raised, axis=1, keepdims=True)
    inside = routes < experts_axis
    gate_window = jnp.sum(jnp.where(inside, gate_values, 0.0), axis=1)
    expert_window = jnp.sum(jnp.where(inside, routes, 0), axis=1)
    present = jnp.any(inside, axis=1)
    capacity = local_rows // (experts_axis * experts_axis)
    member_table = (
        present[:, None] & (expert_window[:, None] == jnp.arange(experts_axis)[None, :])
    ).astype(jnp.int32)
    ranking = jnp.sum(jnp.cumsum(member_table, axis=0) * member_table, axis=1) - 1
    slot_index = expert_window * capacity + ranking
    select = (
        (jnp.arange(experts_axis * capacity)[:, None] == slot_index[None, :]) & present[None, :]
    ).astype(jnp.bfloat16)
    outgoing = (
        jnp.dot(select, normed_second, preferred_element_type=jnp.float32)
        .astype(jnp.bfloat16)
        .reshape(experts_axis, capacity, model_width)
    )
    gateup_here = expert_gateup[0]
    down_here = expert_down[0]
    hidden_units = down_here.shape[0]
    slot_items = lax.all_to_all(outgoing, "expert", split_axis=0, concat_axis=0, tiled=True)
    flattened = slot_items.reshape(-1, slot_items.shape[-1])
    gate_up = jnp.dot(flattened, gateup_here, preferred_element_type=jnp.float32)
    active = (jax.nn.silu(gate_up[:, :hidden_units]) * gate_up[:, hidden_units:]).astype(
        jnp.bfloat16
    )
    result = (
        jnp.dot(active, down_here, preferred_element_type=jnp.float32)
        .astype(jnp.bfloat16)
        .reshape(slot_items.shape)
    )
    returned = lax.all_to_all(result, "expert", split_axis=0, concat_axis=0, tiled=True)
    combined = jnp.dot(
        jnp.transpose(select), returned.reshape(-1, model_width), preferred_element_type=jnp.float32
    )
    expert_mix = (gate_window[:, None] * combined).astype(jnp.bfloat16)
    return (hidden, expert_mix)


def solution(mesh):
    return jax.shard_map(
        per_device,
        mesh=mesh,
        in_specs=(
            P(("group", "expert"), None),
            P(),
            P(),
            P("group", "expert"),
            P(None, "group", None),
            P("expert", "group"),
            P(),
            P(),
            P(),
            P(),
            P("expert", None, None),
            P("expert", None, None),
            P(("group", "expert"), None),
        ),
        out_specs=(P(("group", "expert"), None), P(("group", "expert"), None)),
        check_vma=False,
    )
```

time: 374 us -> 334 us (0.89)
  starting transfers between devices: 5 us -> 126 us
  waiting for transfers between devices: 194 us -> 75.3 us
  matrix products: 89.7 us -> 11.7 us
  Pallas kernels: 0 us -> 54.9 us
  between operations: 14.1 us -> 1.86 us
  other arithmetic: 37.6 us -> 29 us
    all_gather x4 -> x0, waiting for transfers between devices: 140 us -> none  [the longest x1 75.6 us: per_device(): lax.all_gather(query_master.astype(jnp.bfloat16), 'group', axis=0, tiled=...]
    ppermute x1 -> x46, starting transfers between devices: 0.56 us -> 122 us  [the longest x9 64.3 us: gather_group(): below = lax.ppermute(below, 'group', [(i, i + 2) for i in range(count - 2)])]
    dot_general x6 -> x0, matrix products: 78 us -> none  [the longest x2 32.5 us: attend(): jnp.einsum('qhd,kd->hqk', query_block, all_keys, preferred_element_type=j...]
    ppermute x1 -> x46, waiting for transfers between devices: 0.13 us -> 63.8 us  [the longest x7 43.5 us: from_xor(): return lax.ppermute(block, axis, [(i, i ^ mask) for i in range(count)])]
    pallas_call x0 -> x4, Pallas kernels: none -> 54.9 us  [the longest x1 22.8 us: project(): pl.pallas_call(functools.partial(project_kernel, heads, places, keys), gr...]
    reduce_scatter x1 -> x0, waiting for transfers between devices: 41.6 us -> none  [per_device(): lax.psum_scatter(jnp.dot(attended, output_part, preferred_element_type=jn...]
    slice x3 -> x7, local copies, waits for them, and re-layouts: 0.21 us -> 4.82 us  [the longest x4 4.6 us: scatter_sum(): arrived = from_xor(blocks[half:], 'expert', stride)]
    mul x2 -> x0, other arithmetic: 4.11 us -> none  [norm_rows(): return widened * inverse_rms * gain_vector]
  transfers between devices with their start and end apart: 7 -> 47, of which waited for: 6 -> 8; matrix products, arithmetic and copies ran while one was open for 31% -> 10% of each run, Pallas kernels for 0% -> 16%
where the time goes in v1:
time: 334 us; the launch traced here: 333 us
  starting transfers between devices  126 us (38%)
  waiting for transfers between devices  75.3 us (23%)
  Pallas kernels  54.9 us (16%)
  other arithmetic  29 us (9%)
  blocking collectives  17.1 us (5%)
  local copies, waits for them, and re-layouts  16.7 us (5%)
  matrix products  11.7 us (4%)
    ppermute x9, starting transfers between devices, gather_group(): below = lax.ppermute(below, 'group', [(i, i + 2) for i in range(count - 2)])  64.3 us
    ppermute x7, waiting for transfers between devices, from_xor(): return lax.ppermute(block, axis, [(i, i ^ mask) for i in range(count)])  43.5 us
    ppermute x21, starting transfers between devices, cross(): return lax.ppermute(shard, 'group', route)  38.9 us
    pallas_call x1, Pallas kernels, project(): pl.pallas_call(functools.partial(project_kernel, heads, places, keys), gr...  22.8 us
    ppermute x9, waiting for transfers between devices, gather_group(): above = lax.ppermute(above, 'group', [(i, i - 2) for i in range(2, count)])  17.1 us
    all_to_all x1, blocking collectives, per_device(): lax.all_to_all(outgoing, 'expert', split_axis=0, concat_axis=0, tiled=True)  17.1 us
    pallas_call x1, Pallas kernels, attend(): pl.pallas_call(functools.partial(attend_kernel, tile), grid_spec=pltpu.Pr...  17 us
    pallas_call x2, Pallas kernels, output_part(): pl.pallas_call(functools.partial(output_kernel, places, keys), grid_spec=...  15.1 us
  transfers between devices with their start and end apart: 47, of which 8 were waited for; matrix products, arithmetic and copies ran while one was open for 10% of the time, Pallas kernels for 16%

profile of v1, /device:TPU:0, one launch (start us, length us, event | category | flops | bytes accessed | tf_op | source)
XLA Modules:
  0.0 332.6 jit_solution(12704461271041997997)
XLA Ops:
  0.6 3.0 collective-permute-start
  4.7 22.5 %collective-permute-done = bf16[1,256,2048]{2,1,0:T(8,128)(2,1)} collective-permute-done((bf16[1,256,2048]{2,1,0:T(8,128)(2,1)}, bf16[1,256,2048]{2,1,0:T(8,128)(2,1)}, u32[]{:S(2)}, u32[]{:S(2)}) %collective-permute-start) | collective-permute-done | bytes 1048608 | tf_op jit(solution)/shard_map/ppermute | solution.py:35
  27.2 3.1 pad_maximum_fusion.1
  32.5 5.4 %collective-permute-start.4 = (bf16[256,1280]{1,0:T(8,128)(2,1)}, bf16[256,1280]{1,0:T(8,128)(2,1)}, u32[]{:S(2)}, u32[]{:S(2)}) collective-permute-start(bf16[256,1280]{1,0:T(8,128)(2,1)} %pad_maximum_fusion.3.rest_0_), channel_id=1, source_target_pairs={{0,8},{4,12},{8,16},{12,20},{16,24},{20,28},{1,9},{5,13},{9,17},{1... | collective-permute-start | bytes 1966088 | tf_op jit(solution)/shard_map/ppermute | solution.py:51
  40.2 10.4 %collective-permute-done.3.rest_2_ = bf16[256,1280]{1,0:T(8,128)(2,1)} collective-permute-done((bf16[256,1280]{1,0:T(8,128)(2,1)}, bf16[256,1280]{1,0:T(8,128)(2,1)}, u32[]{:S(2)}, u32[]{:S(2)}) %collective-permute-start.3) | collective-permute-done | bytes 655392 | tf_op jit(solution)/shard_map/ppermute | solution.py:50
  51.9 5.4 %collective-permute-start.8 = (bf16[256,1280]{1,0:T(8,128)(2,1)}, bf16[256,1280]{1,0:T(8,128)(2,1)}, u32[]{:S(2)}, u32[]{:S(2)}) collective-permute-start(bf16[256,1280]{1,0:T(8,128)(2,1)} %collective-permute-done.4.rest_3_), channel_id=1, source_target_pairs={{0,8},{4,12},{8,16},{12,20},{16,24},{20,28},{1,9},{5,13},{9,17},{1... | collective-permute-start | bytes 1966088 | tf_op jit(solution)/shard_map/ppermute | solution.py:51
  57.3 2.1 convert.17
  59.4 1.9 fusion.23
  62.7 3.5 %collective-permute-start.5 = (bf16[256,1280]{1,0:T(8,128)(2,1)}, bf16[256,1280]{1,0:T(8,128)(2,1)S(1)}, u32[]{:S(2)}, u32[]{:S(2)}) collective-permute-start(bf16[256,1280]{1,0:T(8,128)(2,1)} %collective-permute-done.3.rest_2_), channel_id=1, source_target_pairs={{0,4},{4,0},{8,12},{12,8},{16,20},{20,16},{1,5},{5,1},{9,13},{13,9... | collective-permute-start | bytes 1966088 | tf_op jit(solution)/shard_map/ppermute | solution.py:45
  66.2 3.0 collective-permute-done.7.rest_6_
  70.5 4.6 %collective-permute-start.12 = (bf16[256,1280]{1,0:T(8,128)(2,1)}, bf16[256,1280]{1,0:T(8,128)(2,1)S(1)}, u32[]{:S(2)}, u32[]{:S(2)}) collective-permute-start(bf16[256,1280]{1,0:T(8,128)(2,1)} %collective-permute-done.8.rest_7_), channel_id=1, source_target_pairs={{0,8},{4,12},{8,16},{12,20},{16,24},{20,28},{1,9},{5,13},{9,17},{1... | collective-permute-start | bytes 1966088 | tf_op jit(solution)/shard_map/ppermute | solution.py:51
  76.6 2.3 fusion
  79.0 3.5 %collective-permute-start.9 = (bf16[256,1280]{1,0:T(8,128)(2,1)}, bf16[256,1280]{1,0:T(8,128)(2,1)S(1)}, u32[]{:S(2)}, u32[]{:S(2)}) collective-permute-start(bf16[256,1280]{1,0:T(8,128)(2,1)} %collective-permute-done.7.rest_6_), channel_id=1, source_target_pairs={{0,4},{4,0},{8,12},{12,8},{1,5},{5,1},{9,13},{13,9},{2,6},{6,2},{1... | collective-permute-start | bytes 1966088 | tf_op jit(solution)/shard_map/ppermute | solution.py:45
  83.2 3.6 %collective-permute-done.11.rest_10_ = bf16[256,1280]{1,0:T(8,128)(2,1)S(1)} collective-permute-done((bf16[256,1280]{1,0:T(8,128)(2,1)}, bf16[256,1280]{1,0:T(8,128)(2,1)S(1)}, u32[]{:S(2)}, u32[]{:S(2)}) %collective-permute-start.11) | collective-permute-done | bytes 655392 | tf_op jit(solution)/shard_map/ppermute | solution.py:50
  86.9 3.4 %collective-permute-start.13 = (bf16[256,1280]{1,0:T(8,128)(2,1)S(1)}, bf16[256,1280]{1,0:T(8,128)(2,1)S(1)}, u32[]{:S(2)}, u32[]{:S(2)}) collective-permute-start(bf16[256,1280]{1,0:T(8,128)(2,1)S(1)} %collective-permute-done.11.rest_10_), channel_id=1, source_target_pairs={{0,4},{4,0},{1,5},{5,1},{2,6},{6,2},{3,7},{7,3}} | collective-permute-start | bytes 1966088 | tf_op jit(solution)/shard_map/ppermute | solution.py:45
  91.0 3.9 %fusion.2.rows = bf16[4,256,2048]{2,1,0:T(8,128)(2,1)} fusion(f32[2048]{0:T(1024)S(1)} %copy-done.8, f32[4,256]{1,0:T(4,128)S(1)} %add_rsqrt_fusion, bf16[2,256,2048]{2,1,0:T(8,128)(2,1)} %collective-permute-done.1, bf16[1,256,2048]{2,1,0:T(8,128)(2,1)} %collective-permute-done, bf16[1,256,2048]{2,1,0:T(8,128)(2,1)S(1)} %bitcast.64), kind=kLoop, calls=%fused_computation.4 | loop fusion | flops 12582912 | bytes 8400896 | tf_op jit(solution)/shard_map/convert_element_type | solution.py:359
  95.6 3.2 collective-permute-done.9.rest_8_
  100.1 15.8 %collective-permute-start.33 = (bf16[1024,128]{1,0:T(8,128)(2,1)S(1)}, bf16[1024,128]{1,0:T(8,128)(2,1)}, u32[]{:S(2)}, u32[]{:S(2)}) collective-permute-start(bf16[1024,128]{1,0:T(8,128)(2,1)S(1)} %get-tuple-element.11.rest_0_), channel_id=1, source_target_pairs={{0,8},{4,12},{8,16},{12,20},{16,24},{20,28},{1,9},{5,13},{9,17},{1... | collective-permute-start | bytes 786440 | tf_op jit(solution)/shard_map/ppermute | solution.py:51
  119.6 22.8 %shard_map.149 = (bf16[8,1024,128]{2,1,0:T(8,128)(2,1)}, bf16[1024,128]{1,0:T(8,128)(2,1)}, bf16[1024,128]{1,0:T(8,128)(2,1)}) custom-call(s32[6]{0:T(128)} %pad_add_fusion.meta, bf16[4,256,2048]{2,1,0:T(8,128)(2,1)} %fusion.2.rows, f32[1024,128]{1,0:T(8,128)} %get-tuple-element.19.cosine, f32[1024,128]{1,0:T(8,128)} %get-tuple-element.20.sine, ...), custom_call_target="tpu_custom_call" | custom-call | flops 5368709120 | bytes 12058624 | tf_op jit(solution)/shard_map/pallas_call | solution.py:143
  142.4 4.6 %collective-permute-start.18 = (bf16[1024,128]{1,0:T(8,128)(2,1)S(1)}, bf16[1024,128]{1,0:T(8,128)(2,1)S(1)}, u32[]{:S(2)}, u32[]{:S(2)}) collective-permute-start(bf16[1024,128]{1,0:T(8,128)(2,1)S(1)} %get-tuple-element.10.rest_0_), channel_id=1, source_target_pairs={{0,8},{4,12},{8,16},{12,20},{16,24},{20,28},{1,9},{5,13},{9,17},{1... | collective-permute-start | bytes 786440 | tf_op jit(solution)/shard_map/ppermute | solution.py:51
  147.0 2.4 collective-permute-start.34
  154.1 5.7 %collective-permute-start.37 = (bf16[1024,128]{1,0:T(8,128)(2,1)}, bf16[1024,128]{1,0:T(8,128)(2,1)S(1)}, u32[]{:S(2)}, u32[]{:S(2)}) collective-permute-start(bf16[1024,128]{1,0:T(8,128)(2,1)} %collective-permute-done.33.rest_3_), channel_id=1, source_target_pairs={{0,8},{4,12},{8,16},{12,20},{16,24},{20,28},{1,9},{5,13},{9,17},{1... | collective-permute-start | bytes 786440 | tf_op jit(solution)/shard_map/ppermute | solution.py:51
  159.9 3.4 %collective-permute-start.19 = (bf16[1024,128]{1,0:T(8,128)(2,1)S(1)}, bf16[1024,128]{1,0:T(8,128)(2,1)S(1)}, u32[]{:S(2)}, u32[]{:S(2)}) collective-permute-start(bf16[1024,128]{1,0:T(8,128)(2,1)S(1)} %collective-permute-done.17.rest_2_), channel_id=1, source_target_pairs={{0,4},{4,0},{8,12},{12,8},{16,20},{20,16},{1,5},{5,1},{9,13},{13,9... | collective-permute-start | bytes 786440 | tf_op jit(solution)/shard_map/ppermute | solution.py:45
  165.2 8.0 %collective-permute-start.22 = (bf16[1024,128]{1,0:T(8,128)(2,1)S(1)}, bf16[1024,128]{1,0:T(8,128)(2,1)S(1)}, u32[]{:S(2)}, u32[]{:S(2)}) collective-permute-start(bf16[1024,128]{1,0:T(8,128)(2,1)S(1)} %collective-permute-done.18.rest_3_), channel_id=1, source_target_pairs={{0,8},{4,12},{8,16},{12,20},{16,24},{20,28},{1,9},{5,13},{9,17},{1... | collective-permute-start | bytes 786440 | tf_op jit(solution)/shard_map/ppermute | solution.py:51
  173.3 3.4 %collective-permute-start.38 = (bf16[1024,128]{1,0:T(8,128)(2,1)S(1)}, bf16[1024,128]{1,0:T(8,128)(2,1)S(1)}, u32[]{:S(2)}, u32[]{:S(2)}) collective-permute-start(bf16[1024,128]{1,0:T(8,128)(2,1)S(1)} %collective-permute-done.36.rest_6_), channel_id=1, source_target_pairs={{0,4},{4,0},{8,12},{12,8},{1,5},{5,1},{9,13},{13,9},{2,6},{6,2},{1... | collective-permute-start | bytes 786440 | tf_op jit(solution)/shard_map/ppermute | solution.py:45
  178.7 5.0 %collective-permute-start.41 = (bf16[1024,128]{1,0:T(8,128)(2,1)S(1)}, bf16[1024,128]{1,0:T(8,128)(2,1)S(1)}, u32[]{:S(2)}, u32[]{:S(2)}) collective-permute-start(bf16[1024,128]{1,0:T(8,128)(2,1)S(1)} %collective-permute-done.37.rest_7_), channel_id=1, source_target_pairs={{0,8},{4,12},{8,16},{12,20},{16,24},{20,28},{1,9},{5,13},{9,17},{1... | collective-permute-start | bytes 786440 | tf_op jit(solution)/shard_map/ppermute | solution.py:51
  187.8 9.8 %collective-permute-start.26 = (bf16[1024,128]{1,0:T(8,128)(2,1)S(1)}, bf16[1024,128]{1,0:T(8,128)(2,1)S(1)}, u32[]{:S(2)}, u32[]{:S(2)}) collective-permute-start(bf16[1024,128]{1,0:T(8,128)(2,1)S(1)} %collective-permute-done.22.rest_7_), channel_id=1, source_target_pairs={{0,8},{4,12},{8,16},{12,20},{16,24},{20,28},{1,9},{5,13},{9,17},{1... | collective-permute-start | bytes 786440 | tf_op jit(solution)/shard_map/ppermute | solution.py:51
  197.7 3.1 collective-permute-start.42
  201.6 17.0 %shard_map.150.rows = bf16[1024,1024]{1,0:T(8,128)(2,1)} custom-call(s32[2]{0:T(128)} %pad_add_fusion.1.meta, bf16[8,1024,128]{2,1,0:T(8,128)(2,1)} %get-tuple-element.5.query, bf16[1024,128]{1,0:T(8,128)(2,1)} %get-tuple-element.6.own_key, bf16[1024,128]{1,0:T(8,128)(2,1)} %get-tuple-element.7.own_value, bf16[1024,128]{1,0:T(8,128)(2,1)} %get-tuple-element.13.far_key, ...), custom_call_target="tpu_custom_call" | custom-call | flops 8589934592 | bytes 5242880 | tf_op jit(solution)/shard_map/pallas_call | solution.py:246
  218.8 2.8 collective-permute-start.23
  222.3 3.1 collective-permute-start.27
  226.1 7.5 %shard_map.152 = bf16[4,256,1024]{2,1,0:T(8,128)(2,1)} custom-call(s32[6]{0:T(128)} %pad_add_fusion.meta, bf16[1024,1024]{1,0:T(8,128)(2,1)} %shard_map.150.rows, bf16[1024,128]{1,0:T(8,128)(2,1)} %copy-done.7, bf16[1024,128]{1,0:T(8,128)(2,1)} %collective-permute-done.31.rest_1_, bf16[1024,128]{1,0:T(8,128)(2,1)} %collective-permute-done.32.rest_2_, ...), custom_call_target="tpu_custom_call" | custom-call | flops 2147483648 | bytes 6291456 | tf_op jit(solution)/shard_map/pallas_call | solution.py:291
  233.7 2.3 slice.87
  237.6 7.5 %shard_map.151 = bf16[4,256,1024]{2,1,0:T(8,128)(2,1)} custom-call(s32[6]{0:T(128)} %pad_add_fusion.meta, bf16[1024,1024]{1,0:T(8,128)(2,1)} %shard_map.150.rows, bf16[1024,128]{1,0:T(8,128)(2,1)} %copy-done.6, bf16[1024,128]{1,0:T(8,128)(2,1)} %copy-done.19, bf16[1024,128]{1,0:T(8,128)(2,1)} %copy-done.20, bf16[1024,128]{1,0:T(8,128)(2,1)} %copy-done.21, ...), custom_call_target="tpu_custom_call" | custom-call | flops 2147483648 | bytes 6291456 | tf_op jit(solution)/shard_map/pallas_call | solution.py:291
  245.2 2.3 slice.82
  249.9 2.1 add_convert_fusion.1
  255.9 11.0 %collective-permute-done.45 = bf16[1,256,1024]{2,1,0:T(8,128)(2,1)S(1)} collective-permute-done((bf16[1,256,1024]{2,1,0:T(8,128)(2,1)S(1)}, bf16[1,256,1024]{2,1,0:T(8,128)(2,1)S(1)}, u32[]{:S(2)}, u32[]{:S(2)}) %collective-permute-start.45) | collective-permute-done | bytes 524320 | tf_op jit(solution)/shard_map/ppermute | solution.py:35
  267.2 10.0 %collective-permute-done.30 = bf16[1,256,1024]{2,1,0:T(8,128)(2,1)S(1)} collective-permute-done((bf16[1,256,1024]{2,1,0:T(8,128)(2,1)S(1)}, bf16[1,256,1024]{2,1,0:T(8,128)(2,1)S(1)}, u32[]{:S(2)}, u32[]{:S(2)}) %collective-permute-start.30) | collective-permute-done | bytes 524320 | tf_op jit(solution)/shard_map/ppermute | solution.py:35
  277.7 2.9 copy.20
  280.7 3.9 %reshape.85 = f32[256,2048]{1,0:T(8,128)} reshape(f32[256,8,2,128]{3,2,1,0:T(2,128)} %copy.20) | data formatting | bytes 4194304 | tf_op jit(solution)/shard_map/reshape | solution.py:372
  284.6 2.3 fusion.11
  287.5 17.1 %all_to_all.10 = bf16[4,64,2048]{2,1,0:T(8,128)(2,1)S(1)} all-to-all(bf16[4,64,2048]{2,1,0:T(8,128)(2,1)S(1)} %bitcast.69), channel_id=1, replica_groups=mesh['group'=8,'expert'=4] {'expert'}, dimensions={0} | all-to-all | bytes 2097152 | tf_op jit(solution)/shard_map/all_to_all | solution.py:404
  304.5 4.6 %fusion.3 = f32[256,1536]{1,0:T(8,128)S(1)} fusion(bf16[256,2048]{1,0:T(8,128)(2,1)S(1)} %bitcast.68, bf16[1,2048,1536]{2,1,0:T(8,128)(2,1)} %param.24), kind=kOutput, calls=%fused_computation.5 | convolution fusion | flops 1610612736 | bytes 8912896 | tf_op jit(solution)/shard_map/dot_general | solution.py:406
  309.1 2.0 fusion.8
  311.1 4.2 %all-to-all-start.1 = ((bf16[4,64,2048]{2,1,0:T(8,128)(2,1)}), bf16[4,64,2048]{2,1,0:T(8,128)(2,1)}, u32[]{:S(2)}, u32[]{:S(2)}) async-start(bf16[4,64,2048]{2,1,0:T(8,128)(2,1)} %bitcast.67), calls=%async_computation.1 | async-start | bytes 2097152 | tf_op jit(solution)/shard_map/all_to_all | solution.py:415
  315.4 1.9 fusion.18
  318.4 11.5 %all-to-all-done.1 = bf16[4,64,2048]{2,1,0:T(8,128)(2,1)} async-done(((bf16[4,64,2048]{2,1,0:T(8,128)(2,1)}), bf16[4,64,2048]{2,1,0:T(8,128)(2,1)}, u32[]{:S(2)}, u32[]{:S(2)}) %all-to-all-start.1) | async-done | bytes 1048608 | tf_op jit(solution)/shard_map/all_to_all | solution.py:415
  329.9 2.7 fusion.7
  (201 shorter events, 43.4 us)
Async XLA Ops:
  0.6 308.5 %copy-start = (bf16[1,768,2048]{2,1,0:T(8,128)(2,1)S(1)}, bf16[1,768,2048]{2,1,0:T(8,128)(2,1)}, u32[]{:S(2)}) copy-start(bf16[1,768,2048]{2,1,0:T(8,128)(2,1)} %param.25) | copy-start | bytes 9437188
  0.6 26.5 %collective-permute-start = (bf16[1,256,2048]{2,1,0:T(8,128)(2,1)}, bf16[1,256,2048]{2,1,0:T(8,128)(2,1)}, u32[]{:S(2)}, u32[]{:S(2)}) collective-permute-start(bf16[1,256,2048]{2,1,0:T(8,128)(2,1)} %bitcast.61), channel_id=1, source_target_pairs={{0,2},{1,3},{2,0},{3,1},{4,6},{5,7},{6,4},{7,5},{8,10},{9,11},{10,... | collective-permute-start | bytes 3145736 | tf_op jit(solution)/shard_map/ppermute | solution.py:35
  30.2 45.5 %collective-permute-start.1 = (bf16[2,256,2048]{2,1,0:T(8,128)(2,1)}, bf16[2,256,2048]{2,1,0:T(8,128)(2,1)}, u32[]{:S(2)}, u32[]{:S(2)}) collective-permute-start(bf16[2,256,2048]{2,1,0:T(8,128)(2,1)} %pad_maximum_fusion.1), channel_id=1, source_target_pairs={{0,1},{1,0},{2,3},{3,2},{4,5},{5,4},{6,7},{7,6},{8,9},{9,8},{10,11... | collective-permute-start | bytes 6291464 | tf_op jit(solution)/shard_map/ppermute | solution.py:35
  31.2 19.4 %collective-permute-start.3 = (bf16[256,1280]{1,0:T(8,128)(2,1)}, bf16[256,1280]{1,0:T(8,128)(2,1)}, u32[]{:S(2)}, u32[]{:S(2)}) collective-permute-start(bf16[256,1280]{1,0:T(8,128)(2,1)} %pad_maximum_fusion.3.rest_0_), channel_id=1, source_target_pairs={{8,0},{12,4},{16,8},{20,12},{24,16},{28,20},{9,1},{13,5},{17,9},{2... | collective-permute-start | bytes 1966088 | tf_op jit(solution)/shard_map/ppermute | solution.py:50
  32.5 19.4 %collective-permute-start.4 = (bf16[256,1280]{1,0:T(8,128)(2,1)}, bf16[256,1280]{1,0:T(8,128)(2,1)}, u32[]{:S(2)}, u32[]{:S(2)}) collective-permute-start(bf16[256,1280]{1,0:T(8,128)(2,1)} %pad_maximum_fusion.3.rest_0_), channel_id=1, source_target_pairs={{0,8},{4,12},{8,16},{12,20},{16,24},{20,28},{1,9},{5,13},{9,17},{1... | collective-permute-start | bytes 1966088 | tf_op jit(solution)/shard_map/ppermute | solution.py:51
  37.9 41.1 %collective-permute-start.2 = (bf16[256,1280]{1,0:T(8,128)(2,1)}, bf16[256,1280]{1,0:T(8,128)(2,1)}, u32[]{:S(2)}, u32[]{:S(2)}) collective-permute-start(bf16[256,1280]{1,0:T(8,128)(2,1)} %pad_maximum_fusion.3.rest_0_), channel_id=1, source_target_pairs={{0,4},{4,0},{8,12},{12,8},{16,20},{20,16},{24,28},{28,24},{1,5},{5... | collective-permute-start | bytes 1966088 | tf_op jit(solution)/shard_map/ppermute | solution.py:45
  50.6 18.6 %collective-permute-start.7 = (bf16[256,1280]{1,0:T(8,128)(2,1)}, bf16[256,1280]{1,0:T(8,128)(2,1)}, u32[]{:S(2)}, u32[]{:S(2)}) collective-permute-start(bf16[256,1280]{1,0:T(8,128)(2,1)} %collective-permute-done.3.rest_2_), channel_id=1, source_target_pairs={{8,0},{12,4},{16,8},{20,12},{24,16},{28,20},{9,1},{13,5},{17,9},{2... | collective-permute-start | bytes 1966088 | tf_op jit(solution)/shard_map/ppermute | solution.py:50
  51.9 18.6 %collective-permute-start.8 = (bf16[256,1280]{1,0:T(8,128)(2,1)}, bf16[256,1280]{1,0:T(8,128)(2,1)}, u32[]{:S(2)}, u32[]{:S(2)}) collective-permute-start(bf16[256,1280]{1,0:T(8,128)(2,1)} %collective-permute-done.4.rest_3_), channel_id=1, source_target_pairs={{0,8},{4,12},{8,16},{12,20},{16,24},{20,28},{1,9},{5,13},{9,17},{1... | collective-permute-start | bytes 1966088 | tf_op jit(solution)/shard_map/ppermute | solution.py:51
  62.7 19.8 %collective-permute-start.5 = (bf16[256,1280]{1,0:T(8,128)(2,1)}, bf16[256,1280]{1,0:T(8,128)(2,1)S(1)}, u32[]{:S(2)}, u32[]{:S(2)}) collective-permute-start(bf16[256,1280]{1,0:T(8,128)(2,1)} %collective-permute-done.3.rest_2_), channel_id=1, source_target_pairs={{0,4},{4,0},{8,12},{12,8},{16,20},{20,16},{1,5},{5,1},{9,13},{13,9... | collective-permute-start | bytes 1966088 | tf_op jit(solution)/shard_map/ppermute | solution.py:45
  69.2 17.6 %collective-permute-start.11 = (bf16[256,1280]{1,0:T(8,128)(2,1)}, bf16[256,1280]{1,0:T(8,128)(2,1)S(1)}, u32[]{:S(2)}, u32[]{:S(2)}) collective-permute-start(bf16[256,1280]{1,0:T(8,128)(2,1)} %collective-permute-done.7.rest_6_), channel_id=1, source_target_pairs={{8,0},{12,4},{16,8},{20,12},{24,16},{28,20},{9,1},{13,5},{17,9},{2... | collective-permute-start | bytes 1966088 | tf_op jit(solution)/shard_map/ppermute | solution.py:50
  70.5 19.8 %collective-permute-start.12 = (bf16[256,1280]{1,0:T(8,128)(2,1)}, bf16[256,1280]{1,0:T(8,128)(2,1)S(1)}, u32[]{:S(2)}, u32[]{:S(2)}) collective-permute-start(bf16[256,1280]{1,0:T(8,128)(2,1)} %collective-permute-done.8.rest_7_), channel_id=1, source_target_pairs={{0,8},{4,12},{8,16},{12,20},{16,24},{20,28},{1,9},{5,13},{9,17},{1... | collective-permute-start | bytes 1966088 | tf_op jit(solution)/shard_map/ppermute | solution.py:51
  75.8 19.2 %collective-permute-start.6 = (bf16[256,1280]{1,0:T(8,128)(2,1)}, bf16[256,1280]{1,0:T(8,128)(2,1)S(1)}, u32[]{:S(2)}, u32[]{:S(2)}) collective-permute-start(bf16[256,1280]{1,0:T(8,128)(2,1)} %collective-permute-done.4.rest_3_), channel_id=1, source_target_pairs={{8,12},{12,8},{16,20},{20,16},{24,28},{28,24},{9,13},{13,9},{17,21... | collective-permute-start | bytes 1966088 | tf_op jit(solution)/shard_map/ppermute | solution.py:45
  79.0 19.8 %collective-permute-start.9 = (bf16[256,1280]{1,0:T(8,128)(2,1)}, bf16[256,1280]{1,0:T(8,128)(2,1)S(1)}, u32[]{:S(2)}, u32[]{:S(2)}) collective-permute-start(bf16[256,1280]{1,0:T(8,128)(2,1)} %collective-permute-done.7.rest_6_), channel_id=1, source_target_pairs={{0,4},{4,0},{8,12},{12,8},{1,5},{5,1},{9,13},{13,9},{2,6},{6,2},{1... | collective-permute-start | bytes 1966088 | tf_op jit(solution)/shard_map/ppermute | solution.py:45
  82.5 17.5 %collective-permute-start.10 = (bf16[256,1280]{1,0:T(8,128)(2,1)}, bf16[256,1280]{1,0:T(8,128)(2,1)S(1)}, u32[]{:S(2)}, u32[]{:S(2)}) collective-permute-start(bf16[256,1280]{1,0:T(8,128)(2,1)} %collective-permute-done.8.rest_7_), channel_id=1, source_target_pairs={{16,20},{20,16},{24,28},{28,24},{17,21},{21,17},{25,29},{29,25},{1... | collective-permute-start | bytes 1966088 | tf_op jit(solution)/shard_map/ppermute | solution.py:45
  86.9 29.0 %collective-permute-start.13 = (bf16[256,1280]{1,0:T(8,128)(2,1)S(1)}, bf16[256,1280]{1,0:T(8,128)(2,1)S(1)}, u32[]{:S(2)}, u32[]{:S(2)}) collective-permute-start(bf16[256,1280]{1,0:T(8,128)(2,1)S(1)} %collective-permute-done.11.rest_10_), channel_id=1, source_target_pairs={{0,4},{4,0},{1,5},{5,1},{2,6},{6,2},{3,7},{7,3}} | collective-permute-start | bytes 1966088 | tf_op jit(solution)/shard_map/ppermute | solution.py:45
  90.3 27.1 %collective-permute-start.14 = (bf16[256,1280]{1,0:T(8,128)(2,1)S(1)}, bf16[256,1280]{1,0:T(8,128)(2,1)S(1)}, u32[]{:S(2)}, u32[]{:S(2)}) collective-permute-start(bf16[256,1280]{1,0:T(8,128)(2,1)S(1)} %collective-permute-done.12.rest_11_), channel_id=1, source_target_pairs={{24,28},{28,24},{25,29},{29,25},{26,30},{30,26},{27,31},{31,27}} | collective-permute-start | bytes 1966088 | tf_op jit(solution)/shard_map/ppermute | solution.py:45
  95.0 47.4 %collective-permute-start.31 = (bf16[1024,128]{1,0:T(8,128)(2,1)S(1)}, bf16[1024,128]{1,0:T(8,128)(2,1)}, u32[]{:S(2)}, u32[]{:S(2)}) collective-permute-start(bf16[1024,128]{1,0:T(8,128)(2,1)S(1)} %get-tuple-element.11.rest_0_), channel_id=1, source_target_pairs={{0,4},{4,0},{8,12},{12,8},{16,20},{20,16},{24,28},{28,24},{1,5},{5... | collective-permute-start | bytes 786440 | tf_op jit(solution)/shard_map/ppermute | solution.py:45
  98.8 48.2 %collective-permute-start.32 = (bf16[1024,128]{1,0:T(8,128)(2,1)S(1)}, bf16[1024,128]{1,0:T(8,128)(2,1)}, u32[]{:S(2)}, u32[]{:S(2)}) collective-permute-start(bf16[1024,128]{1,0:T(8,128)(2,1)S(1)} %get-tuple-element.11.rest_0_), channel_id=1, source_target_pairs={{8,0},{12,4},{16,8},{20,12},{24,16},{28,20},{9,1},{13,5},{17,9},{2... | collective-permute-start | bytes 786440 | tf_op jit(solution)/shard_map/ppermute | solution.py:50
  100.1 49.4 %collective-permute-start.33 = (bf16[1024,128]{1,0:T(8,128)(2,1)S(1)}, bf16[1024,128]{1,0:T(8,128)(2,1)}, u32[]{:S(2)}, u32[]{:S(2)}) collective-permute-start(bf16[1024,128]{1,0:T(8,128)(2,1)S(1)} %get-tuple-element.11.rest_0_), channel_id=1, source_target_pairs={{0,8},{4,12},{8,16},{12,20},{16,24},{20,28},{1,9},{5,13},{9,17},{1... | collective-permute-start | bytes 786440 | tf_op jit(solution)/shard_map/ppermute | solution.py:51
  115.9 35.3 %collective-permute-start.16 = (bf16[1024,128]{1,0:T(8,128)(2,1)S(1)}, bf16[1024,128]{1,0:T(8,128)(2,1)S(1)}, u32[]{:S(2)}, u32[]{:S(2)}) collective-permute-start(bf16[1024,128]{1,0:T(8,128)(2,1)S(1)} %get-tuple-element.10.rest_0_), channel_id=1, source_target_pairs={{0,4},{4,0},{8,12},{12,8},{16,20},{20,16},{24,28},{28,24},{1,5},{5... | collective-permute-start | bytes 786440 | tf_op jit(solution)/shard_map/ppermute | solution.py:45
  118.3 34.6 %collective-permute-start.17 = (bf16[1024,128]{1,0:T(8,128)(2,1)S(1)}, bf16[1024,128]{1,0:T(8,128)(2,1)S(1)}, u32[]{:S(2)}, u32[]{:S(2)}) collective-permute-start(bf16[1024,128]{1,0:T(8,128)(2,1)S(1)} %get-tuple-element.10.rest_0_), channel_id=1, source_target_pairs={{8,0},{12,4},{16,8},{20,12},{24,16},{28,20},{9,1},{13,5},{17,9},{2... | collective-permute-start | bytes 786440 | tf_op jit(solution)/shard_map/ppermute | solution.py:50
  142.4 11.7 %collective-permute-start.18 = (bf16[1024,128]{1,0:T(8,128)(2,1)S(1)}, bf16[1024,128]{1,0:T(8,128)(2,1)S(1)}, u32[]{:S(2)}, u32[]{:S(2)}) collective-permute-start(bf16[1024,128]{1,0:T(8,128)(2,1)S(1)} %get-tuple-element.10.rest_0_), channel_id=1, source_target_pairs={{0,8},{4,12},{8,16},{12,20},{16,24},{20,28},{1,9},{5,13},{9,17},{1... | collective-permute-start | bytes 786440 | tf_op jit(solution)/shard_map/ppermute | solution.py:51
  147.0 12.8 %collective-permute-start.34 = (bf16[1024,128]{1,0:T(8,128)(2,1)}, bf16[1024,128]{1,0:T(8,128)(2,1)S(1)}, u32[]{:S(2)}, u32[]{:S(2)}) collective-permute-start(bf16[1024,128]{1,0:T(8,128)(2,1)} %collective-permute-done.32.rest_2_), channel_id=1, source_target_pairs={{0,4},{4,0},{8,12},{12,8},{16,20},{20,16},{1,5},{5,1},{9,13},{13,9... | collective-permute-start | bytes 786440 | tf_op jit(solution)/shard_map/ppermute | solution.py:45
  149.5 13.8 %collective-permute-start.35 = (bf16[1024,128]{1,0:T(8,128)(2,1)}, bf16[1024,128]{1,0:T(8,128)(2,1)S(1)}, u32[]{:S(2)}, u32[]{:S(2)}) collective-permute-start(bf16[1024,128]{1,0:T(8,128)(2,1)} %collective-permute-done.33.rest_3_), channel_id=1, source_target_pairs={{8,12},{12,8},{16,20},{20,16},{24,28},{28,24},{9,13},{13,9},{17,21... | collective-permute-start | bytes 786440 | tf_op jit(solution)/shard_map/ppermute | solution.py:45
  151.3 27.4 %collective-permute-start.15 = (bf16[2,1024,128]{2,1,0:T(8,128)(2,1)S(1)}, bf16[2,1024,128]{2,1,0:T(8,128)(2,1)S(1)}, u32[]{:S(2)}, u32[]{:S(2)}) collective-permute-start(bf16[2,1024,128]{2,1,0:T(8,128)(2,1)S(1)} %pad_maximum_fusion.6), channel_id=1, source_target_pairs={{0,4},{4,0},{8,12},{12,8},{16,20},{20,16},{24,28},{28,24},{1,5},{5... | collective-permute-start | bytes 1572872 | tf_op jit(solution)/shard_map/ppermute | solution.py:35
  152.8 12.4 %collective-permute-start.36 = (bf16[1024,128]{1,0:T(8,128)(2,1)}, bf16[1024,128]{1,0:T(8,128)(2,1)S(1)}, u32[]{:S(2)}, u32[]{:S(2)}) collective-permute-start(bf16[1024,128]{1,0:T(8,128)(2,1)} %collective-permute-done.32.rest_2_), channel_id=1, source_target_pairs={{8,0},{12,4},{16,8},{20,12},{24,16},{28,20},{9,1},{13,5},{17,9},{2... | collective-permute-start | bytes 786440 | tf_op jit(solution)/shard_map/ppermute | solution.py:50
  154.1 19.1 %collective-permute-start.37 = (bf16[1024,128]{1,0:T(8,128)(2,1)}, bf16[1024,128]{1,0:T(8,128)(2,1)S(1)}, u32[]{:S(2)}, u32[]{:S(2)}) collective-permute-start(bf16[1024,128]{1,0:T(8,128)(2,1)} %collective-permute-done.33.rest_3_), channel_id=1, source_target_pairs={{0,8},{4,12},{8,16},{12,20},{16,24},{20,28},{1,9},{5,13},{9,17},{1... | collective-permute-start | bytes 786440 | tf_op jit(solution)/shard_map/ppermute | solution.py:51
  159.9 16.8 %collective-permute-start.19 = (bf16[1024,128]{1,0:T(8,128)(2,1)S(1)}, bf16[1024,128]{1,0:T(8,128)(2,1)S(1)}, u32[]{:S(2)}, u32[]{:S(2)}) collective-permute-start(bf16[1024,128]{1,0:T(8,128)(2,1)S(1)} %collective-permute-done.17.rest_2_), channel_id=1, source_target_pairs={{0,4},{4,0},{8,12},{12,8},{16,20},{20,16},{1,5},{5,1},{9,13},{13,9... | collective-permute-start | bytes 786440 | tf_op jit(solution)/shard_map/ppermute | solution.py:45
  163.3 14.7 %collective-permute-start.21 = (bf16[1024,128]{1,0:T(8,128)(2,1)S(1)}, bf16[1024,128]{1,0:T(8,128)(2,1)S(1)}, u32[]{:S(2)}, u32[]{:S(2)}) collective-permute-start(bf16[1024,128]{1,0:T(8,128)(2,1)S(1)} %collective-permute-done.17.rest_2_), channel_id=1, source_target_pairs={{8,0},{12,4},{16,8},{20,12},{24,16},{28,20},{9,1},{13,5},{17,9},{2... | collective-permute-start | bytes 786440 | tf_op jit(solution)/shard_map/ppermute | solution.py:50
  165.2 20.6 %collective-permute-start.22 = (bf16[1024,128]{1,0:T(8,128)(2,1)S(1)}, bf16[1024,128]{1,0:T(8,128)(2,1)S(1)}, u32[]{:S(2)}, u32[]{:S(2)}) collective-permute-start(bf16[1024,128]{1,0:T(8,128)(2,1)S(1)} %collective-permute-done.18.rest_3_), channel_id=1, source_target_pairs={{0,8},{4,12},{8,16},{12,20},{16,24},{20,28},{1,9},{5,13},{9,17},{1... | collective-permute-start | bytes 786440 | tf_op jit(solution)/shard_map/ppermute | solution.py:51
  173.3 13.2 %collective-permute-start.38 = (bf16[1024,128]{1,0:T(8,128)(2,1)S(1)}, bf16[1024,128]{1,0:T(8,128)(2,1)S(1)}, u32[]{:S(2)}, u32[]{:S(2)}) collective-permute-start(bf16[1024,128]{1,0:T(8,128)(2,1)S(1)} %collective-permute-done.36.rest_6_), channel_id=1, source_target_pairs={{0,4},{4,0},{8,12},{12,8},{1,5},{5,1},{9,13},{13,9},{2,6},{6,2},{1... | collective-permute-start | bytes 786440 | tf_op jit(solution)/shard_map/ppermute | solution.py:45
  176.7 21.0 %collective-permute-start.40 = (bf16[1024,128]{1,0:T(8,128)(2,1)S(1)}, bf16[1024,128]{1,0:T(8,128)(2,1)S(1)}, u32[]{:S(2)}, u32[]{:S(2)}) collective-permute-start(bf16[1024,128]{1,0:T(8,128)(2,1)S(1)} %collective-permute-done.36.rest_6_), channel_id=1, source_target_pairs={{8,0},{12,4},{16,8},{20,12},{24,16},{28,20},{9,1},{13,5},{17,9},{2... | collective-permute-start | bytes 786440 | tf_op jit(solution)/shard_map/ppermute | solution.py:50
  178.0 9.8 %collective-permute-start.39 = (bf16[1024,128]{1,0:T(8,128)(2,1)S(1)}, bf16[1024,128]{1,0:T(8,128)(2,1)S(1)}, u32[]{:S(2)}, u32[]{:S(2)}) collective-permute-start(bf16[1024,128]{1,0:T(8,128)(2,1)S(1)} %collective-permute-done.37.rest_7_), channel_id=1, source_target_pairs={{16,20},{20,16},{24,28},{28,24},{17,21},{21,17},{25,29},{29,25},{1... | collective-permute-start | bytes 786440 | tf_op jit(solution)/shard_map/ppermute | solution.py:45
  178.7 22.0 %collective-permute-start.41 = (bf16[1024,128]{1,0:T(8,128)(2,1)S(1)}, bf16[1024,128]{1,0:T(8,128)(2,1)S(1)}, u32[]{:S(2)}, u32[]{:S(2)}) collective-permute-start(bf16[1024,128]{1,0:T(8,128)(2,1)S(1)} %collective-permute-done.37.rest_7_), channel_id=1, source_target_pairs={{0,8},{4,12},{8,16},{12,20},{16,24},{20,28},{1,9},{5,13},{9,17},{1... | collective-permute-start | bytes 786440 | tf_op jit(solution)/shard_map/ppermute | solution.py:51
  185.8 50.1 %collective-permute-start.20 = (bf16[1024,128]{1,0:T(8,128)(2,1)S(1)}, bf16[1024,128]{1,0:T(8,128)(2,1)S(1)}, u32[]{:S(2)}, u32[]{:S(2)}) collective-permute-start(bf16[1024,128]{1,0:T(8,128)(2,1)S(1)} %collective-permute-done.18.rest_3_), channel_id=1, source_target_pairs={{8,12},{12,8},{16,20},{20,16},{24,28},{28,24},{9,13},{13,9},{17,21... | collective-permute-start | bytes 786440 | tf_op jit(solution)/shard_map/ppermute | solution.py:45
  186.5 32.2 %collective-permute-start.25 = (bf16[1024,128]{1,0:T(8,128)(2,1)S(1)}, bf16[1024,128]{1,0:T(8,128)(2,1)S(1)}, u32[]{:S(2)}, u32[]{:S(2)}) collective-permute-start(bf16[1024,128]{1,0:T(8,128)(2,1)S(1)} %collective-permute-done.21.rest_6_), channel_id=1, source_target_pairs={{8,0},{12,4},{16,8},{20,12},{24,16},{28,20},{9,1},{13,5},{17,9},{2... | collective-permute-start | bytes 786440 | tf_op jit(solution)/shard_map/ppermute | solution.py:50
  187.8 33.7 %collective-permute-start.26 = (bf16[1024,128]{1,0:T(8,128)(2,1)S(1)}, bf16[1024,128]{1,0:T(8,128)(2,1)S(1)}, u32[]{:S(2)}, u32[]{:S(2)}) collective-permute-start(bf16[1024,128]{1,0:T(8,128)(2,1)S(1)} %collective-permute-done.22.rest_7_), channel_id=1, source_target_pairs={{0,8},{4,12},{8,16},{12,20},{16,24},{20,28},{1,9},{5,13},{9,17},{1... | collective-permute-start | bytes 786440 | tf_op jit(solution)/shard_map/ppermute | solution.py:51
  197.7 24.6 %collective-permute-start.42 = (bf16[1024,128]{1,0:T(8,128)(2,1)S(1)}, bf16[1024,128]{1,0:T(8,128)(2,1)S(1)}, u32[]{:S(2)}, u32[]{:S(2)}) collective-permute-start(bf16[1024,128]{1,0:T(8,128)(2,1)S(1)} %collective-permute-done.40.rest_10_), channel_id=1, source_target_pairs={{0,4},{4,0},{1,5},{5,1},{2,6},{6,2},{3,7},{7,3}} | collective-permute-start | bytes 786440 | tf_op jit(solution)/shard_map/ppermute | solution.py:45
  200.8 24.6 %collective-permute-start.43 = (bf16[1024,128]{1,0:T(8,128)(2,1)S(1)}, bf16[1024,128]{1,0:T(8,128)(2,1)S(1)}, u32[]{:S(2)}, u32[]{:S(2)}) collective-permute-start(bf16[1024,128]{1,0:T(8,128)(2,1)S(1)} %collective-permute-done.41.rest_11_), channel_id=1, source_target_pairs={{24,28},{28,24},{25,29},{29,25},{26,30},{30,26},{27,31},{31,27}} | collective-permute-start | bytes 786440 | tf_op jit(solution)/shard_map/ppermute | solution.py:45
  218.8 17.2 %collective-permute-start.23 = (bf16[1024,128]{1,0:T(8,128)(2,1)S(1)}, bf16[1024,128]{1,0:T(8,128)(2,1)S(1)}, u32[]{:S(2)}, u32[]{:S(2)}) collective-permute-start(bf16[1024,128]{1,0:T(8,128)(2,1)S(1)} %collective-permute-done.21.rest_6_), channel_id=1, source_target_pairs={{0,4},{4,0},{8,12},{12,8},{1,5},{5,1},{9,13},{13,9},{2,6},{6,2},{1... | collective-permute-start | bytes 786440 | tf_op jit(solution)/shard_map/ppermute | solution.py:45
  221.6 14.4 %collective-permute-start.24 = (bf16[1024,128]{1,0:T(8,128)(2,1)S(1)}, bf16[1024,128]{1,0:T(8,128)(2,1)S(1)}, u32[]{:S(2)}, u32[]{:S(2)}) collective-permute-start(bf16[1024,128]{1,0:T(8,128)(2,1)S(1)} %collective-permute-done.22.rest_7_), channel_id=1, source_target_pairs={{16,20},{20,16},{24,28},{28,24},{17,21},{21,17},{25,29},{29,25},{1... | collective-permute-start | bytes 786440 | tf_op jit(solution)/shard_map/ppermute | solution.py:45
  222.3 13.7 %collective-permute-start.27 = (bf16[1024,128]{1,0:T(8,128)(2,1)S(1)}, bf16[1024,128]{1,0:T(8,128)(2,1)S(1)}, u32[]{:S(2)}, u32[]{:S(2)}) collective-permute-start(bf16[1024,128]{1,0:T(8,128)(2,1)S(1)} %collective-permute-done.25.rest_10_), channel_id=1, source_target_pairs={{0,4},{4,0},{1,5},{5,1},{2,6},{6,2},{3,7},{7,3}} | collective-permute-start | bytes 786440 | tf_op jit(solution)/shard_map/ppermute | solution.py:45
  225.4 10.6 %collective-permute-start.28 = (bf16[1024,128]{1,0:T(8,128)(2,1)S(1)}, bf16[1024,128]{1,0:T(8,128)(2,1)S(1)}, u32[]{:S(2)}, u32[]{:S(2)}) collective-permute-start(bf16[1024,128]{1,0:T(8,128)(2,1)S(1)} %collective-permute-done.26.rest_11_), channel_id=1, source_target_pairs={{24,28},{28,24},{25,29},{29,25},{26,30},{30,26},{27,31},{31,27}} | collective-permute-start | bytes 786440 | tf_op jit(solution)/shard_map/ppermute | solution.py:45
  235.9 13.9 %collective-permute-start.44 = (bf16[2,256,1024]{2,1,0:T(8,128)(2,1)}, bf16[2,256,1024]{2,1,0:T(8,128)(2,1)}, u32[]{:S(2)}, u32[]{:S(2)}) collective-permute-start(bf16[2,256,1024]{2,1,0:T(8,128)(2,1)} %slice.87), channel_id=1, source_target_pairs={{0,1},{1,0},{2,3},{3,2},{4,5},{5,4},{6,7},{7,6},{8,9},{9,8},{10,11... | collective-permute-start | bytes 3145736 | tf_op jit(solution)/shard_map/ppermute | solution.py:35
  247.4 6.2 %collective-permute-start.29 = (bf16[2,256,1024]{2,1,0:T(8,128)(2,1)}, bf16[2,256,1024]{2,1,0:T(8,128)(2,1)}, u32[]{:S(2)}, u32[]{:S(2)}) collective-permute-start(bf16[2,256,1024]{2,1,0:T(8,128)(2,1)} %slice.82), channel_id=1, source_target_pairs={{0,1},{1,0},{2,3},{3,2},{4,5},{5,4},{6,7},{7,6},{8,9},{9,8},{10,11... | collective-permute-start | bytes 3145736 | tf_op jit(solution)/shard_map/ppermute | solution.py:35
  252.0 14.8 %collective-permute-start.45 = (bf16[1,256,1024]{2,1,0:T(8,128)(2,1)S(1)}, bf16[1,256,1024]{2,1,0:T(8,128)(2,1)S(1)}, u32[]{:S(2)}, u32[]{:S(2)}) collective-permute-start(bf16[1,256,1024]{2,1,0:T(8,128)(2,1)S(1)} %slice.89), channel_id=1, source_target_pairs={{0,2},{1,3},{2,0},{3,1},{4,6},{5,7},{6,4},{7,5},{8,10},{9,11},{10,... | collective-permute-start | bytes 1572872 | tf_op jit(solution)/shard_map/ppermute | solution.py:35
  255.3 21.9 %collective-permute-start.30 = (bf16[1,256,1024]{2,1,0:T(8,128)(2,1)S(1)}, bf16[1,256,1024]{2,1,0:T(8,128)(2,1)S(1)}, u32[]{:S(2)}, u32[]{:S(2)}) collective-permute-start(bf16[1,256,1024]{2,1,0:T(8,128)(2,1)S(1)} %slice.84), channel_id=1, source_target_pairs={{0,2},{1,3},{2,0},{3,1},{4,6},{5,7},{6,4},{7,5},{8,10},{9,11},{10,... | collective-permute-start | bytes 1572872 | tf_op jit(solution)/shard_map/ppermute | solution.py:35
  311.1 18.8 %all-to-all-start.1 = ((bf16[4,64,2048]{2,1,0:T(8,128)(2,1)}), bf16[4,64,2048]{2,1,0:T(8,128)(2,1)}, u32[]{:S(2)}, u32[]{:S(2)}) async-start(bf16[4,64,2048]{2,1,0:T(8,128)(2,1)} %bitcast.67), calls=%async_computation.1 | async-start | bytes 2097152 | tf_op jit(solution)/shard_map/all_to_all | solution.py:415
  (45 other events, 1018.6 us)

commit v2 on v1

v2 whole, which is shorter than its diff:
```python
import functools
import math

import jax
import jax.numpy as jnp
from jax import lax
from jax.experimental import pallas as pl
from jax.experimental.pallas import tpu as pltpu
from jax.sharding import PartitionSpec as P

QUERY_HEADS = 32
KEY_VALUE_HEADS = 4
HEAD_DIMENSION = 128

epsilon = 1e-06
rope_theta = 1000000.0
VMEM_LIMIT = 56 * 1024 * 1024
STAGE_WIDTH = 128
FREE = pl.CostEstimate(flops=0, bytes_accessed=0, transcendentals=0)


def norm_rows(values, gain_vector):
    widened = values.astype(jnp.float32)
    inverse_rms = lax.rsqrt(jnp.mean(widened * widened, axis=-1, keepdims=True) + epsilon)
    return widened * inverse_rms * gain_vector


def local_positions(parity, row_count):
    indices = jnp.arange(row_count)
    quarter = row_count // 2
    offset = jnp.where(parity == 0, jnp.where(indices < quarter, 0, 2 * quarter), quarter)
    return indices + offset


def from_xor(block, axis, mask):
    count = lax.axis_size(axis)
    return lax.ppermute(block, axis, [(i, i ^ mask) for i in range(count)])


def cross(block):
    return from_xor(block, "group", 1)


def after(block, *others):
    return lax.optimization_barrier((block, *others))[0]


LINE = ((0, 1, 2, 3), (1, 0, 2, 3), (2, 3, 1, 0), (3, 2, 1, 0))
PAIRS = ((0, 1), (1, 0), (2, 3), (3, 2))
MIDDLE = ((1, 2), (2, 1))
OUTWARD = ((1, 0), (2, 3))


def along(block, moves):
    return lax.ppermute(block, "group", [(2 * a + s, 2 * b + s) for a, b in moves for s in range(2)])


def line_rounds(block):
    place = lax.axis_index("group") // 2
    edge = (place == 0) | (place == 3)
    crossed = [None] * 4
    crossed[0], near, inner = yield cross(block), along(block, PAIRS), along(block, MIDDLE)
    crossed[1], inner_far, outer = yield cross(near), along(near, MIDDLE), along(inner, OUTWARD)
    third = jnp.where(edge, outer, inner)
    crossed[2], outer = yield cross(third), along(inner_far, OUTWARD)
    fourth = jnp.where(edge, outer, inner_far)
    (crossed[3],) = yield (cross(fourth),)
    return [block, near, third, fourth] + crossed


def advance(rounds, results=None):
    try:
        return lax.optimization_barrier(rounds.send(results)), None
    except StopIteration as end:
        return None, end.value


def gather_chain(block, start=(), ready=()):
    if lax.axis_size("group") != 8:
        return [(block,)] * 4, list(lax.all_gather(block, "group"))
    chain = line_rounds(after(block, *start))
    brought = [None]
    for step in range(4):
        if step == 3 and ready:
            brought[-1] = after(brought[-1], *ready)
        brought.append(advance(chain, brought[-1])[0])
    return brought[1:], advance(chain, brought[-1])[1]


def held_groups(place, side):
    groups = lax.axis_size("group")
    if groups != 8:
        return jnp.arange(groups)
    places = jnp.sum(jnp.where(jnp.arange(4)[:, None] == place, jnp.array(LINE, jnp.int32), 0), axis=0)
    return jnp.concatenate([2 * places + side, 2 * places + 1 - side])


def doubling_masks(count):
    masks, stride = [0], count // 2
    while stride:
        masks = masks + [mask ^ stride for mask in masks]
        stride //= 2
    return masks


def gather_tokens(rows):
    blocks = [rows]
    stride = lax.axis_size("expert") // 2
    while stride:
        blocks = blocks + [from_xor(block, "expert", stride) for block in blocks]
        stride //= 2
    return blocks


def scatter_sum(kept, sent):
    stride = 1
    while True:
        half = kept.shape[0] // 2
        arrived = from_xor(sent, "expert", stride)
        if not half:
            return kept[0], arrived[0]
        summed = [
            kept[part].astype(jnp.float32) + arrived[part].astype(jnp.float32)
            for part in (slice(None, half), slice(half, None))
        ]
        kept, sent = [part.astype(jnp.bfloat16) for part in summed]
        stride *= 2


def stack_shards(meta, shard_refs, weights):
    depth = weights.shape[0] // len(shard_refs)
    for index, ref in enumerate(shard_refs):
        weights[pl.ds(pl.multiple_of(meta[index] * depth, depth), depth), :] = ref[...]


def turn(values, cosines, sines, mixer):
    values = values.astype(jnp.bfloat16)
    wide = values.astype(jnp.float32)
    both = jnp.concatenate([values, (wide * wide).astype(jnp.bfloat16)], axis=1)
    mixed = jnp.dot(both, mixer, preferred_element_type=jnp.float32)
    dim = values.shape[1]
    inverse = lax.rsqrt(mixed[:, dim:] + epsilon)
    return ((wide * cosines + mixed[:, :dim] * sines) * inverse).astype(jnp.bfloat16)


def query_kernel(shard_count, meta, rows, cosine, sine, mixer, *rest):
    count, tile, width = rows.shape
    dim = HEAD_DIMENSION
    if shard_count > 1:
        query_out, weights = rest[shard_count:]
        stack_shards(meta, rest[:shard_count], weights)
        columns = weights[...]
    else:
        query_out = rest[1]
        columns = rest[0][...].reshape(width, 2 * dim)
    projected = jnp.dot(rows[...].reshape(count * tile, width), columns, preferred_element_type=jnp.float32)
    for block in range(count):
        spot = pl.ds(pl.multiple_of(meta[meta.shape[0] - count + block] * tile, tile), tile)
        here = slice(block * tile, (block + 1) * tile)
        for head in range(2):
            query_out[head, here, :] = turn(
                projected[here, head * dim : (head + 1) * dim], cosine[spot, :], sine[spot, :], mixer[...]
            )


def key_kernel(shard_count, meta, rows, cosine, sine, mixer, *rest):
    pair_out, weights = rest[shard_count:]
    stack_shards(meta, rest[:shard_count], weights)
    count, tile, width = rows.shape
    dim = HEAD_DIMENSION
    projected = jnp.dot(
        rows[...].reshape(count * tile, width), weights[...], preferred_element_type=jnp.float32
    )
    for block in range(count):
        spot = pl.ds(pl.multiple_of(meta[shard_count + block] * tile, tile), tile)
        here = slice(block * tile, (block + 1) * tile)
        pair_out[0, spot, :] = turn(projected[here, :dim], cosine[spot, :], sine[spot, :], mixer[...])
        pair_out[1, spot, :] = projected[here, dim:].astype(jnp.bfloat16)


def project(kernel, first, steps, meta, blocks, shards, cosine, sine, mixer):
    count, tile, width = blocks.shape
    dim = HEAD_DIMENSION
    shard_count = len(shards)
    if shard_count > 1:
        shard = pl.BlockSpec((shards[0].shape[0], 2 * dim), lambda n, meta: (0, first + n))
        scratch = [pltpu.VMEM((width, 2 * dim), jnp.bfloat16)]
    else:
        shard = pl.BlockSpec((*shards[0].shape[:2], 2 * dim), lambda n, meta: (0, 0, first + n))
        scratch = []
    table = pl.BlockSpec((count * tile, dim), lambda n, meta: (0, 0))
    return pl.pallas_call(
        functools.partial(kernel, shard_count),
        grid_spec=pltpu.PrefetchScalarGridSpec(
            num_scalar_prefetch=1,
            grid=(steps,),
            in_specs=[
                pl.BlockSpec((count, tile, width), lambda n, meta: (0, 0, 0)),
                table,
                table,
                pl.BlockSpec((2 * dim, 2 * dim), lambda n, meta: (0, 0)),
            ]
            + [shard] * shard_count,
            out_specs=pl.BlockSpec((2, count * tile, dim), lambda n, meta: (n, 0, 0)),
            scratch_shapes=scratch,
        ),
        out_shape=jax.ShapeDtypeStruct((2 * steps, count * tile, dim), jnp.bfloat16),
        compiler_params=pltpu.CompilerParams(vmem_limit_bytes=VMEM_LIMIT),
        cost_estimate=pl.CostEstimate(
            flops=4 * steps * count * tile * width * dim,
            bytes_accessed=2 * (count * tile * width + steps * 2 * dim * (width + count * tile)),
            transcendentals=0,
        ),
    )(meta, blocks, cosine, sine, mixer, *shards)


def attend_kernel(tile, meta, own, far, *rest):
    *queries, out, keys, values, total = rest
    heads, dim = total.shape[0], HEAD_DIMENSION
    query = [part.at[head] for part in queries for head in range(part.shape[0])]
    row_count = own.shape[1]
    half = row_count // 2
    parity, length = meta[0], meta[1]
    step = pl.program_id(0)

    @pl.when(step == 0)
    def _():
        ones = jnp.ones((half, dim), jnp.bfloat16)
        for pair, whose in ((own, parity), (far, 1 - parity)):
            for part in range(2):
                base = jnp.where(whose == 0, 3 * half * part, half * (1 + part))
                base = pl.multiple_of(base, half)
                source = pl.ds(part * half, half)
                keys[pl.ds(base, half), :] = pair[0, source, :]
                valid = base + lax.broadcasted_iota(jnp.int32, (half, dim), 0) < length
                zero = jnp.zeros((half, dim), jnp.bfloat16)
                values[pl.ds(base, half), :dim] = jnp.where(valid, pair[1, source, :], zero)
                values[pl.ds(base, half), dim:] = jnp.where(valid, ones, zero)

    first = meta[2 + step] * tile
    first = first + jnp.where(parity == 0, jnp.where(first < half, 0, 2 * half), half)

    def weigh(head, start, width, masked):
        scores = lax.dot_general(
            query[head][...], keys[pl.ds(start, width), :], (((1,), (1,)), ((), ())),
            preferred_element_type=jnp.float32,
        )
        weights = jnp.exp2(scores)
        if masked:
            below = lax.broadcasted_iota(jnp.int32, weights.shape, 1) <= lax.broadcasted_iota(
                jnp.int32, weights.shape, 0
            )
            weights = jnp.where(below, weights, 0.0)
        return jnp.dot(
            weights.astype(jnp.bfloat16), values[pl.ds(start, width), :], preferred_element_type=jnp.float32
        )

    diagonal = pl.multiple_of(first, tile)
    for head in range(heads):
        total[head] = weigh(head, diagonal, tile, True)

    def wide(index, _):
        start = pl.multiple_of(index * half, half)
        for head in range(heads):
            total[head] += weigh(head, start, half, False)
        return 0

    lax.fori_loop(0, first // half, wide, 0)

    def narrow(index, _):
        start = pl.multiple_of(index * tile, tile)
        for head in range(heads):
            total[head] += weigh(head, start, tile, False)
        return 0

    lax.fori_loop(first // half * (half // tile), first // tile, narrow, 0)
    for head in range(heads):
        summed = total[head]
        out[:, head * dim : (head + 1) * dim] = (summed[:, :dim] / summed[:, dim:]).astype(jnp.bfloat16)


def attend(meta, queries, own, far, tile):
    _, row_count, dim = queries[0].shape
    heads = sum(part.shape[0] for part in queries)
    whole = pl.BlockSpec((2, row_count, dim), lambda i, meta: (0, 0, 0))
    return pl.pallas_call(
        functools.partial(attend_kernel, tile),
        grid_spec=pltpu.PrefetchScalarGridSpec(
            num_scalar_prefetch=1,
            grid=(row_count // tile,),
            in_specs=[whole] * 2
            + [pl.BlockSpec((part.shape[0], tile, dim), lambda i, meta: (0, i, 0)) for part in queries],
            out_specs=pl.BlockSpec((tile, heads * dim), lambda i, meta: (i, 0)),
            scratch_shapes=[
                pltpu.VMEM((2 * row_count, dim), jnp.bfloat16),
                pltpu.VMEM((2 * row_count, 2 * dim), jnp.bfloat16),
                pltpu.VMEM((heads, tile, 2 * dim), jnp.float32),
            ],
        ),
        out_shape=jax.ShapeDtypeStruct((row_count, heads * dim), jnp.bfloat16),
        compiler_params=pltpu.CompilerParams(vmem_limit_bytes=VMEM_LIMIT),
        cost_estimate=FREE,
    )(meta, own, far, *queries)


def output_kernel(shard_count, meta, rows, *rest):
    kept, sent, weights = rest[shard_count:]
    width = STAGE_WIDTH
    if shard_count > 1:
        shards = [ref[...] for ref in rest[:shard_count]]
    else:
        shards = [rest[0][group] for group in range(rest[0].shape[0])]
    for index, shard in enumerate(shards):
        weights[:, pl.ds(pl.multiple_of(meta[index] * width, width), width)] = shard
    half = rows.shape[0] // 2
    for part, out in enumerate((kept, sent)):
        left = rows[part * half : (part + 1) * half].reshape(-1, rows.shape[2])
        product = jnp.dot(left, weights[...], preferred_element_type=jnp.float32)
        out[...] = product.astype(jnp.bfloat16).reshape(out.shape)


def output_part(meta, rows, shards, groups):
    count, tile, depth = rows.shape
    half, width = count // 2, groups * STAGE_WIDTH

    def whole(shape):
        return pl.BlockSpec(shape, lambda n, meta: (0,) * len(shape))

    return pl.pallas_call(
        functools.partial(output_kernel, len(shards)),
        grid_spec=pltpu.PrefetchScalarGridSpec(
            num_scalar_prefetch=1,
            grid=(1,),
            in_specs=[whole(rows.shape)] + [whole(shard.shape) for shard in shards],
            out_specs=[whole((half, tile, width))] * 2,
            scratch_shapes=[pltpu.VMEM((depth, width), jnp.bfloat16)],
        ),
        out_shape=[jax.ShapeDtypeStruct((half, tile, width), jnp.bfloat16)] * 2,
        compiler_params=pltpu.CompilerParams(vmem_limit_bytes=VMEM_LIMIT),
        cost_estimate=FREE,
    )(meta, rows, *shards)


def finish_kernel(states, gain, *rest):
    *terms, hidden_out, normed_out = rest
    stages = len(terms) // 2
    width = STAGE_WIDTH
    for stage in range(stages):
        total = terms[2 * stage][...].astype(jnp.float32) + terms[2 * stage + 1][...].astype(jnp.float32)
        for group in range(total.shape[1] // width):
            start = (group * stages + stage) * width
            here = slice(start, start + width)
            value = states[:, here].astype(jnp.float32) + total[:, group * width : (group + 1) * width]
            hidden_out[:, here] = value.astype(jnp.bfloat16)
    hidden = hidden_out[...].astype(jnp.float32)
    inverse = lax.rsqrt(jnp.mean(hidden * hidden, axis=-1, keepdims=True) + epsilon)
    normed_out[...] = (hidden * inverse * gain[...]).astype(jnp.bfloat16)


def finish(states, gain, terms):
    rows, width = states.shape
    tile = min(64, rows)

    def block(columns):
        return pl.BlockSpec((tile, columns), lambda i: (i, 0))

    return pl.pallas_call(
        finish_kernel,
        grid=(rows // tile,),
        in_specs=[block(width), pl.BlockSpec((1, width), lambda i: (0, 0))]
        + [block(term.shape[1]) for term in terms],
        out_specs=[block(width)] * 2,
        out_shape=[jax.ShapeDtypeStruct((rows, width), jnp.bfloat16)] * 2,
        compiler_params=pltpu.CompilerParams(vmem_limit_bytes=VMEM_LIMIT),
        cost_estimate=FREE,
    )(states, gain[None, :], *terms)


def per_device(
    hidden_in,
    norm_attention,
    norm_experts,
    query_master,
    trainer_key_value_weight,
    output_master,
    query_gain,
    key_gain,
    lengths,
    router,
    expert_gateup,
    expert_down,
    routes,
):
    experts_axis = lax.axis_size("expert")
    group_member = lax.axis_index("expert")
    group_index = lax.axis_index("group")
    heads = QUERY_HEADS // experts_axis
    dim = HEAD_DIMENSION
    rows_here, model_width = hidden_in.shape
    local_rows = rows_here * experts_axis

    groups = lax.axis_size("group")
    place, side = group_index // 2, group_index % 2
    common_head = group_member * heads // (QUERY_HEADS // KEY_VALUE_HEADS)
    pair = lax.dynamic_slice_in_dim(trainer_key_value_weight, common_head * dim, dim, 2)
    joined = jnp.concatenate([pair[0], pair[1]], axis=1).astype(jnp.bfloat16)
    query_all = lax.all_gather(query_master.astype(jnp.bfloat16), "group")
    stages = output_master.shape[1] // STAGE_WIDTH
    output_here = [
        output_master[:, stage * STAGE_WIDTH : (stage + 1) * STAGE_WIDTH].astype(jnp.bfloat16)
        for stage in range(stages)
    ]
    blocks = gather_tokens(after(hidden_in, joined))
    normed = jnp.stack([norm_rows(block, norm_attention).astype(jnp.bfloat16) for block in blocks])
    pair_rounds, pair_shards = gather_chain(joined)

    masks = doubling_masks(experts_axis)
    block_order = jnp.bitwise_xor(group_member, jnp.array(masks, jnp.int32))
    held = held_groups(place, side)
    meta = jnp.concatenate([held, block_order]).astype(jnp.int32)

    parity = side
    own_places = local_positions(parity, local_rows).astype(jnp.float32)
    exponents = jnp.arange(dim // 2).astype(jnp.float32)
    inverse = jnp.exp(exponents * (-2.0 * math.log(rope_theta) / dim))
    angles = own_places[:, None] * inverse[None, :]
    cosine_values, sine_values = jnp.cos(angles), jnp.sin(angles)
    cosine = jnp.concatenate([cosine_values, cosine_values], axis=1)
    sine = jnp.concatenate([-sine_values, sine_values], axis=1)

    def tables(gain):
        return cosine * gain, sine * jnp.roll(gain, dim // 2)

    lanes = jnp.arange(dim)
    swap = (lanes[:, None] == (lanes[None, :] + dim // 2) % dim).astype(jnp.float32)
    nothing = jnp.zeros((dim, dim), jnp.float32)
    mixer = jnp.block([[swap, nothing], [nothing, nothing + 1.0 / dim]]).astype(jnp.bfloat16)
    query_tables = tables(query_gain * (dim**-0.5 * math.log2(math.e)))
    key_tables = tables(key_gain)
    own_pair = project(key_kernel, 0, 1, meta, normed, pair_shards, *key_tables, mixer)
    far_pair = cross(own_pair)
    _, output_shards = gather_chain(output_here[0], pair_rounds[-1], (far_pair,))
    stage_shards = [output_shards] + [[lax.all_gather(part, "group")] for part in output_here[1:]]
    queries = [project(query_kernel, 0, heads // 2, meta, normed, [query_all], *query_tables, mixer)]

    valid_length = jnp.sum(jnp.where(jnp.arange(lengths.shape[0]) == group_index // 2, lengths, 0))
    attend_meta = jnp.concatenate([jnp.stack([parity, valid_length]), block_order]).astype(jnp.int32)
    attended = attend(attend_meta, queries, own_pair, far_pair, rows_here)

    attended = attended.reshape(experts_axis, rows_here, heads * dim)
    terms = []
    for stage, shards in enumerate(stage_shards):
        order = held if len(shards) > 1 else jnp.arange(groups)
        terms += scatter_sum(*output_part(order.astype(jnp.int32), attended, shards, groups))
    hidden, normed_second = finish(hidden_in, norm_experts, terms)

    logits = jnp.dot(normed_second, router, preferred_element_type=jnp.float32)
    route_table = routes[:, :, None] == jnp.arange(logits.shape[1])[None, None, :]
    picked = jnp.sum(jnp.where(route_table, logits[:, None, :], 0.0), axis=-1)
    raised = jnp.exp(picked)
    gate_values = raised / jnp.sum(raised, axis=1, keepdims=True)
    inside = routes < experts_axis
    gate_window = jnp.sum(jnp.where(inside, gate_values, 0.0), axis=1)
    expert_window = jnp.sum(jnp.where(inside, routes, 0), axis=1)
    present = jnp.any(inside, axis=1)
    capacity = local_rows // (experts_axis * experts_axis)
    member_table = (present[:, None] & (expert_window[:, None] == block_order[None, :])).astype(jnp.int32)
    ranking = jnp.cumsum(member_table, axis=0) - 1
    slot_index = jnp.sum(member_table * (ranking + jnp.arange(experts_axis) * capacity), axis=1)
    select = (
        (jnp.arange(experts_axis * capacity)[:, None] == slot_index[None, :]) & present[None, :]
    ).astype(jnp.bfloat16)
    outgoing = (
        jnp.dot(select, normed_second, preferred_element_type=jnp.float32)
        .astype(jnp.bfloat16)
        .reshape(experts_axis, capacity, model_width)
    )

    def exchange(slots):
        return jnp.stack([slots[0]] + [from_xor(slots[j], "expert", masks[j]) for j in range(1, experts_axis)])

    gateup_here = expert_gateup[0]
    down_here = expert_down[0]
    hidden_units = down_here.shape[0]
    slot_items = exchange(outgoing)
    flattened = slot_items.reshape(-1, slot_items.shape[-1])
    gate_up = jnp.dot(flattened, gateup_here, preferred_element_type=jnp.float32)
    active = (jax.nn.silu(gate_up[:, :hidden_units]) * gate_up[:, hidden_units:]).astype(
        jnp.bfloat16
    )
    result = (
        jnp.dot(active, down_here, preferred_element_type=jnp.float32)
        .astype(jnp.bfloat16)
        .reshape(slot_items.shape)
    )
    returned = exchange(result)
    combined = jnp.dot(
        jnp.transpose(select), returned.reshape(-1, model_width), preferred_element_type=jnp.float32
    )
    expert_mix = (gate_window[:, None] * combined).astype(jnp.bfloat16)
    return (hidden, expert_mix)


def solution(mesh):
    return jax.shard_map(
        per_device,
        mesh=mesh,
        in_specs=(
            P(("group", "expert"), None),
            P(),
            P(),
            P("group", "expert"),
            P(None, "group", None),
            P("expert", "group"),
            P(),
            P(),
            P(),
            P(),
            P("expert", None, None),
            P("expert", None, None),
            P(("group", "expert"), None),
        ),
        out_specs=(P(("group", "expert"), None), P(("group", "expert"), None)),
        check_vma=False,
    )
```

time: 334 us -> 250 us (0.75)
  the two profiles are of different devices: /device:TPU:0 before, /device:TPU:8 now
where the time goes in v2:
time: 250 us; the launch traced here: 249 us
  waiting for transfers between devices  88.7 us (35%)
  Pallas kernels  53.7 us (21%)
  starting transfers between devices  41.7 us (17%)
  other arithmetic  37.1 us (15%)
  between operations  14.7 us (6%)
  matrix products  9.28 us (4%)
  local copies, waits for them, and re-layouts  3.95 us (2%)
    ppermute x22, waiting for transfers between devices, from_xor(): return lax.ppermute(block, axis, [(i, i ^ mask) for i in range(count)])  73.5 us
    ppermute x10, starting transfers between devices, along(): lax.ppermute(block, 'group', [(2 * a + s, 2 * b + s) for a, b in moves fo...  24.2 us
    pallas_call x2, Pallas kernels, project(): pl.pallas_call(functools.partial(kernel, shard_count), grid_spec=pltpu.Pr...  18.3 us
    ppermute x22, starting transfers between devices, from_xor(): return lax.ppermute(block, axis, [(i, i ^ mask) for i in range(count)])  17.4 us
    pallas_call x1, Pallas kernels, attend(): pl.pallas_call(functools.partial(attend_kernel, tile), grid_spec=pltpu.Pr...  17 us
    ppermute x10, waiting for transfers between devices, along(): lax.ppermute(block, 'group', [(2 * a + s, 2 * b + s) for a, b in moves fo...  15.2 us
    pallas_call x2, Pallas kernels, output_part(): pl.pallas_call(functools.partial(output_kernel, len(shards)), grid_spec=p...  14.1 us
    convert_element_type x2, other arithmetic, scatter_sum(): kept, sent = [part.astype(jnp.bfloat16) for part in summed]  5.55 us
  transfers between devices with their start and end apart: 34, of which 15 were waited for; matrix products, arithmetic and copies ran while one was open for 15% of the time, Pallas kernels for 20%

profile of v2, /device:TPU:8, one launch (start us, length us, event | category | flops | bytes accessed | tf_op | source)
XLA Modules:
  0.0 249.2 jit_solution(3400150700248822180)
XLA Ops:
  7.2 2.3 convert_element_type.110
  10.6 1.6 collective-permute-start
  12.2 1.5 collective-permute-start.3
  14.1 4.6 %collective-permute-start.5 = (bf16[256,256]{1,0:T(8,128)(2,1)S(1)}, bf16[256,256]{1,0:T(8,128)(2,1)}, u32[]{:S(2)}, u32[]{:S(2)}) collective-permute-start(bf16[256,256]{1,0:T(8,128)(2,1)S(1)} %pad_maximum_fusion.5.rest_0_), channel_id=1, source_target_pairs={{8,16},{12,20},{16,8},{20,12},{9,17},{13,21},{17,9},{21,13},{10,18... | collective-permute-start | bytes 393224 | tf_op jit(solution)/shard_map/ppermute | solution.py:55
  18.7 1.4 convert.24
  24.2 2.6 %fusion.34 = (f32[1024,64]{1,0:T(8,128)S(1)}, f32[1024,64]{1,0:T(8,128)S(1)}, f32[1024,64]{1,0:T(8,128)S(1)}) fusion(f32[64]{0:T(128)} %multiply_exponential_fusion, f32[1024]{0:T(1024)S(1)} %add_convert_fusion.4), kind=kLoop, calls=%fused_computation.61 | loop fusion | flops 131072 | bytes 790784 | tf_op jit(solution)/shard_map/neg | solution.py:429
  26.9 2.3 fusion.27
  30.4 2.2 collective-permute-start.7
  32.6 1.9 collective-permute-start.8
  35.2 7.1 %collective-permute-done.7 = bf16[256,256]{1,0:T(8,128)(2,1)} collective-permute-done((bf16[256,256]{1,0:T(8,128)(2,1)}, bf16[256,256]{1,0:T(8,128)(2,1)}, u32[]{:S(2)}, u32[]{:S(2)}) %collective-permute-start.7) | collective-permute-done | bytes 131104 | tf_op jit(solution)/shard_map/ppermute | solution.py:55
  43.2 1.5 collective-permute-start.9
  44.8 2.1 collective-permute-start.10
  46.9 1.5 fusion.8
  48.6 7.1 %collective-permute-done.10 = bf16[256,256]{1,0:T(8,128)(2,1)S(1)} collective-permute-done((bf16[256,256]{1,0:T(8,128)(2,1)}, bf16[256,256]{1,0:T(8,128)(2,1)S(1)}, u32[]{:S(2)}, u32[]{:S(2)}) %collective-permute-start.10) | collective-permute-done | bytes 131104 | tf_op jit(solution)/shard_map/ppermute | solution.py:55
  57.4 8.4 %collective-permute-done.11.rest_7_ = bf16[256,256]{1,0:T(8,128)(2,1)S(1)} collective-permute-done((bf16[256,256]{1,0:T(8,128)(2,1)S(1)}, bf16[256,256]{1,0:T(8,128)(2,1)S(1)}, u32[]{:S(2)}, u32[]{:S(2)}) %collective-permute-start.11) | collective-permute-done | bytes 131104 | tf_op jit(solution)/shard_map/ppermute | solution.py:37
  65.8 1.8 collective-permute-start.14
  67.6 4.0 %collective-permute-start.15 = (bf16[1024,128]{1,0:T(8,128)(2,1)S(1)}, bf16[1024,128]{1,0:T(8,128)(2,1)S(1)}, u32[]{:S(2)}, u32[]{:S(2)}) collective-permute-start(bf16[1024,128]{1,0:T(8,128)(2,1)S(1)} %get-tuple-element.37.rest_0_), channel_id=1, source_target_pairs={{8,16},{12,20},{16,8},{20,12},{9,17},{13,21},{17,9},{21,13},{10,18... | collective-permute-start | bytes 786440 | tf_op jit(solution)/shard_map/ppermute | solution.py:55
  72.4 6.0 %collective-permute-done.13.rest_4_ = bf16[1024,128]{1,0:T(8,128)(2,1)S(1)} collective-permute-done((bf16[1024,128]{1,0:T(8,128)(2,1)S(1)}, bf16[1024,128]{1,0:T(8,128)(2,1)S(1)}, u32[]{:S(2)}, u32[]{:S(2)}) %collective-permute-start.13) | collective-permute-done | bytes 262176 | tf_op jit(solution)/shard_map/ppermute | solution.py:37
  79.4 3.0 %collective-permute-start.16 = (bf16[1024,128]{1,0:T(8,128)(2,1)S(1)}, bf16[1024,128]{1,0:T(8,128)(2,1)S(1)}, u32[]{:S(2)}, u32[]{:S(2)}) collective-permute-start(bf16[1024,128]{1,0:T(8,128)(2,1)S(1)} %collective-permute-done.14.rest_1_), channel_id=1, source_target_pairs={{0,4},{4,0},{8,12},{12,8},{16,20},{20,16},{24,28},{28,24},{1,5},{5... | collective-permute-start | bytes 786440 | tf_op jit(solution)/shard_map/ppermute | solution.py:37
  82.4 4.4 %collective-permute-start.17 = (bf16[1024,128]{1,0:T(8,128)(2,1)S(1)}, bf16[1024,128]{1,0:T(8,128)(2,1)S(1)}, u32[]{:S(2)}, u32[]{:S(2)}) collective-permute-start(bf16[1024,128]{1,0:T(8,128)(2,1)S(1)} %collective-permute-done.14.rest_1_), channel_id=1, source_target_pairs={{8,16},{12,20},{16,8},{20,12},{9,17},{13,21},{17,9},{21,13},{10,18... | collective-permute-start | bytes 786440 | tf_op jit(solution)/shard_map/ppermute | solution.py:55
  86.8 1.3 collective-permute-start.18
  88.1 1.5 fusion.11
  89.6 1.5 fusion.14
  91.5 2.6 %fusion.23 = (bf16[1,256,2048]{2,1,0:T(8,128)(2,1)S(1)}, bf16[1,256,2048]{2,1,0:T(8,128)(2,1)S(1)}, bf16[1,256,2048]{2,1,0:T(8,128)(2,1)S(1)}, bf16[1,256,2048]{2,1,0:T(8,128)(2,1)S(1)}) fusion(bf16[256,2048]{1,0:T(8,128)(2,1)S(1)} %copy-done.1, f32[2048]{0:T(1024)S(1)} %copy-done.18, f32[256]{0:T(256)S(1)} %add_rsqrt_fusion.3, f32[256]{0:T(256)S(1)} %add_rsqrt_fusion.2, ...), kind=kLoop, calls=%fused_computation.32 | loop fusion | flops 8388608 | bytes 8400896 | tf_op jit(solution)/shard_map/stack | solution.py:414
  94.1 2.3 pad_maximum_fusion.rows
  96.4 6.0 %shard_map.158.own = bf16[2,1024,128]{2,1,0:T(8,128)(2,1)} custom-call(s32[12]{0:T(128)} %pad_add_fusion.2.meta, bf16[4,256,2048]{2,1,0:T(8,128)(2,1)} %pad_maximum_fusion.rows, f32[1024,128]{1,0:T(8,128)} %get-tuple-element.71.cosine, f32[1024,128]{1,0:T(8,128)} %get-tuple-element.87.sine, bf16[256,256]{1,0:T(8,128)(2,1)} %pad_maximum_fusion.6.mixer, ...), custom_call_target="tpu_custom_call" | custom-call | flops 1073741824 | bytes 5767168 | tf_op jit(solution)/shard_map/pallas_call | solution.py:192
  102.5 2.1 collective-permute-start.19
  104.5 1.5 collective-permute-start.20
  106.0 14.2 %collective-permute-done.19.rest_6_ = bf16[1024,128]{1,0:T(8,128)(2,1)S(1)} collective-permute-done((bf16[1024,128]{1,0:T(8,128)(2,1)S(1)}, bf16[1024,128]{1,0:T(8,128)(2,1)S(1)}, u32[]{:S(2)}, u32[]{:S(2)}) %collective-permute-start.19) | collective-permute-done | bytes 262176 | tf_op jit(solution)/shard_map/ppermute | solution.py:37
  122.3 1.3 pad_add_fusion.1.meta
  123.6 3.9 %collective-permute-done.21.rest_7_ = bf16[1024,128]{1,0:T(8,128)(2,1)} collective-permute-done((bf16[1024,128]{1,0:T(8,128)(2,1)S(1)}, bf16[1024,128]{1,0:T(8,128)(2,1)}, u32[]{:S(2)}, u32[]{:S(2)}) %collective-permute-start.21) | collective-permute-done | bytes 262176 | tf_op jit(solution)/shard_map/ppermute | solution.py:37
  127.5 12.4 %shard_map.159.rest_0_ = bf16[8,1024,128]{2,1,0:T(8,128)(2,1)} custom-call(s32[12]{0:T(128)} %pad_add_fusion.2.meta, bf16[4,256,2048]{2,1,0:T(8,128)(2,1)} %pad_maximum_fusion.rows, f32[1024,128]{1,0:T(8,128)} %get-tuple-element.70.cosine, f32[1024,128]{1,0:T(8,128)} %get-tuple-element.88.sine, bf16[256,256]{1,0:T(8,128)(2,1)} %pad_maximum_fusion.6.mixer, ...), custom_call_target="tpu_custom_call" | custom-call | flops 4294967296 | bytes 10485760 | tf_op jit(solution)/shard_map/pallas_call | solution.py:192
  139.9 17.0 %shard_map.160 = bf16[1024,1024]{1,0:T(8,128)(2,1)} custom-call(s32[6]{0:T(128)} %pad_add_fusion.1.meta, bf16[2,1024,128]{2,1,0:T(8,128)(2,1)} %shard_map.158.own, bf16[2,1024,128]{2,1,0:T(8,128)(2,1)} %collective-permute-done.12.far, bf16[8,1024,128]{2,1,0:T(8,128)(2,1)} %shard_map.159.rest_0_), custom_call_target="tpu_custom_call" | custom-call | tf_op jit(solution)/shard_map/pallas_call | solution.py:286
  156.9 6.9 %shard_map.161 = (bf16[2,256,1024]{2,1,0:T(8,128)(2,1)}, bf16[2,256,1024]{2,1,0:T(8,128)(2,1)}) custom-call(s32[8]{0:T(128)} %pad_add_fusion.meta, bf16[4,256,1024]{2,1,0:T(8,128)(2,1)} %bitcast.68, bf16[1024,128]{1,0:T(8,128)(2,1)} %copy-done.4, bf16[1024,128]{1,0:T(8,128)(2,1)} %copy-done.12, bf16[1024,128]{1,0:T(8,128)(2,1)} %copy-done.5, ...), custom_call_target="tpu_custom_call" | custom-call | tf_op jit(solution)/shard_map/pallas_call | solution.py:329
  164.4 7.2 %shard_map.162 = (bf16[2,256,1024]{2,1,0:T(8,128)(2,1)}, bf16[2,256,1024]{2,1,0:T(8,128)(2,1)}) custom-call(s32[8]{0:T(128)} %iota.47.meta, bf16[4,256,1024]{2,1,0:T(8,128)(2,1)} %bitcast.69, bf16[8,1024,128]{2,1,0:T(8,128)(2,1)} %bitcast.71), custom_call_target="tpu_custom_call" | custom-call | tf_op jit(solution)/shard_map/pallas_call | solution.py:329
  172.5 3.0 %add_convert_fusion.2 = (bf16[1,256,1024]{2,1,0:T(8,128)(2,1)}, bf16[256,1024]{1,0:T(8,128)(2,1)}) fusion(bf16[2,256,1024]{2,1,0:T(8,128)(2,1)} %collective-permute-done.22, bf16[2,256,1024]{2,1,0:T(8,128)(2,1)} %get-tuple-element.48), kind=kLoop, calls=%fused_computation.39 | loop fusion | flops 2097152 | bytes 3145728 | tf_op jit(solution)/shard_map/convert_element_type | solution.py:126
  176.5 2.6 %add_convert_fusion = (bf16[1,256,1024]{2,1,0:T(8,128)(2,1)}, bf16[256,1024]{1,0:T(8,128)(2,1)}) fusion(bf16[2,256,1024]{2,1,0:T(8,128)(2,1)} %collective-permute-done.24, bf16[2,256,1024]{2,1,0:T(8,128)(2,1)S(1)} %copy-done.3), kind=kLoop, calls=%fused_computation.37 | loop fusion | flops 2097152 | bytes 3145728 | tf_op jit(solution)/shard_map/convert_element_type | solution.py:126
  180.1 1.2 reduce-window.6
  181.8 8.7 %collective-permute-done.23 = bf16[1,256,1024]{2,1,0:T(8,128)(2,1)} collective-permute-done((bf16[1,256,1024]{2,1,0:T(8,128)(2,1)}, bf16[1,256,1024]{2,1,0:T(8,128)(2,1)}, u32[]{:S(2)}, u32[]{:S(2)}) %collective-permute-start.23) | collective-permute-done | bytes 524320 | tf_op jit(solution)/shard_map/ppermute | solution.py:37
  190.6 10.3 %collective-permute-done.25 = bf16[1,256,1024]{2,1,0:T(8,128)(2,1)} collective-permute-done((bf16[1,256,1024]{2,1,0:T(8,128)(2,1)}, bf16[1,256,1024]{2,1,0:T(8,128)(2,1)}, u32[]{:S(2)}, u32[]{:S(2)}) %collective-permute-start.25) | collective-permute-done | bytes 524320 | tf_op jit(solution)/shard_map/ppermute | solution.py:37
  200.8 4.3 %shard_map.163 = (bf16[256,2048]{1,0:T(8,128)(2,1)}, bf16[256,2048]{1,0:T(8,128)(2,1)}) custom-call(bf16[256,2048]{1,0:T(8,128)(2,1)} %states.1, f32[1,2048]{1,0:T(1,128)} %bitcast.81, bf16[256,1024]{1,0:T(8,128)(2,1)} %get-tuple-element.57.rest_0_, bf16[256,1024]{1,0:T(8,128)(2,1)} %bitcast.12.rest_1_, bf16[256,1024]{1,0:T(8,128)(2,1)} %get-tuple-element.55.rest_2_, ...), custom_call_target="tpu_custom_call" | custom-call | tf_op jit(solution)/shard_map/pallas_call | solution.py:367
  205.1 1.8 convolution_convert_fusion
  209.7 5.9 %collective-permute-done.28 = bf16[64,2048]{1,0:T(8,128)(2,1)S(1)} collective-permute-done((bf16[64,2048]{1,0:T(8,128)(2,1)S(1)}, bf16[64,2048]{1,0:T(8,128)(2,1)S(1)}, u32[]{:S(2)}, u32[]{:S(2)}) %collective-permute-start.28) | collective-permute-done | bytes 262176 | tf_op jit(solution)/shard_map/ppermute | solution.py:37
  215.6 4.9 %collective-permute-done.26 = bf16[64,2048]{1,0:T(8,128)(2,1)S(1)} collective-permute-done((bf16[64,2048]{1,0:T(8,128)(2,1)S(1)}, bf16[64,2048]{1,0:T(8,128)(2,1)S(1)}, u32[]{:S(2)}, u32[]{:S(2)}) %collective-permute-start.26) | collective-permute-done | bytes 262176 | tf_op jit(solution)/shard_map/ppermute | solution.py:37
  220.7 4.6 %fusion = f32[256,1536]{1,0:T(8,128)S(1)} fusion(bf16[256,2048]{1,0:T(8,128)(2,1)S(1)} %bitcast.72, bf16[1,2048,1536]{2,1,0:T(8,128)(2,1)} %param.25), kind=kOutput, calls=%fused_computation | convolution fusion | flops 1610612736 | bytes 8912896 | tf_op jit(solution)/shard_map/dot_general | solution.py:487
  229.8 4.9 %collective-permute-done.31 = bf16[64,2048]{1,0:T(8,128)(2,1)S(1)} collective-permute-done((bf16[64,2048]{1,0:T(8,128)(2,1)S(1)}, bf16[64,2048]{1,0:T(8,128)(2,1)S(1)}, u32[]{:S(2)}, u32[]{:S(2)}) %collective-permute-start.31) | collective-permute-done | bytes 262176 | tf_op jit(solution)/shard_map/ppermute | solution.py:37
  234.8 6.0 %collective-permute-done.29 = bf16[64,2048]{1,0:T(8,128)(2,1)S(1)} collective-permute-done((bf16[64,2048]{1,0:T(8,128)(2,1)S(1)}, bf16[64,2048]{1,0:T(8,128)(2,1)S(1)}, u32[]{:S(2)}, u32[]{:S(2)}) %collective-permute-start.29) | collective-permute-done | bytes 262176 | tf_op jit(solution)/shard_map/ppermute | solution.py:37
  240.9 1.5 fusion.4
  (156 shorter events, 26.0 us)
Async XLA Ops:
  7.2 218.1 %copy-start = (bf16[1,768,2048]{2,1,0:T(8,128)(2,1)S(1)}, bf16[1,768,2048]{2,1,0:T(8,128)(2,1)}, u32[]{:S(2)}) copy-start(bf16[1,768,2048]{2,1,0:T(8,128)(2,1)} %param.26) | copy-start | bytes 9437188
  7.2 120.3 %all-gather.5.cloned.1.call-start = ((), (), s32[]{:S(2)}) async-start(), calls=%async_computation | async-start | bytes 4718592 | tf_op jit(solution)/shard_map/all_gather | solution.py:407
  9.5 154.3 %all-gather.7.cloned.1.call-start = ((), (), s32[]{:S(2)}) async-start(), calls=%async_computation.1 | async-start | bytes 2359296 | tf_op jit(solution)/shard_map/all_gather | solution.py:443
  10.6 61.0 %collective-permute-start = (bf16[256,2048]{1,0:T(8,128)(2,1)}, bf16[256,2048]{1,0:T(8,128)(2,1)}, u32[]{:S(2)}, u32[]{:S(2)}) collective-permute-start(bf16[256,2048]{1,0:T(8,128)(2,1)} %states.1), channel_id=1, source_target_pairs={{0,2},{1,3},{2,0},{3,1},{4,6},{5,7},{6,4},{7,5},{8,10},{9,11},{10,... | collective-permute-start | bytes 3145736 | tf_op jit(solution)/shard_map/ppermute | solution.py:37
  12.2 77.4 %collective-permute-start.1 = (bf16[256,2048]{1,0:T(8,128)(2,1)}, bf16[256,2048]{1,0:T(8,128)(2,1)}, u32[]{:S(2)}, u32[]{:S(2)}) collective-permute-start(bf16[256,2048]{1,0:T(8,128)(2,1)} %states.1), channel_id=1, source_target_pairs={{0,1},{1,0},{2,3},{3,2},{4,5},{5,4},{6,7},{7,6},{8,9},{9,8},{10,11... | collective-permute-start | bytes 3145736 | tf_op jit(solution)/shard_map/ppermute | solution.py:37
  12.2 17.6 %collective-permute-start.3 = (bf16[256,256]{1,0:T(8,128)(2,1)S(1)}, bf16[256,256]{1,0:T(8,128)(2,1)}, u32[]{:S(2)}, u32[]{:S(2)}) collective-permute-start(bf16[256,256]{1,0:T(8,128)(2,1)S(1)} %pad_maximum_fusion.5.rest_0_), channel_id=1, source_target_pairs={{0,4},{4,0},{8,12},{12,8},{16,20},{20,16},{24,28},{28,24},{1,5},{5... | collective-permute-start | bytes 393224 | tf_op jit(solution)/shard_map/ppermute | solution.py:37
  13.7 16.1 %collective-permute-start.4 = (bf16[256,256]{1,0:T(8,128)(2,1)S(1)}, bf16[256,256]{1,0:T(8,128)(2,1)}, u32[]{:S(2)}, u32[]{:S(2)}) collective-permute-start(bf16[256,256]{1,0:T(8,128)(2,1)S(1)} %pad_maximum_fusion.5.rest_0_), channel_id=1, source_target_pairs={{0,8},{4,12},{8,0},{12,4},{16,24},{20,28},{24,16},{28,20},{1,9},{5... | collective-permute-start | bytes 393224 | tf_op jit(solution)/shard_map/ppermute | solution.py:55
  14.1 15.7 %collective-permute-start.5 = (bf16[256,256]{1,0:T(8,128)(2,1)S(1)}, bf16[256,256]{1,0:T(8,128)(2,1)}, u32[]{:S(2)}, u32[]{:S(2)}) collective-permute-start(bf16[256,256]{1,0:T(8,128)(2,1)S(1)} %pad_maximum_fusion.5.rest_0_), channel_id=1, source_target_pairs={{8,16},{12,20},{16,8},{20,12},{9,17},{13,21},{17,9},{21,13},{10,18... | collective-permute-start | bytes 393224 | tf_op jit(solution)/shard_map/ppermute | solution.py:55
  20.9 46.7 %copy-start.4 = (bf16[1024,128]{1,0:T(8,128)(2,1)}, bf16[1024,128]{1,0:T(8,128)(2,1)S(1)}, u32[]{:S(2)}) copy-start(bf16[1024,128]{1,0:T(8,128)(2,1)S(1)} %get-tuple-element.37.rest_0_) | copy-start | bytes 786436
  29.8 5.3 %collective-permute-start.6 = (bf16[256,256]{1,0:T(8,128)(2,1)}, bf16[256,256]{1,0:T(8,128)(2,1)S(1)}, u32[]{:S(2)}, u32[]{:S(2)}) collective-permute-start(bf16[256,256]{1,0:T(8,128)(2,1)} %collective-permute-done.4.rest_1_), channel_id=1, source_target_pairs={{0,4},{4,0},{8,12},{12,8},{16,20},{20,16},{24,28},{28,24},{1,5},{5... | collective-permute-start | bytes 393224 | tf_op jit(solution)/shard_map/ppermute | solution.py:37
  30.4 11.9 %collective-permute-start.7 = (bf16[256,256]{1,0:T(8,128)(2,1)}, bf16[256,256]{1,0:T(8,128)(2,1)}, u32[]{:S(2)}, u32[]{:S(2)}) collective-permute-start(bf16[256,256]{1,0:T(8,128)(2,1)} %collective-permute-done.4.rest_1_), channel_id=1, source_target_pairs={{8,16},{12,20},{16,8},{20,12},{9,17},{13,21},{17,9},{21,13},{10,18... | collective-permute-start | bytes 393224 | tf_op jit(solution)/shard_map/ppermute | solution.py:55
  32.6 9.7 %collective-permute-start.8 = (bf16[256,256]{1,0:T(8,128)(2,1)}, bf16[256,256]{1,0:T(8,128)(2,1)}, u32[]{:S(2)}, u32[]{:S(2)}) collective-permute-start(bf16[256,256]{1,0:T(8,128)(2,1)} %collective-permute-done.5), channel_id=1, source_target_pairs={{8,0},{12,4},{16,24},{20,28},{9,1},{13,5},{17,25},{21,29},{10,2},{... | collective-permute-start | bytes 393224 | tf_op jit(solution)/shard_map/ppermute | solution.py:55
  35.1 36.7 %copy-start.20 = (s32[4]{0:T(128)S(1)}, s32[4]{0:T(128)}, u32[]{:S(2)}) copy-start(s32[4]{0:T(128)} %broadcast_xor_fusion) | copy-start | bytes 52
  35.1 36.7 %copy-start.23 = (s32[4]{0:T(128)S(1)}, s32[4]{0:T(128)}, u32[]{:S(2)}) copy-start(s32[4]{0:T(128)} %get-tuple-element.85) | copy-start | bytes 52
  35.1 36.7 %copy-start.24 = (s32[4]{0:T(128)S(1)}, s32[4]{0:T(128)}, u32[]{:S(2)}) copy-start(s32[4]{0:T(128)} %get-tuple-element.86) | copy-start | bytes 52
  35.2 56.0 %copy-start.15 = (bf16[256,256]{1,0:T(8,128)(2,1)}, bf16[256,256]{1,0:T(8,128)(2,1)S(1)}, u32[]{:S(2)}) copy-start(bf16[256,256]{1,0:T(8,128)(2,1)S(1)} %collective-permute-done.6.rest_5_) | copy-start | bytes 393220
  43.2 48.2 %copy-start.8 = (bf16[256,256]{1,0:T(8,128)(2,1)}, bf16[256,256]{1,0:T(8,128)(2,1)S(1)}, u32[]{:S(2)}) copy-start(bf16[256,256]{1,0:T(8,128)(2,1)S(1)} %broadcast_select_fusion.3.rest_2_) | copy-start | bytes 393220
  43.2 5.3 %collective-permute-start.9 = (bf16[256,256]{1,0:T(8,128)(2,1)S(1)}, bf16[256,256]{1,0:T(8,128)(2,1)S(1)}, u32[]{:S(2)}, u32[]{:S(2)}) collective-permute-start(bf16[256,256]{1,0:T(8,128)(2,1)S(1)} %broadcast_select_fusion.3.rest_2_), channel_id=1, source_target_pairs={{0,4},{4,0},{8,12},{12,8},{16,20},{20,16},{24,28},{28,24},{1,5},{5... | collective-permute-start | bytes 393224 | tf_op jit(solution)/shard_map/ppermute | solution.py:37
  44.8 10.9 %collective-permute-start.10 = (bf16[256,256]{1,0:T(8,128)(2,1)}, bf16[256,256]{1,0:T(8,128)(2,1)S(1)}, u32[]{:S(2)}, u32[]{:S(2)}) collective-permute-start(bf16[256,256]{1,0:T(8,128)(2,1)} %collective-permute-done.7), channel_id=1, source_target_pairs={{8,0},{12,4},{16,24},{20,28},{9,1},{13,5},{17,25},{21,29},{10,2},{... | collective-permute-start | bytes 393224 | tf_op jit(solution)/shard_map/ppermute | solution.py:55
  48.4 43.1 %copy-start.1 = (bf16[256,2048]{1,0:T(8,128)(2,1)S(1)}, bf16[256,2048]{1,0:T(8,128)(2,1)}, u32[]{:S(2)}) copy-start(bf16[256,2048]{1,0:T(8,128)(2,1)} %states.1) | copy-start | bytes 3145732
  48.4 43.1 %copy-start.18 = (f32[2048]{0:T(1024)S(1)}, f32[2048]{0:T(1024)}, u32[]{:S(2)}) copy-start(f32[2048]{0:T(1024)} %param.16) | copy-start | bytes 24580
  48.6 45.5 %copy-start.16 = (bf16[256,256]{1,0:T(8,128)(2,1)}, bf16[256,256]{1,0:T(8,128)(2,1)S(1)}, u32[]{:S(2)}) copy-start(bf16[256,256]{1,0:T(8,128)(2,1)S(1)} %collective-permute-done.9.rest_6_) | copy-start | bytes 393220
  56.6 37.5 %copy-start.9 = (bf16[256,256]{1,0:T(8,128)(2,1)}, bf16[256,256]{1,0:T(8,128)(2,1)S(1)}, u32[]{:S(2)}) copy-start(bf16[256,256]{1,0:T(8,128)(2,1)S(1)} %broadcast_select_fusion.2.rest_3_) | copy-start | bytes 393220
  56.6 9.2 %collective-permute-start.11 = (bf16[256,256]{1,0:T(8,128)(2,1)S(1)}, bf16[256,256]{1,0:T(8,128)(2,1)S(1)}, u32[]{:S(2)}, u32[]{:S(2)}) collective-permute-start(bf16[256,256]{1,0:T(8,128)(2,1)S(1)} %broadcast_select_fusion.2.rest_3_), channel_id=1, source_target_pairs={{0,4},{4,0},{8,12},{12,8},{16,20},{20,16},{24,28},{28,24},{1,5},{5... | collective-permute-start | bytes 393224 | tf_op jit(solution)/shard_map/ppermute | solution.py:37
  65.8 28.3 %copy-start.17 = (bf16[256,256]{1,0:T(8,128)(2,1)}, bf16[256,256]{1,0:T(8,128)(2,1)S(1)}, u32[]{:S(2)}) copy-start(bf16[256,256]{1,0:T(8,128)(2,1)S(1)} %collective-permute-done.11.rest_7_) | copy-start | bytes 393220
  65.8 12.6 %collective-permute-start.13 = (bf16[1024,128]{1,0:T(8,128)(2,1)S(1)}, bf16[1024,128]{1,0:T(8,128)(2,1)S(1)}, u32[]{:S(2)}, u32[]{:S(2)}) collective-permute-start(bf16[1024,128]{1,0:T(8,128)(2,1)S(1)} %get-tuple-element.37.rest_0_), channel_id=1, source_target_pairs={{0,4},{4,0},{8,12},{12,8},{16,20},{20,16},{24,28},{28,24},{1,5},{5... | collective-permute-start | bytes 786440 | tf_op jit(solution)/shard_map/ppermute | solution.py:37
  65.8 12.6 %collective-permute-start.14 = (bf16[1024,128]{1,0:T(8,128)(2,1)S(1)}, bf16[1024,128]{1,0:T(8,128)(2,1)S(1)}, u32[]{:S(2)}, u32[]{:S(2)}) collective-permute-start(bf16[1024,128]{1,0:T(8,128)(2,1)S(1)} %get-tuple-element.37.rest_0_), channel_id=1, source_target_pairs={{0,8},{4,12},{8,0},{12,4},{16,24},{20,28},{24,16},{28,20},{1,9},{5... | collective-permute-start | bytes 786440 | tf_op jit(solution)/shard_map/ppermute | solution.py:55
  67.6 11.8 %collective-permute-start.15 = (bf16[1024,128]{1,0:T(8,128)(2,1)S(1)}, bf16[1024,128]{1,0:T(8,128)(2,1)S(1)}, u32[]{:S(2)}, u32[]{:S(2)}) collective-permute-start(bf16[1024,128]{1,0:T(8,128)(2,1)S(1)} %get-tuple-element.37.rest_0_), channel_id=1, source_target_pairs={{8,16},{12,20},{16,8},{20,12},{9,17},{13,21},{17,9},{21,13},{10,18... | collective-permute-start | bytes 786440 | tf_op jit(solution)/shard_map/ppermute | solution.py:55
  71.6 19.5 %collective-permute-start.2 = (bf16[256,2048]{1,0:T(8,128)(2,1)}, bf16[256,2048]{1,0:T(8,128)(2,1)S(1)}, u32[]{:S(2)}, u32[]{:S(2)}) collective-permute-start(bf16[256,2048]{1,0:T(8,128)(2,1)} %collective-permute-done), channel_id=1, source_target_pairs={{0,1},{1,0},{2,3},{3,2},{4,5},{5,4},{6,7},{7,6},{8,9},{9,8},{10,11... | collective-permute-start | bytes 3145736 | tf_op jit(solution)/shard_map/ppermute | solution.py:37
  79.4 23.0 %collective-permute-start.16 = (bf16[1024,128]{1,0:T(8,128)(2,1)S(1)}, bf16[1024,128]{1,0:T(8,128)(2,1)S(1)}, u32[]{:S(2)}, u32[]{:S(2)}) collective-permute-start(bf16[1024,128]{1,0:T(8,128)(2,1)S(1)} %collective-permute-done.14.rest_1_), channel_id=1, source_target_pairs={{0,4},{4,0},{8,12},{12,8},{16,20},{20,16},{24,28},{28,24},{1,5},{5... | collective-permute-start | bytes 786440 | tf_op jit(solution)/shard_map/ppermute | solution.py:37
  82.4 20.0 %collective-permute-start.17 = (bf16[1024,128]{1,0:T(8,128)(2,1)S(1)}, bf16[1024,128]{1,0:T(8,128)(2,1)S(1)}, u32[]{:S(2)}, u32[]{:S(2)}) collective-permute-start(bf16[1024,128]{1,0:T(8,128)(2,1)S(1)} %collective-permute-done.14.rest_1_), channel_id=1, source_target_pairs={{8,16},{12,20},{16,8},{20,12},{9,17},{13,21},{17,9},{21,13},{10,18... | collective-permute-start | bytes 786440 | tf_op jit(solution)/shard_map/ppermute | solution.py:55
  86.8 15.6 %collective-permute-start.18 = (bf16[1024,128]{1,0:T(8,128)(2,1)S(1)}, bf16[1024,128]{1,0:T(8,128)(2,1)S(1)}, u32[]{:S(2)}, u32[]{:S(2)}) collective-permute-start(bf16[1024,128]{1,0:T(8,128)(2,1)S(1)} %collective-permute-done.15), channel_id=1, source_target_pairs={{8,0},{12,4},{16,24},{20,28},{9,1},{13,5},{17,25},{21,29},{10,2},{... | collective-permute-start | bytes 786440 | tf_op jit(solution)/shard_map/ppermute | solution.py:55
  96.4 25.2 %copy-start.26 = (s32[4]{0:T(128)S(1)}, s32[4]{0:T(128)}, u32[]{:S(2)}) copy-start(s32[4]{0:T(128)} %param.23) | copy-start | bytes 52
  102.4 17.8 %collective-permute-start.12 = (bf16[2,1024,128]{2,1,0:T(8,128)(2,1)}, bf16[2,1024,128]{2,1,0:T(8,128)(2,1)}, u32[]{:S(2)}, u32[]{:S(2)}) collective-permute-start(bf16[2,1024,128]{2,1,0:T(8,128)(2,1)} %shard_map.158.own), channel_id=1, source_target_pairs={{0,4},{4,0},{8,12},{12,8},{16,20},{20,16},{24,28},{28,24},{1,5},{5... | collective-permute-start | bytes 1572872 | tf_op jit(solution)/shard_map/ppermute | solution.py:37
  102.5 37.4 %copy-start.5 = (bf16[1024,128]{1,0:T(8,128)(2,1)}, bf16[1024,128]{1,0:T(8,128)(2,1)S(1)}, u32[]{:S(2)}) copy-start(bf16[1024,128]{1,0:T(8,128)(2,1)S(1)} %broadcast_select_fusion.1.rest_2_) | copy-start | bytes 786436
  102.5 17.7 %collective-permute-start.19 = (bf16[1024,128]{1,0:T(8,128)(2,1)S(1)}, bf16[1024,128]{1,0:T(8,128)(2,1)S(1)}, u32[]{:S(2)}, u32[]{:S(2)}) collective-permute-start(bf16[1024,128]{1,0:T(8,128)(2,1)S(1)} %broadcast_select_fusion.1.rest_2_), channel_id=1, source_target_pairs={{0,4},{4,0},{8,12},{12,8},{16,20},{20,16},{24,28},{28,24},{1,5},{5... | collective-permute-start | bytes 786440 | tf_op jit(solution)/shard_map/ppermute | solution.py:37
  104.5 15.7 %collective-permute-start.20 = (bf16[1024,128]{1,0:T(8,128)(2,1)S(1)}, bf16[1024,128]{1,0:T(8,128)(2,1)S(1)}, u32[]{:S(2)}, u32[]{:S(2)}) collective-permute-start(bf16[1024,128]{1,0:T(8,128)(2,1)S(1)} %collective-permute-done.17), channel_id=1, source_target_pairs={{8,0},{12,4},{16,24},{20,28},{9,1},{13,5},{17,25},{21,29},{10,2},{... | collective-permute-start | bytes 786440 | tf_op jit(solution)/shard_map/ppermute | solution.py:55
  121.0 6.5 %collective-permute-start.21 = (bf16[1024,128]{1,0:T(8,128)(2,1)S(1)}, bf16[1024,128]{1,0:T(8,128)(2,1)}, u32[]{:S(2)}, u32[]{:S(2)}) collective-permute-start(bf16[1024,128]{1,0:T(8,128)(2,1)S(1)} %broadcast_select_fusion.rest_3_), channel_id=1, source_target_pairs={{0,4},{4,0},{8,12},{12,8},{16,20},{20,16},{24,28},{28,24},{1,5},{5... | collective-permute-start | bytes 786440 | tf_op jit(solution)/shard_map/ppermute | solution.py:37
  163.8 8.7 %collective-permute-start.22 = (bf16[2,256,1024]{2,1,0:T(8,128)(2,1)}, bf16[2,256,1024]{2,1,0:T(8,128)(2,1)}, u32[]{:S(2)}, u32[]{:S(2)}) collective-permute-start(bf16[2,256,1024]{2,1,0:T(8,128)(2,1)} %get-tuple-element.49), channel_id=1, source_target_pairs={{0,1},{1,0},{2,3},{3,2},{4,5},{5,4},{6,7},{7,6},{8,9},{9,8},{10,11... | collective-permute-start | bytes 3145736 | tf_op jit(solution)/shard_map/ppermute | solution.py:37
  171.6 4.9 %collective-permute-start.24 = (bf16[2,256,1024]{2,1,0:T(8,128)(2,1)}, bf16[2,256,1024]{2,1,0:T(8,128)(2,1)}, u32[]{:S(2)}, u32[]{:S(2)}) collective-permute-start(bf16[2,256,1024]{2,1,0:T(8,128)(2,1)} %get-tuple-element.51), channel_id=1, source_target_pairs={{0,1},{1,0},{2,3},{3,2},{4,5},{5,4},{6,7},{7,6},{8,9},{9,8},{10,11... | collective-permute-start | bytes 3145736 | tf_op jit(solution)/shard_map/ppermute | solution.py:37
  175.4 15.1 %collective-permute-start.23 = (bf16[1,256,1024]{2,1,0:T(8,128)(2,1)}, bf16[1,256,1024]{2,1,0:T(8,128)(2,1)}, u32[]{:S(2)}, u32[]{:S(2)}) collective-permute-start(bf16[1,256,1024]{2,1,0:T(8,128)(2,1)} %get-tuple-element.56), channel_id=1, source_target_pairs={{0,2},{1,3},{2,0},{3,1},{4,6},{5,7},{6,4},{7,5},{8,10},{9,11},{10,... | collective-permute-start | bytes 1572872 | tf_op jit(solution)/shard_map/ppermute | solution.py:37
  179.1 21.8 %collective-permute-start.25 = (bf16[1,256,1024]{2,1,0:T(8,128)(2,1)}, bf16[1,256,1024]{2,1,0:T(8,128)(2,1)}, u32[]{:S(2)}, u32[]{:S(2)}) collective-permute-start(bf16[1,256,1024]{2,1,0:T(8,128)(2,1)} %get-tuple-element.54), channel_id=1, source_target_pairs={{0,2},{1,3},{2,0},{3,1},{4,6},{5,7},{6,4},{7,5},{8,10},{9,11},{10,... | collective-permute-start | bytes 1572872 | tf_op jit(solution)/shard_map/ppermute | solution.py:37
  207.0 8.6 %collective-permute-start.28 = (bf16[64,2048]{1,0:T(8,128)(2,1)S(1)}, bf16[64,2048]{1,0:T(8,128)(2,1)S(1)}, u32[]{:S(2)}, u32[]{:S(2)}) collective-permute-start(bf16[64,2048]{1,0:T(8,128)(2,1)S(1)} %get-tuple-element.63), channel_id=1, source_target_pairs={{0,3},{1,2},{2,1},{3,0},{4,7},{5,6},{6,5},{7,4},{8,11},{9,10},{10,... | collective-permute-start | bytes 786440 | tf_op jit(solution)/shard_map/ppermute | solution.py:37
  207.1 8.5 %collective-permute-start.27 = (bf16[64,2048]{1,0:T(8,128)(2,1)S(1)}, bf16[64,2048]{1,0:T(8,128)(2,1)S(1)}, u32[]{:S(2)}, u32[]{:S(2)}) collective-permute-start(bf16[64,2048]{1,0:T(8,128)(2,1)S(1)} %get-tuple-element.64), channel_id=1, source_target_pairs={{0,1},{1,0},{2,3},{3,2},{4,5},{5,4},{6,7},{7,6},{8,9},{9,8},{10,11... | collective-permute-start | bytes 786440 | tf_op jit(solution)/shard_map/ppermute | solution.py:37
  208.2 12.3 %collective-permute-start.26 = (bf16[64,2048]{1,0:T(8,128)(2,1)S(1)}, bf16[64,2048]{1,0:T(8,128)(2,1)S(1)}, u32[]{:S(2)}, u32[]{:S(2)}) collective-permute-start(bf16[64,2048]{1,0:T(8,128)(2,1)S(1)} %get-tuple-element.65), channel_id=1, source_target_pairs={{0,2},{1,3},{2,0},{3,1},{4,6},{5,7},{6,4},{7,5},{8,10},{9,11},{10,... | collective-permute-start | bytes 786440 | tf_op jit(solution)/shard_map/ppermute | solution.py:37
  226.4 8.3 %collective-permute-start.31 = (bf16[64,2048]{1,0:T(8,128)(2,1)S(1)}, bf16[64,2048]{1,0:T(8,128)(2,1)S(1)}, u32[]{:S(2)}, u32[]{:S(2)}) collective-permute-start(bf16[64,2048]{1,0:T(8,128)(2,1)S(1)} %get-tuple-element.59), channel_id=1, source_target_pairs={{0,3},{1,2},{2,1},{3,0},{4,7},{5,6},{6,5},{7,4},{8,11},{9,10},{10,... | collective-permute-start | bytes 786440 | tf_op jit(solution)/shard_map/ppermute | solution.py:37
  227.3 7.5 %collective-permute-start.30 = (bf16[64,2048]{1,0:T(8,128)(2,1)S(1)}, bf16[64,2048]{1,0:T(8,128)(2,1)S(1)}, u32[]{:S(2)}, u32[]{:S(2)}) collective-permute-start(bf16[64,2048]{1,0:T(8,128)(2,1)S(1)} %get-tuple-element.60), channel_id=1, source_target_pairs={{0,1},{1,0},{2,3},{3,2},{4,5},{5,4},{6,7},{7,6},{8,9},{9,8},{10,11... | collective-permute-start | bytes 786440 | tf_op jit(solution)/shard_map/ppermute | solution.py:37
  227.6 13.1 %collective-permute-start.29 = (bf16[64,2048]{1,0:T(8,128)(2,1)S(1)}, bf16[64,2048]{1,0:T(8,128)(2,1)S(1)}, u32[]{:S(2)}, u32[]{:S(2)}) collective-permute-start(bf16[64,2048]{1,0:T(8,128)(2,1)S(1)} %get-tuple-element.61), channel_id=1, source_target_pairs={{0,2},{1,3},{2,0},{3,1},{4,6},{5,7},{6,4},{7,5},{8,10},{9,11},{10,... | collective-permute-start | bytes 786440 | tf_op jit(solution)/shard_map/ppermute | solution.py:37
  (14 other events, 127.2 us)
Sparse Core Ops, SparseCore 0:
  10.1 86.8 all-gather.4
  99.2 51.9 all-gather.6

commit v3 on v2

v3 whole, which is shorter than its diff:
```python
import functools
import math

import jax
import jax.numpy as jnp
from jax import lax
from jax.experimental import pallas as pl
from jax.experimental.pallas import tpu as pltpu
from jax.sharding import PartitionSpec as P

QUERY_HEADS = 32
KEY_VALUE_HEADS = 4
HEAD_DIMENSION = 128

epsilon = 1e-06
rope_theta = 1000000.0
VMEM_LIMIT = 32 * 1024 * 1024
FREE = pl.CostEstimate(flops=0, bytes_accessed=0, transcendentals=0)


def norm_rows(values, gain_vector):
    widened = values.astype(jnp.float32)
    inverse_rms = lax.rsqrt(jnp.mean(widened * widened, axis=-1, keepdims=True) + epsilon)
    return widened * inverse_rms * gain_vector


def local_positions(parity, row_count):
    indices = jnp.arange(row_count)
    quarter = row_count // 2
    offset = jnp.where(parity == 0, jnp.where(indices < quarter, 0, 2 * quarter), quarter)
    return indices + offset


def from_xor(block, axis, mask):
    count = lax.axis_size(axis)
    return lax.ppermute(block, axis, [(i, i ^ mask) for i in range(count)])


def cross(block):
    return from_xor(block, "group", 1)


def after(block, *others):
    return lax.optimization_barrier((block, *others))[0]


LINE = ((0, 1, 2, 3), (1, 0, 2, 3), (2, 3, 1, 0), (3, 2, 1, 0))
PAIRS = ((0, 1), (1, 0), (2, 3), (3, 2))
MIDDLE = ((1, 2), (2, 1))
OUTWARD = ((1, 0), (2, 3))


def along(block, moves):
    return lax.ppermute(block, "group", [(2 * a + s, 2 * b + s) for a, b in moves for s in range(2)])


def line_rounds(block, shards, crossed):
    place = lax.axis_index("group") // 2
    edge = (place == 0) | (place == 3)
    shards[0] = block
    if crossed is None:
        shards[1], inner, shards[4] = yield along(block, PAIRS), along(block, MIDDLE), cross(block)
    else:
        shards[4] = crossed
        shards[1], inner = yield along(block, PAIRS), along(block, MIDDLE)
    shards[5], inner_far, outer = yield cross(shards[1]), along(shards[1], MIDDLE), along(inner, OUTWARD)
    shards[2] = jnp.where(edge, outer, inner)
    shards[6], outer = yield cross(shards[2]), along(inner_far, OUTWARD)
    shards[3] = jnp.where(edge, outer, inner_far)
    (shards[7],) = yield (cross(shards[3]),)
    yield ()


class Beside:
    def __init__(self, block, crossed=None):
        groups = lax.axis_size("group")
        self.found = [None] * groups if groups == 8 else list(lax.all_gather(block, "group"))
        self.chain = line_rounds(block, self.found, crossed) if groups == 8 else None
        self.brought = (block,) if self.chain is None else lax.optimization_barrier(next(self.chain))

    def round(self, *ready):
        if self.chain is not None:
            results = after(self.brought, *ready)
            self.brought = lax.optimization_barrier(self.chain.send(results))

    def token(self):
        return self.brought[0]

    def held(self, indices):
        if self.chain is not None and any(self.found[index] is None for index in indices):
            self.chain.send(self.brought)
            self.chain = None
        return [self.found[index] for index in indices]


def held_groups(place, side):
    groups = lax.axis_size("group")
    if groups != 8:
        return jnp.arange(groups)
    places = jnp.sum(jnp.where(jnp.arange(4)[:, None] == place, jnp.array(LINE, jnp.int32), 0), axis=0)
    return jnp.concatenate([2 * places + side, 2 * places + 1 - side])


def doubling_masks(count):
    masks, stride = [0], count // 2
    while stride:
        masks = masks + [mask ^ stride for mask in masks]
        stride //= 2
    return masks


def gather_tokens(rows):
    blocks = [rows]
    stride = lax.axis_size("expert") // 2
    while stride:
        blocks = blocks + [from_xor(block, "expert", stride) for block in blocks]
        stride //= 2
    return blocks


def scatter_sum(kept, sent):
    stride = 1
    while True:
        half = kept.shape[0] // 2
        arrived = from_xor(sent, "expert", stride)
        if not half:
            return (kept[0], arrived[0]), sent
        summed = [
            kept[part].astype(jnp.float32) + arrived[part].astype(jnp.float32)
            for part in (slice(None, half), slice(half, None))
        ]
        kept, sent = [part.astype(jnp.bfloat16) for part in summed]
        stride *= 2


def stack_shards(meta, refs, weights):
    depth = weights.shape[0] // len(refs)
    for index, ref in enumerate(refs):
        weights[pl.ds(pl.multiple_of(meta[2 + index] * depth, depth), depth), :] = ref[...]


def turn(values, cosines, sines, mixer):
    values = values.astype(jnp.bfloat16)
    wide = values.astype(jnp.float32)
    both = jnp.concatenate([values, (wide * wide).astype(jnp.bfloat16)], axis=1)
    mixed = jnp.dot(both, mixer, preferred_element_type=jnp.float32)
    dim = values.shape[1]
    inverse = lax.rsqrt(mixed[:, dim:] + epsilon)
    return ((wide * cosines + mixed[:, :dim] * sines) * inverse).astype(jnp.bfloat16)


def query_kernel(count, meta, *rest):
    rows, (cosine, sine, mixer, *rest) = rest[:count], rest[count:]
    *shards, query_out, weights = rest
    stack_shards(meta, shards, weights)
    tile, dim = rows[0].shape[0], HEAD_DIMENSION
    joined = jnp.concatenate([block[...] for block in rows], axis=0)
    projected = jnp.dot(joined, weights[...], preferred_element_type=jnp.float32)
    for block in range(count):
        spot = pl.ds(pl.multiple_of(meta[2 + len(shards) + block] * tile, tile), tile)
        here = slice(block * tile, (block + 1) * tile)
        for head in range(2):
            query_out[head, here, :] = turn(
                projected[here, head * dim : (head + 1) * dim], cosine[spot, :], sine[spot, :], mixer[...]
            )


def key_kernel(count, meta, *rest):
    rows, (cosine, sine, mixer, *rest) = rest[:count], rest[count:]
    *shards, pair_out, weights = rest
    stack_shards(meta, shards, weights)
    tile, dim = rows[0].shape[0], HEAD_DIMENSION
    joined = jnp.concatenate([block[...] for block in rows], axis=0)
    projected = jnp.dot(joined, weights[...], preferred_element_type=jnp.float32)
    for block in range(count):
        spot = pl.ds(pl.multiple_of(meta[2 + len(shards) + block] * tile, tile), tile)
        here = slice(block * tile, (block + 1) * tile)
        pair_out[0, spot, :] = turn(projected[here, :dim], cosine[spot, :], sine[spot, :], mixer[...])
        pair_out[1, spot, :] = projected[here, dim:].astype(jnp.bfloat16)


def project(kernel, first, steps, meta, blocks, shards, cosine, sine, mixer):
    count, (tile, width) = len(blocks), blocks[0].shape
    dim = HEAD_DIMENSION
    shard = pl.BlockSpec((shards[0].shape[0], 2 * dim), lambda n, meta: (0, first + n))
    table = pl.BlockSpec((count * tile, dim), lambda n, meta: (0, 0))
    return pl.pallas_call(
        functools.partial(kernel, count),
        grid_spec=pltpu.PrefetchScalarGridSpec(
            num_scalar_prefetch=1,
            grid=(steps,),
            in_specs=[pl.BlockSpec((tile, width), lambda n, meta: (0, 0))] * count
            + [
                table,
                table,
                pl.BlockSpec((2 * dim, 2 * dim), lambda n, meta: (0, 0)),
            ]
            + [shard] * len(shards),
            out_specs=pl.BlockSpec((2, count * tile, dim), lambda n, meta: (n, 0, 0)),
            scratch_shapes=[pltpu.VMEM((width, 2 * dim), jnp.bfloat16)],
        ),
        out_shape=jax.ShapeDtypeStruct((2 * steps, count * tile, dim), jnp.bfloat16),
        compiler_params=pltpu.CompilerParams(vmem_limit_bytes=VMEM_LIMIT),
        cost_estimate=pl.CostEstimate(
            flops=16 * steps * count * tile * width * dim, bytes_accessed=2 * count * tile * width, transcendentals=0
        ),
    )(meta, *blocks, cosine, sine, mixer, *shards)


def attend_kernel(tile, start, meta, own, far, *rest):
    *queries, out, keys, values, total = rest
    heads, dim = total.shape[0], HEAD_DIMENSION
    query = [part.at[head] for part in queries for head in range(part.shape[0])]
    row_count = own.shape[1]
    half = row_count // 2
    parity, length = meta[0], meta[1]
    step = pl.program_id(0)

    @pl.when(step == 0)
    def _():
        ones = jnp.ones((half, dim), jnp.bfloat16)
        for pair, whose in ((own, parity), (far, 1 - parity)):
            for part in range(2):
                base = jnp.where(whose == 0, 3 * half * part, half * (1 + part))
                base = pl.multiple_of(base, half)
                source = pl.ds(part * half, half)
                keys[pl.ds(base, half), :] = pair[0, source, :]
                valid = base + lax.broadcasted_iota(jnp.int32, (half, dim), 0) < length
                zero = jnp.zeros((half, dim), jnp.bfloat16)
                values[pl.ds(base, half), :dim] = jnp.where(valid, pair[1, source, :], zero)
                values[pl.ds(base, half), dim:] = jnp.where(valid, ones, zero)

    first = meta[2 + start + step] * tile
    first = first + jnp.where(parity == 0, jnp.where(first < half, 0, 2 * half), half)

    def weigh(head, start, width, masked):
        scores = lax.dot_general(
            query[head][...], keys[pl.ds(start, width), :], (((1,), (1,)), ((), ())),
            preferred_element_type=jnp.float32,
        )
        weights = jnp.exp2(scores)
        if masked:
            below = lax.broadcasted_iota(jnp.int32, weights.shape, 1) <= lax.broadcasted_iota(
                jnp.int32, weights.shape, 0
            )
            weights = jnp.where(below, weights, 0.0)
        return jnp.dot(
            weights.astype(jnp.bfloat16), values[pl.ds(start, width), :], preferred_element_type=jnp.float32
        )

    diagonal = pl.multiple_of(first, tile)
    for head in range(heads):
        total[head] = weigh(head, diagonal, tile, True)

    def wide(index, _):
        start = pl.multiple_of(index * half, half)
        for head in range(heads):
            total[head] += weigh(head, start, half, False)
        return 0

    lax.fori_loop(0, first // half, wide, 0)

    def narrow(index, _):
        start = pl.multiple_of(index * tile, tile)
        for head in range(heads):
            total[head] += weigh(head, start, tile, False)
        return 0

    lax.fori_loop(first // half * (half // tile), first // tile, narrow, 0)
    for head in range(heads):
        summed = total[head]
        out[:, head * dim : (head + 1) * dim] = (summed[:, :dim] / summed[:, dim:]).astype(jnp.bfloat16)


def attend(meta, queries, own, far, tile, part):
    _, row_count, dim = queries[0].shape
    heads = sum(query.shape[0] for query in queries)
    steps = row_count // tile // 2
    start = part * steps
    whole = pl.BlockSpec((2, row_count, dim), lambda i, meta: (0, 0, 0))
    return pl.pallas_call(
        functools.partial(attend_kernel, tile, start),
        grid_spec=pltpu.PrefetchScalarGridSpec(
            num_scalar_prefetch=1,
            grid=(steps,),
            in_specs=[whole] * 2
            + [pl.BlockSpec((query.shape[0], tile, dim), lambda i, meta: (0, start + i, 0)) for query in queries],
            out_specs=pl.BlockSpec((tile, heads * dim), lambda i, meta: (i, 0)),
            scratch_shapes=[
                pltpu.VMEM((2 * row_count, dim), jnp.bfloat16),
                pltpu.VMEM((2 * row_count, 2 * dim), jnp.bfloat16),
                pltpu.VMEM((heads, tile, 2 * dim), jnp.float32),
            ],
        ),
        out_shape=jax.ShapeDtypeStruct((steps * tile, heads * dim), jnp.bfloat16),
        compiler_params=pltpu.CompilerParams(vmem_limit_bytes=VMEM_LIMIT),
        cost_estimate=pl.CostEstimate(
            flops=8 * heads * row_count * row_count * dim, bytes_accessed=4 * row_count * dim, transcendentals=0
        ),
    )(meta, own, far, *queries)


def output_kernel(kept_rows, sent_rows, *rest):
    *shards, kept, sent = rest
    columns = shards[0].shape[1]
    for rows, out in ((sent_rows, sent), (kept_rows, kept)):
        for index, shard in enumerate(shards):
            product = jnp.dot(rows[...], shard[...], preferred_element_type=jnp.float32)
            here = slice(index * columns, (index + 1) * columns)
            out[:, :, here] = product.astype(jnp.bfloat16).reshape(*out.shape[:2], -1)


def output_part(kept_rows, sent_rows, tile, shards):
    rows, depth = kept_rows.shape
    width = len(shards) * shards[0].shape[1]

    def whole(shape):
        return pl.BlockSpec(shape, lambda n: (0,) * len(shape))

    out = (rows // tile, tile, width)
    return pl.pallas_call(
        output_kernel,
        grid=(1,),
        in_specs=[whole((rows, depth))] * 2 + [whole(shards[0].shape)] * len(shards),
        out_specs=[whole(out)] * 2,
        out_shape=[jax.ShapeDtypeStruct(out, jnp.bfloat16)] * 2,
        compiler_params=pltpu.CompilerParams(vmem_limit_bytes=VMEM_LIMIT),
        cost_estimate=pl.CostEstimate(flops=12 * rows * width * depth, bytes_accessed=8 * rows * width, transcendentals=0),
    )(kept_rows, sent_rows, *shards)


def finish_kernel(columns, meta, states, gain, *rest):
    *terms, hidden_out, normed_out = rest
    index = 0
    for kept, arrived in zip(terms[::2], terms[1::2]):
        for part in range(kept.shape[1] // columns):
            here = slice(part * columns, (part + 1) * columns)
            there = pl.ds(pl.multiple_of(meta[index] * columns, columns), columns)
            total = kept[:, here].astype(jnp.float32) + arrived[:, here].astype(jnp.float32)
            hidden_out[:, there] = (states[:, there].astype(jnp.float32) + total).astype(jnp.bfloat16)
            index += 1
    hidden = hidden_out[...].astype(jnp.float32)
    inverse = lax.rsqrt(jnp.mean(hidden * hidden, axis=-1, keepdims=True) + epsilon)
    normed_out[...] = (hidden * inverse * gain[...]).astype(jnp.bfloat16)


def finish(meta, states, gain, terms, columns):
    rows, width = states.shape
    tile = min(64, rows)

    def block(wide):
        return pl.BlockSpec((tile, wide), lambda i, meta: (i, 0))

    return pl.pallas_call(
        functools.partial(finish_kernel, columns),
        grid_spec=pltpu.PrefetchScalarGridSpec(
            num_scalar_prefetch=1,
            grid=(rows // tile,),
            in_specs=[block(width), pl.BlockSpec((1, width), lambda i, meta: (0, 0))]
            + [block(term.shape[1]) for term in terms],
            out_specs=[block(width)] * 2,
        ),
        out_shape=[jax.ShapeDtypeStruct((rows, width), jnp.bfloat16)] * 2,
        compiler_params=pltpu.CompilerParams(vmem_limit_bytes=VMEM_LIMIT),
        cost_estimate=FREE,
    )(meta, states, gain[None, :], *terms)


def per_device(
    hidden_in,
    norm_attention,
    norm_experts,
    query_master,
    trainer_key_value_weight,
    output_master,
    query_gain,
    key_gain,
    lengths,
    router,
    expert_gateup,
    expert_down,
    routes,
):
    experts_axis = lax.axis_size("expert")
    group_member = lax.axis_index("expert")
    group_index = lax.axis_index("group")
    heads = QUERY_HEADS // experts_axis
    dim = HEAD_DIMENSION
    rows_here, model_width = hidden_in.shape
    local_rows = rows_here * experts_axis

    groups = lax.axis_size("group")
    place, side = group_index // 2, group_index % 2
    common_head = group_member * heads // (QUERY_HEADS // KEY_VALUE_HEADS)
    pair = lax.dynamic_slice_in_dim(trainer_key_value_weight, common_head * dim, dim, 2)
    joined = jnp.concatenate([pair[0], pair[1], query_master], axis=1).astype(jnp.bfloat16)
    output_here = output_master.astype(jnp.bfloat16)
    joined_rounds = Beside(joined)
    normed = norm_rows(after(hidden_in, joined), norm_attention).astype(jnp.bfloat16)
    blocks = gather_tokens(normed)
    parity = after(side, joined_rounds.token())
    output_here = after(output_here, joined_rounds.token())
    output_crossed = cross(output_here)
    joined_rounds.round()
    query_gain, key_gain, lengths, routes = lax.optimization_barrier(
        (query_gain, key_gain, lengths, routes, joined_rounds.token())
    )[:4]
    joined_rounds.round()
    output_here, output_crossed = lax.optimization_barrier(
        (output_here, output_crossed, joined_rounds.token())
    )[:2]
    output_rounds = Beside(output_here, output_crossed)
    joined_rounds.round()
    shards = joined_rounds.held(range(groups))
    output_rounds.round(joined_rounds.token())

    masks = doubling_masks(experts_axis)
    block_order = jnp.bitwise_xor(group_member, jnp.array(masks, jnp.int32))
    meta = jnp.concatenate([jnp.stack([place, side]), held_groups(place, side), block_order]).astype(jnp.int32)

    inside = routes < experts_axis
    expert_window = jnp.sum(jnp.where(inside, routes, 0), axis=1)
    present = jnp.any(inside, axis=1)
    capacity = local_rows // (experts_axis * experts_axis)
    member_table = (present[:, None] & (expert_window[:, None] == block_order[None, :])).astype(jnp.int32)
    ranking = jnp.cumsum(member_table, axis=0) - 1
    slot_index = jnp.sum(member_table * (ranking + jnp.arange(experts_axis) * capacity), axis=1)
    select = (
        (jnp.arange(experts_axis * capacity)[:, None] == slot_index[None, :]) & present[None, :]
    ).astype(jnp.bfloat16)

    own_places = local_positions(parity, local_rows).astype(jnp.float32)
    exponents = jnp.arange(dim // 2).astype(jnp.float32)
    inverse = jnp.exp(exponents * (-2.0 * math.log(rope_theta) / dim))
    angles = own_places[:, None] * inverse[None, :]
    cosine_values, sine_values = jnp.cos(angles), jnp.sin(angles)
    cosine = jnp.concatenate([cosine_values, cosine_values], axis=1)
    sine = jnp.concatenate([-sine_values, sine_values], axis=1)

    def tables(gain):
        return cosine * gain, sine * jnp.roll(gain, dim // 2)

    lanes = jnp.arange(dim)
    swap = (lanes[:, None] == (lanes[None, :] + dim // 2) % dim).astype(jnp.float32)
    nothing = jnp.zeros((dim, dim), jnp.float32)
    mixer = jnp.block([[swap, nothing], [nothing, nothing + 1.0 / dim]]).astype(jnp.bfloat16)
    query_tables = tables(query_gain * (dim**-0.5 * math.log2(math.e)))
    key_tables = tables(key_gain)
    blocks[0] = after(blocks[0], select)
    own_pair = project(key_kernel, 0, 1, meta, blocks, shards, *key_tables, mixer)
    far_pair = cross(own_pair)
    rows_now = [after(blocks[0], own_pair)] + blocks[1:]
    queries = [project(query_kernel, 1, heads // 2, meta, rows_now, shards, *query_tables, mixer)]
    queries[0] = after(queries[0], output_rounds.token())
    output_rounds.round(queries[0], far_pair)

    valid_length = jnp.sum(jnp.where(jnp.arange(lengths.shape[0]) == group_index // 2, lengths, 0))
    attend_meta = jnp.concatenate([jnp.stack([parity, valid_length]), block_order]).astype(jnp.int32)
    sent_rows = attend(attend_meta, queries, own_pair, far_pair, rows_here, 1)
    queries[0] = after(queries[0], output_rounds.token())
    output_rounds.round(sent_rows)
    kept_rows = attend(attend_meta, queries, own_pair, far_pair, rows_here, 0)

    order = [0, 1, 2, 4, 5, 3, 6, 7] if groups == 8 else list(range(groups))
    cut = groups * 5 // 8
    output_shards = output_rounds.held(order)
    terms = []
    for part in (output_shards[:cut], output_shards[cut:]):
        both, _ = scatter_sum(*output_part(kept_rows, sent_rows, rows_here, part))
        terms += both
    finish_meta = jnp.stack([meta[2 + i] for i in order])
    hidden, normed_second = finish(finish_meta, hidden_in, norm_experts, terms, output_here.shape[1])

    logits = jnp.dot(normed_second, router, preferred_element_type=jnp.float32)
    route_table = routes[:, :, None] == jnp.arange(logits.shape[1])[None, None, :]
    picked = jnp.sum(jnp.where(route_table, logits[:, None, :], 0.0), axis=-1)
    raised = jnp.exp(picked)
    gate_values = raised / jnp.sum(raised, axis=1, keepdims=True)
    gate_window = jnp.sum(jnp.where(inside, gate_values, 0.0), axis=1)
    outgoing = (
        jnp.dot(select, normed_second, preferred_element_type=jnp.float32)
        .astype(jnp.bfloat16)
        .reshape(experts_axis, capacity, model_width)
    )

    def exchange(slots):
        return jnp.stack([slots[0]] + [from_xor(slots[j], "expert", masks[j]) for j in range(1, experts_axis)])

    gateup_here = expert_gateup[0]
    down_here = expert_down[0]
    hidden_units = down_here.shape[0]
    slot_items = exchange(outgoing)
    flattened = slot_items.reshape(-1, slot_items.shape[-1])
    gate_up = jnp.dot(flattened, gateup_here, preferred_element_type=jnp.float32)
    active = (jax.nn.silu(gate_up[:, :hidden_units]) * gate_up[:, hidden_units:]).astype(
        jnp.bfloat16
    )
    result = (
        jnp.dot(active, down_here, preferred_element_type=jnp.float32)
        .astype(jnp.bfloat16)
        .reshape(slot_items.shape)
    )
    returned = exchange(result)
    combined = jnp.dot(
        jnp.transpose(select), returned.reshape(-1, model_width), preferred_element_type=jnp.float32
    )
    expert_mix = (gate_window[:, None] * combined).astype(jnp.bfloat16)
    return (hidden, expert_mix)


def solution(mesh):
    return jax.shard_map(
        per_device,
        mesh=mesh,
        in_specs=(
            P(("group", "expert"), None),
            P(),
            P(),
            P("group", "expert"),
            P(None, "group", None),
            P("expert", "group"),
            P(),
            P(),
            P(),
            P(),
            P("expert", None, None),
            P("expert", None, None),
            P(("group", "expert"), None),
        ),
        out_specs=(P(("group", "expert"), None), P(("group", "expert"), None)),
        check_vma=False,
    )
```

time: 250 us -> 226 us (0.904)
  the two profiles are of different devices: /device:TPU:8 before, /device:TPU:0 now
where the time goes in v3:
time: 226 us; the launch traced here: 225 us
  waiting for transfers between devices  97 us (43%)
  Pallas kernels  43.9 us (19%)
  starting transfers between devices  31.5 us (14%)
  other arithmetic  25.9 us (11%)
  local copies, waits for them, and re-layouts  16.6 us (7%)
  matrix products  8.59 us (4%)
    ppermute x22, waiting for transfers between devices, from_xor(): return lax.ppermute(block, axis, [(i, i ^ mask) for i in range(count)])  79.2 us
    ppermute x22, starting transfers between devices, from_xor(): return lax.ppermute(block, axis, [(i, i ^ mask) for i in range(count)])  18.4 us
    ppermute x10, waiting for transfers between devices, along(): lax.ppermute(block, 'group', [(2 * a + s, 2 * b + s) for a, b in moves fo...  17.8 us
    pallas_call x2, Pallas kernels, project(): pl.pallas_call(functools.partial(kernel, count), grid_spec=pltpu.Prefetch...  15.9 us
    pallas_call x2, Pallas kernels, attend(): pl.pallas_call(functools.partial(attend_kernel, tile, start), grid_spec=p...  15.7 us
    ppermute x10, starting transfers between devices, along(): lax.ppermute(block, 'group', [(2 * a + s, 2 * b + s) for a, b in moves fo...  13.1 us
    unnamed x66, local copies, waits for them, and re-layouts  9.65 us
    pallas_call x2, Pallas kernels, output_part(): pl.pallas_call(output_kernel, grid=(1,), in_specs=[whole((rows, depth))]...  8.2 us
  transfers between devices with their start and end apart: 32, of which 16 were waited for; matrix products, arithmetic and copies ran while one was open for 12% of the time, Pallas kernels for 16%

profile of v3, /device:TPU:0, one launch (start us, length us, event | category | flops | bytes accessed | tf_op | source)
XLA Modules:
  0.0 224.7 jit_solution(6991490098936062121)
XLA Ops:
  0.7 2.2 %convert.21 = bf16[256,1024]{1,0:T(8,128)(2,1)} convert(f32[256,1024]{1,0:T(8,128)} %param.18) | non-fusion elementwise | flops 262144 | bytes 1572864 | tf_op jit(solution)/shard_map/convert.6
  4.0 1.9 pad_maximum_fusion.2.rest_7_
  5.9 3.0 %collective-permute-start = (bf16[256,1280]{1,0:T(8,128)(2,1)}, bf16[256,1280]{1,0:T(8,128)(2,1)}, u32[]{:S(2)}, u32[]{:S(2)}) collective-permute-start(bf16[256,1280]{1,0:T(8,128)(2,1)} %pad_maximum_fusion.2.rest_7_), channel_id=1, source_target_pairs={{0,8},{4,12},{8,0},{12,4},{16,24},{20,28},{24,16},{28,20},{1,9},{5... | collective-permute-start | bytes 1966088 | tf_op jit(solution)/shard_map/ppermute | solution.py:54
  8.9 1.5 collective-permute-start.1
  10.5 1.5 collective-permute-start.2
  12.3 1.3 fusion.10.rest_0_
  13.6 1.5 collective-permute-start.3
  15.1 2.1 convert_element_type.84.rest_0_
  17.5 6.5 %collective-permute-done.rest_8_ = bf16[256,1280]{1,0:T(8,128)(2,1)} collective-permute-done((bf16[256,1280]{1,0:T(8,128)(2,1)}, bf16[256,1280]{1,0:T(8,128)(2,1)}, u32[]{:S(2)}, u32[]{:S(2)}) %collective-permute-start) | collective-permute-done | bytes 655392 | tf_op jit(solution)/shard_map/ppermute | solution.py:54
  24.0 3.0 %collective-permute-done.2.rest_11_ = bf16[256,1280]{1,0:T(8,128)(2,1)} collective-permute-done((bf16[256,1280]{1,0:T(8,128)(2,1)}, bf16[256,1280]{1,0:T(8,128)(2,1)}, u32[]{:S(2)}, u32[]{:S(2)}) %collective-permute-start.2) | collective-permute-done | bytes 655392 | tf_op jit(solution)/shard_map/ppermute | solution.py:36
  27.0 1.5 collective-permute-start.6
  29.2 1.3 collective-permute-start.8
  30.6 11.8 %collective-permute-done.6.rest_12_ = bf16[256,1280]{1,0:T(8,128)(2,1)S(1)} collective-permute-done((bf16[256,1280]{1,0:T(8,128)(2,1)}, bf16[256,1280]{1,0:T(8,128)(2,1)S(1)}, u32[]{:S(2)}, u32[]{:S(2)}) %collective-permute-start.6) | collective-permute-done | bytes 655392 | tf_op jit(solution)/shard_map/ppermute | solution.py:36
  43.3 5.1 %collective-permute-done.8 = bf16[256,1280]{1,0:T(8,128)(2,1)S(1)} collective-permute-done((bf16[256,1280]{1,0:T(8,128)(2,1)}, bf16[256,1280]{1,0:T(8,128)(2,1)S(1)}, u32[]{:S(2)}, u32[]{:S(2)}) %collective-permute-start.8) | collective-permute-done | bytes 655392 | tf_op jit(solution)/shard_map/ppermute | solution.py:54
  50.0 1.3 collective-permute-start.10
  52.1 1.6 collective-permute-start.13
  53.6 12.6 %collective-permute-done.9.rest_13_ = bf16[256,1280]{1,0:T(8,128)(2,1)S(1)} collective-permute-done((bf16[256,1280]{1,0:T(8,128)(2,1)S(1)}, bf16[256,1280]{1,0:T(8,128)(2,1)S(1)}, u32[]{:S(2)}, u32[]{:S(2)}) %collective-permute-start.9) | collective-permute-done | bytes 655392 | tf_op jit(solution)/shard_map/ppermute | solution.py:36
  69.3 8.3 %collective-permute-done.13.rest_3_ = bf16[1024,256]{1,0:T(8,128)(2,1)} collective-permute-done((bf16[1024,256]{1,0:T(8,128)(2,1)}, bf16[1024,256]{1,0:T(8,128)(2,1)}, u32[]{:S(2)}, u32[]{:S(2)}) %collective-permute-start.13) | collective-permute-done | bytes 524320 | tf_op jit(solution)/shard_map/ppermute | solution.py:36
  79.5 1.9 fusion.21
  81.8 5.2 %collective-permute-done.14.rest_1_ = bf16[1024,256]{1,0:T(8,128)(2,1)S(1)} collective-permute-done((bf16[1024,256]{1,0:T(8,128)(2,1)}, bf16[1024,256]{1,0:T(8,128)(2,1)S(1)}, u32[]{:S(2)}, u32[]{:S(2)}) %collective-permute-start.14) | collective-permute-done | bytes 524320 | tf_op jit(solution)/shard_map/ppermute | solution.py:54
  88.1 4.5 %shard_map.158.own = bf16[2,1024,128]{2,1,0:T(8,128)(2,1)S(1)} custom-call(s32[14]{0:T(128)S(1)} %concatenate.42.meta, bf16[256,2048]{1,0:T(8,128)(2,1)} %fusion.10.rest_0_, bf16[256,2048]{1,0:T(8,128)(2,1)} %collective-permute-done.3.rest_1_, bf16[256,2048]{1,0:T(8,128)(2,1)} %collective-permute-done.4.rest_2_, ...), custom_call_target="tpu_custom_call" | custom-call | flops 4294967296 | bytes 4194304 | tf_op jit(solution)/shard_map/pallas_call | solution.py:187
  93.2 1.5 collective-permute-start.16
  95.4 1.3 collective-permute-start.18
  96.7 11.4 %shard_map.159.rest_0_ = bf16[8,1024,128]{2,1,0:T(8,128)(2,1)S(1)} custom-call(s32[14]{0:T(128)S(1)} %concatenate.42.meta, bf16[256,2048]{1,0:T(8,128)(2,1)} %fusion.10.rest_0_, bf16[256,2048]{1,0:T(8,128)(2,1)} %collective-permute-done.3.rest_1_, bf16[256,2048]{1,0:T(8,128)(2,1)} %collective-permute-done.4.rest_2_, ...), custom_call_target="tpu_custom_call" | custom-call | flops 17179869184 | bytes 4194304 | tf_op jit(solution)/shard_map/pallas_call | solution.py:187
  108.1 7.7 %collective-permute-done.16.rest_4_ = bf16[1024,256]{1,0:T(8,128)(2,1)S(1)} collective-permute-done((bf16[1024,256]{1,0:T(8,128)(2,1)S(1)}, bf16[1024,256]{1,0:T(8,128)(2,1)S(1)}, u32[]{:S(2)}, u32[]{:S(2)}) %collective-permute-start.16) | collective-permute-done | bytes 524320 | tf_op jit(solution)/shard_map/ppermute | solution.py:36
  116.5 1.5 collective-permute-start.20
  118.0 8.7 %shard_map.161.sent_rows = bf16[512,1024]{1,0:T(8,128)(2,1)S(1)} custom-call(s32[6]{0:T(128)S(1)} %pad_add_fusion.1.meta, bf16[2,1024,128]{2,1,0:T(8,128)(2,1)S(1)} %shard_map.158.own, bf16[2,1024,128]{2,1,0:T(8,128)(2,1)S(1)} %collective-permute-done.12.far, bf16[8,1024,128]{2,1,0:T(8,128)(2,1)S(1)} %shard_map.159.rest_0_), custom_call_target="tpu_custom_call" | custom-call | flops 8589934592 | bytes 524288 | tf_op jit(solution)/shard_map/pallas_call | solution.py:281
  128.7 1.5 collective-permute-start.23
  130.2 7.0 %shard_map.160.kept_rows = bf16[512,1024]{1,0:T(8,128)(2,1)S(1)} custom-call(s32[6]{0:T(128)S(1)} %pad_add_fusion.1.meta, bf16[2,1024,128]{2,1,0:T(8,128)(2,1)S(1)} %shard_map.158.own, bf16[2,1024,128]{2,1,0:T(8,128)(2,1)S(1)} %collective-permute-done.12.far, bf16[8,1024,128]{2,1,0:T(8,128)(2,1)S(1)} %shard_map.159.rest_0_), custom_call_target="tpu_custom_call" | custom-call | flops 8589934592 | bytes 524288 | tf_op jit(solution)/shard_map/pallas_call | solution.py:281
  137.2 5.2 %shard_map.162 = (bf16[2,256,1280]{2,1,0:T(8,128)(2,1)S(1)}, bf16[2,256,1280]{2,1,0:T(8,128)(2,1)}) custom-call(bf16[512,1024]{1,0:T(8,128)(2,1)S(1)} %shard_map.160.kept_rows, bf16[512,1024]{1,0:T(8,128)(2,1)S(1)} %shard_map.161.sent_rows, bf16[1024,256]{1,0:T(8,128)(2,1)} %convert_element_type.84.rest_0_, ...), custom_call_target="tpu_custom_call" | custom-call | flops 8053063680 | bytes 5242880 | tf_op jit(solution)/shard_map/pallas_call | solution.py:321
  147.6 3.0 %shard_map.163 = (bf16[2,256,768]{2,1,0:T(8,128)(2,1)S(1)}, bf16[2,256,768]{2,1,0:T(8,128)(2,1)S(1)}) custom-call(bf16[512,1024]{1,0:T(8,128)(2,1)S(1)} %copy-done.18, bf16[512,1024]{1,0:T(8,128)(2,1)S(1)} %copy-done.16, bf16[1024,256]{1,0:T(8,128)(2,1)} %broadcast_select_fusion.2.rest_0_, bf16[1024,256]{1,0:T(8,128)(2,1)S(1)} %copy-done.14, ...), custom_call_target="tpu_custom_call" | custom-call | flops 4831838208 | bytes 3145728 | tf_op jit(solution)/shard_map/pallas_call | solution.py:321
  153.0 2.6 %add_convert_fusion = (bf16[1,256,1280]{2,1,0:T(8,128)(2,1)}, bf16[256,1280]{1,0:T(8,128)(2,1)}) fusion(bf16[2,256,1280]{2,1,0:T(8,128)(2,1)} %collective-permute-done.21, bf16[2,256,1280]{2,1,0:T(8,128)(2,1)S(1)} %copy-done.5), kind=kLoop, calls=%fused_computation.13 | loop fusion | flops 2621440 | bytes 3932160 | tf_op jit(solution)/shard_map/convert_element_type | solution.py:132
  155.6 1.5 collective-permute-start.22
  159.3 2.2 %reduce-window.6 = s32[4,2,128]{2,1,0:T(2,128)S(1)} reduce-window(s32[4,2,128]{2,1,0:T(2,128)} %and_convert_fusion, s32[]{:T(128)} %constant.88.clone.1), window={size=1x1x128 pad=0_0x0_0x127_0}, to_apply=%region_8.9 | reduce-window | flops 130048 | bytes 8196 | tf_op jit(solution)/shard_map/reduce-window
  162.2 1.3 copy.23
  163.5 1.3 reduce-window.9
  164.8 1.3 slice.132
  166.1 1.3 copy.24
  168.9 12.1 %collective-permute-done.25 = bf16[1,256,768]{2,1,0:T(8,128)(2,1)} collective-permute-done((bf16[1,256,768]{2,1,0:T(8,128)(2,1)}, bf16[1,256,768]{2,1,0:T(8,128)(2,1)}, u32[]{:S(2)}, u32[]{:S(2)}) %collective-permute-start.25) | collective-permute-done | bytes 393248 | tf_op jit(solution)/shard_map/ppermute | solution.py:36
  183.3 4.1 %shard_map.164 = (bf16[256,2048]{1,0:T(8,128)(2,1)}, bf16[256,2048]{1,0:T(8,128)(2,1)S(1)}) custom-call(s32[8]{0:T(128)S(1)} %pad_add_fusion.meta, bf16[256,2048]{1,0:T(8,128)(2,1)S(1)} %copy-done.2, f32[1,2048]{1,0:T(1,128)S(1)} %bitcast.60, bf16[256,1280]{1,0:T(8,128)(2,1)S(1)} %copy-done.3, bf16[256,1280]{1,0:T(8,128)(2,1)} %bitcast.8.rest_1_, ...), custom_call_target="tpu_custom_call" | custom-call | tf_op jit(solution)/shard_map/pallas_call | solution.py:354
  189.0 1.3 collective-permute-start.27
  191.3 6.0 %collective-permute-done.28 = bf16[64,2048]{1,0:T(8,128)(2,1)S(1)} collective-permute-done((bf16[64,2048]{1,0:T(8,128)(2,1)S(1)}, bf16[64,2048]{1,0:T(8,128)(2,1)S(1)}, u32[]{:S(2)}, u32[]{:S(2)}) %collective-permute-start.28) | collective-permute-done | bytes 262176 | tf_op jit(solution)/shard_map/ppermute | solution.py:36
  197.2 5.7 %collective-permute-done.26 = bf16[64,2048]{1,0:T(8,128)(2,1)S(1)} collective-permute-done((bf16[64,2048]{1,0:T(8,128)(2,1)S(1)}, bf16[64,2048]{1,0:T(8,128)(2,1)S(1)}, u32[]{:S(2)}, u32[]{:S(2)}) %collective-permute-start.26) | collective-permute-done | bytes 262176 | tf_op jit(solution)/shard_map/ppermute | solution.py:36
  203.0 4.6 %fusion = f32[256,1536]{1,0:T(8,128)S(1)} fusion(bf16[256,2048]{1,0:T(8,128)(2,1)S(1)} %bitcast.62, bf16[1,2048,1536]{2,1,0:T(8,128)(2,1)} %param.25), kind=kOutput, calls=%fused_computation | convolution fusion | flops 1610612736 | bytes 8912896 | tf_op jit(solution)/shard_map/dot_general | solution.py:494
  209.2 1.8 collective-permute-start.29
  212.2 5.0 %collective-permute-done.31 = bf16[64,2048]{1,0:T(8,128)(2,1)S(1)} collective-permute-done((bf16[64,2048]{1,0:T(8,128)(2,1)S(1)}, bf16[64,2048]{1,0:T(8,128)(2,1)S(1)}, u32[]{:S(2)}, u32[]{:S(2)}) %collective-permute-start.31) | collective-permute-done | bytes 262176 | tf_op jit(solution)/shard_map/ppermute | solution.py:36
  217.2 5.8 %collective-permute-done.29 = bf16[64,2048]{1,0:T(8,128)(2,1)S(1)} collective-permute-done((bf16[64,2048]{1,0:T(8,128)(2,1)S(1)}, bf16[64,2048]{1,0:T(8,128)(2,1)S(1)}, u32[]{:S(2)}, u32[]{:S(2)}) %collective-permute-start.29) | collective-permute-done | bytes 262176 | tf_op jit(solution)/shard_map/ppermute | solution.py:36
  223.2 1.5 fusion.4
  (154 shorter events, 35.7 us)
Async XLA Ops:
  0.6 207.0 %copy-start = (bf16[1,768,2048]{2,1,0:T(8,128)(2,1)S(1)}, bf16[1,768,2048]{2,1,0:T(8,128)(2,1)}, u32[]{:S(2)}) copy-start(bf16[1,768,2048]{2,1,0:T(8,128)(2,1)} %param.26) | copy-start | bytes 9437188
  0.7 11.6 %copy-start.25 = (f32[2048]{0:T(1024)S(1)}, f32[2048]{0:T(1024)}, u32[]{:S(2)}) copy-start(f32[2048]{0:T(1024)} %param.16) | copy-start | bytes 24580
  2.9 9.0 %copy-start.1 = (bf16[256,2048]{1,0:T(8,128)(2,1)S(1)}, bf16[256,2048]{1,0:T(8,128)(2,1)}, u32[]{:S(2)}) copy-start(bf16[256,2048]{1,0:T(8,128)(2,1)} %states.1) | copy-start | bytes 3145732
  5.9 18.1 %collective-permute-start = (bf16[256,1280]{1,0:T(8,128)(2,1)}, bf16[256,1280]{1,0:T(8,128)(2,1)}, u32[]{:S(2)}, u32[]{:S(2)}) collective-permute-start(bf16[256,1280]{1,0:T(8,128)(2,1)} %pad_maximum_fusion.2.rest_7_), channel_id=1, source_target_pairs={{0,8},{4,12},{8,0},{12,4},{16,24},{20,28},{24,16},{28,20},{1,9},{5... | collective-permute-start | bytes 1966088 | tf_op jit(solution)/shard_map/ppermute | solution.py:54
  8.9 15.0 %collective-permute-start.1 = (bf16[256,1280]{1,0:T(8,128)(2,1)}, bf16[256,1280]{1,0:T(8,128)(2,1)}, u32[]{:S(2)}, u32[]{:S(2)}) collective-permute-start(bf16[256,1280]{1,0:T(8,128)(2,1)} %pad_maximum_fusion.2.rest_7_), channel_id=1, source_target_pairs={{8,16},{12,20},{16,8},{20,12},{9,17},{13,21},{17,9},{21,13},{10,18... | collective-permute-start | bytes 1966088 | tf_op jit(solution)/shard_map/ppermute | solution.py:54
  10.5 16.5 %collective-permute-start.2 = (bf16[256,1280]{1,0:T(8,128)(2,1)}, bf16[256,1280]{1,0:T(8,128)(2,1)}, u32[]{:S(2)}, u32[]{:S(2)}) collective-permute-start(bf16[256,1280]{1,0:T(8,128)(2,1)} %pad_maximum_fusion.2.rest_7_), channel_id=1, source_target_pairs={{0,4},{4,0},{8,12},{12,8},{16,20},{20,16},{24,28},{28,24},{1,5},{5... | collective-permute-start | bytes 1966088 | tf_op jit(solution)/shard_map/ppermute | solution.py:36
  12.3 18.3 %copy-start.30 = (f32[128]{0:T(128)S(1)}, f32[128]{0:T(128)}, u32[]{:S(2)}) copy-start(f32[128]{0:T(128)} %param.21) | copy-start | bytes 1540
  13.6 37.7 %copy-start.31 = (s32[4]{0:T(128)S(1)}, s32[4]{0:T(128)}, u32[]{:S(2)}) copy-start(s32[4]{0:T(128)} %param.23) | copy-start | bytes 52
  13.6 40.1 %collective-permute-start.3 = (bf16[256,2048]{1,0:T(8,128)(2,1)}, bf16[256,2048]{1,0:T(8,128)(2,1)}, u32[]{:S(2)}, u32[]{:S(2)}) collective-permute-start(bf16[256,2048]{1,0:T(8,128)(2,1)} %fusion.10.rest_0_), channel_id=1, source_target_pairs={{0,2},{1,3},{2,0},{3,1},{4,6},{5,7},{6,4},{7,5},{8,10},{9,11},{10,... | collective-permute-start | bytes 3145736 | tf_op jit(solution)/shard_map/ppermute | solution.py:36
  15.1 73.0 %collective-permute-start.4 = (bf16[256,2048]{1,0:T(8,128)(2,1)}, bf16[256,2048]{1,0:T(8,128)(2,1)}, u32[]{:S(2)}, u32[]{:S(2)}) collective-permute-start(bf16[256,2048]{1,0:T(8,128)(2,1)} %fusion.10.rest_0_), channel_id=1, source_target_pairs={{0,1},{1,0},{2,3},{3,2},{4,5},{5,4},{6,7},{7,6},{8,9},{9,8},{10,11... | collective-permute-start | bytes 3145736 | tf_op jit(solution)/shard_map/ppermute | solution.py:36
  17.3 134.9 %copy-start.27 = (s32[4]{0:T(128)}, s32[4]{0:T(128)S(1)}, u32[]{:S(2)}) copy-start(s32[4]{0:T(128)S(1)} %broadcast_xor_fusion) | copy-start | bytes 52
  27.0 15.5 %collective-permute-start.6 = (bf16[256,1280]{1,0:T(8,128)(2,1)}, bf16[256,1280]{1,0:T(8,128)(2,1)S(1)}, u32[]{:S(2)}, u32[]{:S(2)}) collective-permute-start(bf16[256,1280]{1,0:T(8,128)(2,1)} %collective-permute-done.rest_8_), channel_id=1, source_target_pairs={{0,4},{4,0},{8,12},{12,8},{16,20},{20,16},{24,28},{28,24},{1,5},{5... | collective-permute-start | bytes 1966088 | tf_op jit(solution)/shard_map/ppermute | solution.py:36
  28.5 14.9 %collective-permute-start.7 = (bf16[256,1280]{1,0:T(8,128)(2,1)}, bf16[256,1280]{1,0:T(8,128)(2,1)S(1)}, u32[]{:S(2)}, u32[]{:S(2)}) collective-permute-start(bf16[256,1280]{1,0:T(8,128)(2,1)} %collective-permute-done.rest_8_), channel_id=1, source_target_pairs={{8,16},{12,20},{16,8},{20,12},{9,17},{13,21},{17,9},{21,13},{10,18... | collective-permute-start | bytes 1966088 | tf_op jit(solution)/shard_map/ppermute | solution.py:54
  29.2 19.3 %collective-permute-start.8 = (bf16[256,1280]{1,0:T(8,128)(2,1)}, bf16[256,1280]{1,0:T(8,128)(2,1)S(1)}, u32[]{:S(2)}, u32[]{:S(2)}) collective-permute-start(bf16[256,1280]{1,0:T(8,128)(2,1)} %collective-permute-done.1), channel_id=1, source_target_pairs={{8,0},{12,4},{16,24},{20,28},{9,1},{13,5},{17,25},{21,29},{10,2},{... | collective-permute-start | bytes 1966088 | tf_op jit(solution)/shard_map/ppermute | solution.py:54
  48.5 17.7 %collective-permute-start.9 = (bf16[256,1280]{1,0:T(8,128)(2,1)S(1)}, bf16[256,1280]{1,0:T(8,128)(2,1)S(1)}, u32[]{:S(2)}, u32[]{:S(2)}) collective-permute-start(bf16[256,1280]{1,0:T(8,128)(2,1)S(1)} %broadcast_select_fusion.1.rest_9_), channel_id=1, source_target_pairs={{0,4},{4,0},{8,12},{12,8},{16,20},{20,16},{24,28},{28,24},{1,5},{5... | collective-permute-start | bytes 1966088 | tf_op jit(solution)/shard_map/ppermute | solution.py:36
  50.0 17.2 %collective-permute-start.10 = (bf16[256,1280]{1,0:T(8,128)(2,1)S(1)}, bf16[256,1280]{1,0:T(8,128)(2,1)S(1)}, u32[]{:S(2)}, u32[]{:S(2)}) collective-permute-start(bf16[256,1280]{1,0:T(8,128)(2,1)S(1)} %collective-permute-done.7), channel_id=1, source_target_pairs={{8,0},{12,4},{16,24},{20,28},{9,1},{13,5},{17,25},{21,29},{10,2},{... | collective-permute-start | bytes 1966088 | tf_op jit(solution)/shard_map/ppermute | solution.py:54
  52.1 25.5 %collective-permute-start.13 = (bf16[1024,256]{1,0:T(8,128)(2,1)}, bf16[1024,256]{1,0:T(8,128)(2,1)}, u32[]{:S(2)}, u32[]{:S(2)}) collective-permute-start(bf16[1024,256]{1,0:T(8,128)(2,1)} %convert_element_type.84.rest_0_), channel_id=1, source_target_pairs={{0,4},{4,0},{8,12},{12,8},{16,20},{20,16},{24,28},{28,24},{1,5},{5... | collective-permute-start | bytes 1572872 | tf_op jit(solution)/shard_map/ppermute | solution.py:36
  53.6 34.4 %collective-permute-start.5 = (bf16[256,2048]{1,0:T(8,128)(2,1)}, bf16[256,2048]{1,0:T(8,128)(2,1)}, u32[]{:S(2)}, u32[]{:S(2)}) collective-permute-start(bf16[256,2048]{1,0:T(8,128)(2,1)} %collective-permute-done.3.rest_1_), channel_id=1, source_target_pairs={{0,1},{1,0},{2,3},{3,2},{4,5},{5,4},{6,7},{7,6},{8,9},{9,8},{10,11... | collective-permute-start | bytes 3145736 | tf_op jit(solution)/shard_map/ppermute | solution.py:36
  68.1 20.0 %collective-permute-start.11 = (bf16[256,1280]{1,0:T(8,128)(2,1)}, bf16[256,1280]{1,0:T(8,128)(2,1)}, u32[]{:S(2)}, u32[]{:S(2)}) collective-permute-start(bf16[256,1280]{1,0:T(8,128)(2,1)} %broadcast_select_fusion.rest_10_), channel_id=1, source_target_pairs={{0,4},{4,0},{8,12},{12,8},{16,20},{20,16},{24,28},{28,24},{1,5},{5... | collective-permute-start | bytes 1966088 | tf_op jit(solution)/shard_map/ppermute | solution.py:36
  77.6 9.4 %collective-permute-start.14 = (bf16[1024,256]{1,0:T(8,128)(2,1)}, bf16[1024,256]{1,0:T(8,128)(2,1)S(1)}, u32[]{:S(2)}, u32[]{:S(2)}) collective-permute-start(bf16[1024,256]{1,0:T(8,128)(2,1)} %convert_element_type.84.rest_0_), channel_id=1, source_target_pairs={{0,8},{4,12},{8,0},{12,4},{16,24},{20,28},{24,16},{28,20},{1,9},{5... | collective-permute-start | bytes 1572872 | tf_op jit(solution)/shard_map/ppermute | solution.py:54
  78.8 8.2 %collective-permute-start.15 = (bf16[1024,256]{1,0:T(8,128)(2,1)}, bf16[1024,256]{1,0:T(8,128)(2,1)S(1)}, u32[]{:S(2)}, u32[]{:S(2)}) collective-permute-start(bf16[1024,256]{1,0:T(8,128)(2,1)} %convert_element_type.84.rest_0_), channel_id=1, source_target_pairs={{8,16},{12,20},{16,8},{20,12},{9,17},{13,21},{17,9},{21,13},{10,18... | collective-permute-start | bytes 1572872 | tf_op jit(solution)/shard_map/ppermute | solution.py:54
  81.4 6.6 %copy-start.7 = (bf16[256,1280]{1,0:T(8,128)(2,1)S(1)}, bf16[256,1280]{1,0:T(8,128)(2,1)}, u32[]{:S(2)}) copy-start(bf16[256,1280]{1,0:T(8,128)(2,1)} %copy-done.6) | copy-start | bytes 1966084
  81.4 6.6 %copy-start.10 = (bf16[256,1280]{1,0:T(8,128)(2,1)S(1)}, bf16[256,1280]{1,0:T(8,128)(2,1)}, u32[]{:S(2)}) copy-start(bf16[256,1280]{1,0:T(8,128)(2,1)} %copy-done.9) | copy-start | bytes 1966084
  81.4 6.6 %copy-start.12 = (bf16[256,1280]{1,0:T(8,128)(2,1)S(1)}, bf16[256,1280]{1,0:T(8,128)(2,1)}, u32[]{:S(2)}) copy-start(bf16[256,1280]{1,0:T(8,128)(2,1)} %copy-done.11) | copy-start | bytes 1966084
  92.6 23.3 %collective-permute-start.12 = (bf16[2,1024,128]{2,1,0:T(8,128)(2,1)S(1)}, bf16[2,1024,128]{2,1,0:T(8,128)(2,1)S(1)}, u32[]{:S(2)}, u32[]{:S(2)}) collective-permute-start(bf16[2,1024,128]{2,1,0:T(8,128)(2,1)S(1)} %shard_map.158.own), channel_id=1, source_target_pairs={{0,4},{4,0},{8,12},{12,8},{16,20},{20,16},{24,28},{28,24},{1,5},{5... | collective-permute-start | bytes 1572872 | tf_op jit(solution)/shard_map/ppermute | solution.py:36
  93.2 22.6 %collective-permute-start.16 = (bf16[1024,256]{1,0:T(8,128)(2,1)S(1)}, bf16[1024,256]{1,0:T(8,128)(2,1)S(1)}, u32[]{:S(2)}, u32[]{:S(2)}) collective-permute-start(bf16[1024,256]{1,0:T(8,128)(2,1)S(1)} %collective-permute-done.14.rest_1_), channel_id=1, source_target_pairs={{0,4},{4,0},{8,12},{12,8},{16,20},{20,16},{24,28},{28,24},{1,5},{5... | collective-permute-start | bytes 1572872 | tf_op jit(solution)/shard_map/ppermute | solution.py:36
  94.7 21.2 %collective-permute-start.17 = (bf16[1024,256]{1,0:T(8,128)(2,1)S(1)}, bf16[1024,256]{1,0:T(8,128)(2,1)S(1)}, u32[]{:S(2)}, u32[]{:S(2)}) collective-permute-start(bf16[1024,256]{1,0:T(8,128)(2,1)S(1)} %collective-permute-done.14.rest_1_), channel_id=1, source_target_pairs={{8,16},{12,20},{16,8},{20,12},{9,17},{13,21},{17,9},{21,13},{10,18... | collective-permute-start | bytes 1572872 | tf_op jit(solution)/shard_map/ppermute | solution.py:54
  95.4 20.5 %collective-permute-start.18 = (bf16[1024,256]{1,0:T(8,128)(2,1)S(1)}, bf16[1024,256]{1,0:T(8,128)(2,1)S(1)}, u32[]{:S(2)}, u32[]{:S(2)}) collective-permute-start(bf16[1024,256]{1,0:T(8,128)(2,1)S(1)} %collective-permute-done.15), channel_id=1, source_target_pairs={{8,0},{12,4},{16,24},{20,28},{9,1},{13,5},{17,25},{21,29},{10,2},{... | collective-permute-start | bytes 1572872 | tf_op jit(solution)/shard_map/ppermute | solution.py:54
  115.9 10.8 %collective-permute-start.19 = (bf16[1024,256]{1,0:T(8,128)(2,1)S(1)}, bf16[1024,256]{1,0:T(8,128)(2,1)S(1)}, u32[]{:S(2)}, u32[]{:S(2)}) collective-permute-start(bf16[1024,256]{1,0:T(8,128)(2,1)S(1)} %broadcast_select_fusion.3.rest_2_), channel_id=1, source_target_pairs={{0,4},{4,0},{8,12},{12,8},{16,20},{20,16},{24,28},{28,24},{1,5},{5... | collective-permute-start | bytes 1572872 | tf_op jit(solution)/shard_map/ppermute | solution.py:36
  116.5 11.3 %collective-permute-start.20 = (bf16[1024,256]{1,0:T(8,128)(2,1)S(1)}, bf16[1024,256]{1,0:T(8,128)(2,1)S(1)}, u32[]{:S(2)}, u32[]{:S(2)}) collective-permute-start(bf16[1024,256]{1,0:T(8,128)(2,1)S(1)} %collective-permute-done.17), channel_id=1, source_target_pairs={{8,0},{12,4},{16,24},{20,28},{9,1},{13,5},{17,25},{21,29},{10,2},{... | collective-permute-start | bytes 1572872 | tf_op jit(solution)/shard_map/ppermute | solution.py:54
  126.7 10.5 %copy-start.15 = (bf16[512,1024]{1,0:T(8,128)(2,1)}, bf16[512,1024]{1,0:T(8,128)(2,1)S(1)}, u32[]{:S(2)}) copy-start(bf16[512,1024]{1,0:T(8,128)(2,1)S(1)} %shard_map.161.sent_rows) | copy-start | bytes 3145732
  128.7 15.3 %collective-permute-start.23 = (bf16[1024,256]{1,0:T(8,128)(2,1)}, bf16[1024,256]{1,0:T(8,128)(2,1)}, u32[]{:S(2)}, u32[]{:S(2)}) collective-permute-start(bf16[1024,256]{1,0:T(8,128)(2,1)} %broadcast_select_fusion.2.rest_0_), channel_id=1, source_target_pairs={{0,4},{4,0},{8,12},{12,8},{16,20},{20,16},{24,28},{28,24},{1,5},{5... | collective-permute-start | bytes 1572872 | tf_op jit(solution)/shard_map/ppermute | solution.py:36
  143.5 9.4 %collective-permute-start.21 = (bf16[2,256,1280]{2,1,0:T(8,128)(2,1)}, bf16[2,256,1280]{2,1,0:T(8,128)(2,1)}, u32[]{:S(2)}, u32[]{:S(2)}) collective-permute-start(bf16[2,256,1280]{2,1,0:T(8,128)(2,1)} %get-tuple-element.75), channel_id=1, source_target_pairs={{0,1},{1,0},{2,3},{3,2},{4,5},{5,4},{6,7},{7,6},{8,9},{9,8},{10,11... | collective-permute-start | bytes 3932168 | tf_op jit(solution)/shard_map/ppermute | solution.py:36
  143.6 6.9 %copy-start.19 = (s32[256,8]{1,0:T(8,128)}, s32[256,8]{1,0:T(8,128)S(1)}, u32[]{:S(2)}) copy-start(s32[256,8]{1,0:T(8,128)S(1)} %copy.20) | copy-start | bytes 24580
  143.8 8.5 %copy-start.22 = (pred[256]{0:T(512)(128)(4,1)}, pred[256]{0:T(512)(128)(4,1)S(1)}, u32[]{:S(2)}) copy-start(pred[256]{0:T(512)(128)(4,1)S(1)} %fusion.31) | copy-start | bytes 772
  143.9 8.4 %copy-start.24 = (s32[256]{0:T(256)}, s32[256]{0:T(256)S(1)}, u32[]{:S(2)}) copy-start(s32[256]{0:T(256)S(1)} %select_reduce_fusion.1) | copy-start | bytes 3076
  144.0 9.0 %copy-start.5 = (bf16[2,256,1280]{2,1,0:T(8,128)(2,1)S(1)}, bf16[2,256,1280]{2,1,0:T(8,128)(2,1)}, u32[]{:S(2)}) copy-start(bf16[2,256,1280]{2,1,0:T(8,128)(2,1)} %copy-done.4) | copy-start | bytes 3932164
  150.6 6.5 %collective-permute-start.24 = (bf16[2,256,768]{2,1,0:T(8,128)(2,1)S(1)}, bf16[2,256,768]{2,1,0:T(8,128)(2,1)S(1)}, u32[]{:S(2)}, u32[]{:S(2)}) collective-permute-start(bf16[2,256,768]{2,1,0:T(8,128)(2,1)S(1)} %get-tuple-element.80), channel_id=1, source_target_pairs={{0,1},{1,0},{2,3},{3,2},{4,5},{5,4},{6,7},{7,6},{8,9},{9,8},{10,11... | collective-permute-start | bytes 2359304 | tf_op jit(solution)/shard_map/ppermute | solution.py:36
  155.6 25.4 %copy-start.8 = (f32[2048]{0:T(1024)S(1)}, f32[2048]{0:T(1024)}, u32[]{:S(2)}) copy-start(f32[2048]{0:T(1024)} %param.17) | copy-start | bytes 24580
  155.6 25.4 %collective-permute-start.22 = (bf16[1,256,1280]{2,1,0:T(8,128)(2,1)}, bf16[1,256,1280]{2,1,0:T(8,128)(2,1)}, u32[]{:S(2)}, u32[]{:S(2)}) collective-permute-start(bf16[1,256,1280]{2,1,0:T(8,128)(2,1)} %get-tuple-element.84), channel_id=1, source_target_pairs={{0,2},{1,3},{2,0},{3,1},{4,6},{5,7},{6,4},{7,5},{8,10},{9,11},{10,... | collective-permute-start | bytes 1966088 | tf_op jit(solution)/shard_map/ppermute | solution.py:36
  158.1 22.9 %collective-permute-start.25 = (bf16[1,256,768]{2,1,0:T(8,128)(2,1)}, bf16[1,256,768]{2,1,0:T(8,128)(2,1)}, u32[]{:S(2)}, u32[]{:S(2)}) collective-permute-start(bf16[1,256,768]{2,1,0:T(8,128)(2,1)} %get-tuple-element.86), channel_id=1, source_target_pairs={{0,2},{1,3},{2,0},{3,1},{4,6},{5,7},{6,4},{7,5},{8,10},{9,11},{10,... | collective-permute-start | bytes 1179656 | tf_op jit(solution)/shard_map/ppermute | solution.py:36
  188.6 8.6 %collective-permute-start.28 = (bf16[64,2048]{1,0:T(8,128)(2,1)S(1)}, bf16[64,2048]{1,0:T(8,128)(2,1)S(1)}, u32[]{:S(2)}, u32[]{:S(2)}) collective-permute-start(bf16[64,2048]{1,0:T(8,128)(2,1)S(1)} %get-tuple-element.93), channel_id=1, source_target_pairs={{0,3},{1,2},{2,1},{3,0},{4,7},{5,6},{6,5},{7,4},{8,11},{9,10},{10,... | collective-permute-start | bytes 786440 | tf_op jit(solution)/shard_map/ppermute | solution.py:36
  189.0 8.3 %collective-permute-start.27 = (bf16[64,2048]{1,0:T(8,128)(2,1)S(1)}, bf16[64,2048]{1,0:T(8,128)(2,1)S(1)}, u32[]{:S(2)}, u32[]{:S(2)}) collective-permute-start(bf16[64,2048]{1,0:T(8,128)(2,1)S(1)} %get-tuple-element.94), channel_id=1, source_target_pairs={{0,1},{1,0},{2,3},{3,2},{4,5},{5,4},{6,7},{7,6},{8,9},{9,8},{10,11... | collective-permute-start | bytes 786440 | tf_op jit(solution)/shard_map/ppermute | solution.py:36
  190.3 12.6 %collective-permute-start.26 = (bf16[64,2048]{1,0:T(8,128)(2,1)S(1)}, bf16[64,2048]{1,0:T(8,128)(2,1)S(1)}, u32[]{:S(2)}, u32[]{:S(2)}) collective-permute-start(bf16[64,2048]{1,0:T(8,128)(2,1)S(1)} %get-tuple-element.95), channel_id=1, source_target_pairs={{0,2},{1,3},{2,0},{3,1},{4,6},{5,7},{6,4},{7,5},{8,10},{9,11},{10,... | collective-permute-start | bytes 786440 | tf_op jit(solution)/shard_map/ppermute | solution.py:36
  208.7 14.5 %copy-start.23 = (pred[256]{0:T(512)(128)(4,1)S(1)}, pred[256]{0:T(512)(128)(4,1)}, u32[]{:S(2)}) copy-start(pred[256]{0:T(512)(128)(4,1)} %copy-done.22) | copy-start | bytes 772
  208.8 8.4 %collective-permute-start.31 = (bf16[64,2048]{1,0:T(8,128)(2,1)S(1)}, bf16[64,2048]{1,0:T(8,128)(2,1)S(1)}, u32[]{:S(2)}, u32[]{:S(2)}) collective-permute-start(bf16[64,2048]{1,0:T(8,128)(2,1)S(1)} %get-tuple-element.89), channel_id=1, source_target_pairs={{0,3},{1,2},{2,1},{3,0},{4,7},{5,6},{6,5},{7,4},{8,11},{9,10},{10,... | collective-permute-start | bytes 786440 | tf_op jit(solution)/shard_map/ppermute | solution.py:36
  209.2 8.1 %collective-permute-start.30 = (bf16[64,2048]{1,0:T(8,128)(2,1)S(1)}, bf16[64,2048]{1,0:T(8,128)(2,1)S(1)}, u32[]{:S(2)}, u32[]{:S(2)}) collective-permute-start(bf16[64,2048]{1,0:T(8,128)(2,1)S(1)} %get-tuple-element.90), channel_id=1, source_target_pairs={{0,1},{1,0},{2,3},{3,2},{4,5},{5,4},{6,7},{7,6},{8,9},{9,8},{10,11... | collective-permute-start | bytes 786440 | tf_op jit(solution)/shard_map/ppermute | solution.py:36
  209.2 13.8 %collective-permute-start.29 = (bf16[64,2048]{1,0:T(8,128)(2,1)S(1)}, bf16[64,2048]{1,0:T(8,128)(2,1)S(1)}, u32[]{:S(2)}, u32[]{:S(2)}) collective-permute-start(bf16[64,2048]{1,0:T(8,128)(2,1)S(1)} %get-tuple-element.91), channel_id=1, source_target_pairs={{0,2},{1,3},{2,0},{3,1},{4,6},{5,7},{6,4},{7,5},{8,10},{9,11},{10,... | collective-permute-start | bytes 786440 | tf_op jit(solution)/shard_map/ppermute | solution.py:36
  (17 other events, 45.4 us)

commit v4 on v3

--- a/solution.py
+++ b/solution.py
@@ -54,28 +54,28 @@
     return lax.ppermute(block, "group", [(2 * a + s, 2 * b + s) for a, b in moves for s in range(2)])
 
 
-def line_rounds(block, shards, crossed):
+def line_rounds(block, shards, crossed, head):
     place = lax.axis_index("group") // 2
     edge = (place == 0) | (place == 3)
     shards[0] = block
     if crossed is None:
-        shards[1], inner, shards[4] = yield along(block, PAIRS), along(block, MIDDLE), cross(block)
+        shards[1], inner, shards[4] = yield along(block, PAIRS), along(block, MIDDLE), cross(block[head:])
     else:
         shards[4] = crossed
         shards[1], inner = yield along(block, PAIRS), along(block, MIDDLE)
-    shards[5], inner_far, outer = yield cross(shards[1]), along(shards[1], MIDDLE), along(inner, OUTWARD)
+    shards[5], inner_far, outer = yield cross(shards[1][head:]), along(shards[1], MIDDLE), along(inner, OUTWARD)
     shards[2] = jnp.where(edge, outer, inner)
-    shards[6], outer = yield cross(shards[2]), along(inner_far, OUTWARD)
+    shards[6], outer = yield cross(shards[2][head:]), along(inner_far, OUTWARD)
     shards[3] = jnp.where(edge, outer, inner_far)
-    (shards[7],) = yield (cross(shards[3]),)
+    (shards[7],) = yield (cross(shards[3][head:]),)
     yield ()
 
 
 class Beside:
-    def __init__(self, block, crossed=None):
+    def __init__(self, block, crossed=None, head=0):
         groups = lax.axis_size("group")
         self.found = [None] * groups if groups == 8 else list(lax.all_gather(block, "group"))
-        self.chain = line_rounds(block, self.found, crossed) if groups == 8 else None
+        self.chain = line_rounds(block, self.found, crossed, head) if groups == 8 else None
         self.brought = (block,) if self.chain is None else lax.optimization_barrier(next(self.chain))
 
     def round(self, *ready):
@@ -118,18 +118,19 @@
     return blocks
 
 
-def scatter_sum(kept, sent):
-    stride = 1
+def sum_terms(terms):
+    return functools.reduce(jnp.add, [term.astype(jnp.float32) for term in terms]).astype(jnp.bfloat16)
+
+
+def scatter_rest(kept, sent):
+    stride = 2
     while True:
-        half = kept.shape[0] // 2
-        arrived = from_xor(sent, "expert", stride)
+        kept = [*kept, from_xor(sent, "expert", stride)]
+        half = sent.shape[0] // 2
         if not half:
-            return (kept[0], arrived[0]), sent
-        summed = [
-            kept[part].astype(jnp.float32) + arrived[part].astype(jnp.float32)
-            for part in (slice(None, half), slice(half, None))
-        ]
-        kept, sent = [part.astype(jnp.bfloat16) for part in summed]
+            return [term[0] for term in kept]
+        whole = sum_terms(kept)
+        kept, sent = [whole[:half]], whole[half:]
         stride *= 2
 
 
@@ -137,6 +138,34 @@
     depth = weights.shape[0] // len(refs)
     for index, ref in enumerate(refs):
         weights[pl.ds(pl.multiple_of(meta[2 + index] * depth, depth), depth), :] = ref[...]
+
+
+def pack_kernel(meta, query, pair, out):
+    dim = HEAD_DIMENSION
+    out[:, :dim] = pair[0].astype(jnp.bfloat16)
+    out[:, dim : 2 * dim] = pair[1].astype(jnp.bfloat16)
+    out[:, 2 * dim :] = query[...].astype(jnp.bfloat16)
+
+
+def pack(head, query, pair):
+    rows, columns = query.shape
+    dim = HEAD_DIMENSION
+    tile = min(64, rows)
+    return pl.pallas_call(
+        pack_kernel,
+        grid_spec=pltpu.PrefetchScalarGridSpec(
+            num_scalar_prefetch=1,
+            grid=(rows // tile,),
+            in_specs=[
+                pl.BlockSpec((tile, columns), lambda i, meta: (i, 0)),
+                pl.BlockSpec((2, tile, dim), lambda i, meta: (0, i, meta[0])),
+            ],
+            out_specs=pl.BlockSpec((tile, columns + 2 * dim), lambda i, meta: (i, 0)),
+        ),
+        out_shape=jax.ShapeDtypeStruct((rows, columns + 2 * dim), jnp.bfloat16),
+        compiler_params=pltpu.CompilerParams(vmem_limit_bytes=VMEM_LIMIT),
+        cost_estimate=FREE,
+    )(head, query, pair)
 
 
 def turn(values, cosines, sines, mixer):
@@ -151,11 +180,16 @@
 
 def query_kernel(count, meta, *rest):
     rows, (cosine, sine, mixer, *rest) = rest[:count], rest[count:]
-    *shards, query_out, weights = rest
+    *shards, query_out, weights, joined = rest
     stack_shards(meta, shards, weights)
     tile, dim = rows[0].shape[0], HEAD_DIMENSION
-    joined = jnp.concatenate([block[...] for block in rows], axis=0)
-    projected = jnp.dot(joined, weights[...], preferred_element_type=jnp.float32)
+
+    @pl.when(pl.program_id(0) == 0)
+    def _():
+        for index, block in enumerate(rows):
+            joined[index * tile : (index + 1) * tile, :] = block[...]
+
+    projected = jnp.dot(joined[...], weights[...], preferred_element_type=jnp.float32)
     for block in range(count):
         spot = pl.ds(pl.multiple_of(meta[2 + len(shards) + block] * tile, tile), tile)
         here = slice(block * tile, (block + 1) * tile)
@@ -167,11 +201,16 @@
 
 def key_kernel(count, meta, *rest):
     rows, (cosine, sine, mixer, *rest) = rest[:count], rest[count:]
-    *shards, pair_out, weights = rest
+    *shards, pair_out, weights, joined = rest
     stack_shards(meta, shards, weights)
     tile, dim = rows[0].shape[0], HEAD_DIMENSION
-    joined = jnp.concatenate([block[...] for block in rows], axis=0)
-    projected = jnp.dot(joined, weights[...], preferred_element_type=jnp.float32)
+
+    @pl.when(pl.program_id(0) == 0)
+    def _():
+        for index, block in enumerate(rows):
+            joined[index * tile : (index + 1) * tile, :] = block[...]
+
+    projected = jnp.dot(joined[...], weights[...], preferred_element_type=jnp.float32)
     for block in range(count):
         spot = pl.ds(pl.multiple_of(meta[2 + len(shards) + block] * tile, tile), tile)
         here = slice(block * tile, (block + 1) * tile)
@@ -197,7 +236,10 @@
             ]
             + [shard] * len(shards),
             out_specs=pl.BlockSpec((2, count * tile, dim), lambda n, meta: (n, 0, 0)),
-            scratch_shapes=[pltpu.VMEM((width, 2 * dim), jnp.bfloat16)],
+            scratch_shapes=[
+                pltpu.VMEM((width, 2 * dim), jnp.bfloat16),
+                pltpu.VMEM((count * tile, width), jnp.bfloat16),
+            ],
         ),
         out_shape=jax.ShapeDtypeStruct((2 * steps, count * tile, dim), jnp.bfloat16),
         compiler_params=pltpu.CompilerParams(vmem_limit_bytes=VMEM_LIMIT),
@@ -207,7 +249,7 @@
     )(meta, *blocks, cosine, sine, mixer, *shards)
 
 
-def attend_kernel(tile, start, meta, own, far, *rest):
+def attend_kernel(tile, block_of, meta, own, far, *rest):
     *queries, out, keys, values, total = rest
     heads, dim = total.shape[0], HEAD_DIMENSION
     query = [part.at[head] for part in queries for head in range(part.shape[0])]
@@ -230,7 +272,7 @@
                 values[pl.ds(base, half), :dim] = jnp.where(valid, pair[1, source, :], zero)
                 values[pl.ds(base, half), dim:] = jnp.where(valid, ones, zero)
 
-    first = meta[2 + start + step] * tile
+    first = meta[2 + block_of(step)] * tile
     first = first + jnp.where(parity == 0, jnp.where(first < half, 0, 2 * half), half)
 
     def weigh(head, start, width, masked):
@@ -276,15 +318,18 @@
     _, row_count, dim = queries[0].shape
     heads = sum(query.shape[0] for query in queries)
     steps = row_count // tile // 2
-    start = part * steps
+
+    def block_of(step):
+        return step + steps // 2 * (part + (step >= steps // 2))
+
     whole = pl.BlockSpec((2, row_count, dim), lambda i, meta: (0, 0, 0))
     return pl.pallas_call(
-        functools.partial(attend_kernel, tile, start),
+        functools.partial(attend_kernel, tile, block_of),
         grid_spec=pltpu.PrefetchScalarGridSpec(
             num_scalar_prefetch=1,
             grid=(steps,),
             in_specs=[whole] * 2
-            + [pl.BlockSpec((query.shape[0], tile, dim), lambda i, meta: (0, start + i, 0)) for query in queries],
+            + [pl.BlockSpec((query.shape[0], tile, dim), lambda i, meta: (0, block_of(i), 0)) for query in queries],
             out_specs=pl.BlockSpec((tile, heads * dim), lambda i, meta: (i, 0)),
             scratch_shapes=[
                 pltpu.VMEM((2 * row_count, dim), jnp.bfloat16),
@@ -300,70 +345,66 @@
     )(meta, own, far, *queries)
 
 
-def output_kernel(kept_rows, sent_rows, *rest):
+def output_kernel(plan, meta, rows, *rest):
     *shards, kept, sent = rest
     columns = shards[0].shape[1]
-    for rows, out in ((sent_rows, sent), (kept_rows, kept)):
-        for index, shard in enumerate(shards):
-            product = jnp.dot(rows[...], shard[...], preferred_element_type=jnp.float32)
-            here = slice(index * columns, (index + 1) * columns)
-            out[:, :, here] = product.astype(jnp.bfloat16).reshape(*out.shape[:2], -1)
-
-
-def output_part(kept_rows, sent_rows, tile, shards):
-    rows, depth = kept_rows.shape
-    width = len(shards) * shards[0].shape[1]
+    half = rows.shape[0] // 2
+    for index, pieces in enumerate(plan):
+        here = pl.ds(pl.multiple_of(meta[index] * columns, columns), columns)
+        for part, out in enumerate((kept, sent)):
+            product = 0.0
+            for shard, start, size, depth in pieces:
+                left = rows[part * half : (part + 1) * half, depth : depth + size]
+                right = shards[shard][start : start + size, :]
+                product += jnp.dot(left, right, preferred_element_type=jnp.float32)
+            out[:, :, here] = product.astype(jnp.bfloat16).reshape(*out.shape[:2], columns)
+
+
+def output_part(plan, meta, rows, tile, shards):
+    count, depth = rows.shape
+    width = len(plan) * shards[0].shape[1]
 
     def whole(shape):
-        return pl.BlockSpec(shape, lambda n: (0,) * len(shape))
-
-    out = (rows // tile, tile, width)
+        return pl.BlockSpec(shape, lambda n, meta: (0,) * len(shape))
+
+    out = (count // 2 // tile, tile, width)
     return pl.pallas_call(
-        output_kernel,
-        grid=(1,),
-        in_specs=[whole((rows, depth))] * 2 + [whole(shards[0].shape)] * len(shards),
-        out_specs=[whole(out)] * 2,
+        functools.partial(output_kernel, plan),
+        grid_spec=pltpu.PrefetchScalarGridSpec(
+            num_scalar_prefetch=1,
+            grid=(1,),
+            in_specs=[whole((count, depth))] + [whole(shard.shape) for shard in shards],
+            out_specs=[whole(out)] * 2,
+        ),
         out_shape=[jax.ShapeDtypeStruct(out, jnp.bfloat16)] * 2,
         compiler_params=pltpu.CompilerParams(vmem_limit_bytes=VMEM_LIMIT),
-        cost_estimate=pl.CostEstimate(flops=12 * rows * width * depth, bytes_accessed=8 * rows * width, transcendentals=0),
-    )(kept_rows, sent_rows, *shards)
-
-
-def finish_kernel(columns, meta, states, gain, *rest):
+        cost_estimate=FREE,
+    )(meta, rows, *shards)
+
+
+def finish_kernel(states, gain, *rest):
     *terms, hidden_out, normed_out = rest
-    index = 0
-    for kept, arrived in zip(terms[::2], terms[1::2]):
-        for part in range(kept.shape[1] // columns):
-            here = slice(part * columns, (part + 1) * columns)
-            there = pl.ds(pl.multiple_of(meta[index] * columns, columns), columns)
-            total = kept[:, here].astype(jnp.float32) + arrived[:, here].astype(jnp.float32)
-            hidden_out[:, there] = (states[:, there].astype(jnp.float32) + total).astype(jnp.bfloat16)
-            index += 1
-    hidden = hidden_out[...].astype(jnp.float32)
+    total = functools.reduce(jnp.add, [term[...].astype(jnp.float32) for term in terms])
+    rounded = (states[...].astype(jnp.float32) + total).astype(jnp.bfloat16)
+    hidden_out[...] = rounded
+    hidden = rounded.astype(jnp.float32)
     inverse = lax.rsqrt(jnp.mean(hidden * hidden, axis=-1, keepdims=True) + epsilon)
     normed_out[...] = (hidden * inverse * gain[...]).astype(jnp.bfloat16)
 
 
-def finish(meta, states, gain, terms, columns):
+def finish(states, gain, terms):
     rows, width = states.shape
     tile = min(64, rows)
-
-    def block(wide):
-        return pl.BlockSpec((tile, wide), lambda i, meta: (i, 0))
-
+    block = pl.BlockSpec((tile, width), lambda i: (i, 0))
     return pl.pallas_call(
-        functools.partial(finish_kernel, columns),
-        grid_spec=pltpu.PrefetchScalarGridSpec(
-            num_scalar_prefetch=1,
-            grid=(rows // tile,),
-            in_specs=[block(width), pl.BlockSpec((1, width), lambda i, meta: (0, 0))]
-            + [block(term.shape[1]) for term in terms],
-            out_specs=[block(width)] * 2,
-        ),
+        finish_kernel,
+        grid=(rows // tile,),
+        in_specs=[block, pl.BlockSpec((1, width), lambda i: (0, 0))] + [block] * len(terms),
+        out_specs=[block] * 2,
         out_shape=[jax.ShapeDtypeStruct((rows, width), jnp.bfloat16)] * 2,
         compiler_params=pltpu.CompilerParams(vmem_limit_bytes=VMEM_LIMIT),
         cost_estimate=FREE,
-    )(meta, states, gain[None, :], *terms)
+    )(states, gain[None, :], *terms)
 
 
 def per_device(
@@ -392,8 +433,7 @@
     groups = lax.axis_size("group")
     place, side = group_index // 2, group_index % 2
     common_head = group_member * heads // (QUERY_HEADS // KEY_VALUE_HEADS)
-    pair = lax.dynamic_slice_in_dim(trainer_key_value_weight, common_head * dim, dim, 2)
-    joined = jnp.concatenate([pair[0], pair[1], query_master], axis=1).astype(jnp.bfloat16)
+    joined = pack(common_head.astype(jnp.int32).reshape(1), query_master, trainer_key_value_weight)
     output_here = output_master.astype(jnp.bfloat16)
     joined_rounds = Beside(joined)
     normed = norm_rows(after(hidden_in, joined), norm_attention).astype(jnp.bfloat16)
@@ -409,7 +449,17 @@
     output_here, output_crossed = lax.optimization_barrier(
         (output_here, output_crossed, joined_rounds.token())
     )[:2]
-    output_rounds = Beside(output_here, output_crossed)
+    depth = output_here.shape[0]
+    if groups == 8:
+        first = depth // 4
+        rest = depth - first
+        output_block = jnp.concatenate([output_here[:first], output_crossed[:first], output_here[first:]], axis=0)
+        output_rounds = Beside(output_block, output_crossed[first:], 2 * first)
+        plan = [((k, 0, first, 0), (k, 2 * first, rest, first)) for k in range(4)]
+        plan += [((k, first, first, 0), (4 + k, 0, rest, first)) for k in range(4)]
+    else:
+        output_rounds = Beside(output_here)
+        plan = [((k, 0, depth, 0),) for k in range(groups)]
     joined_rounds.round()
     shards = joined_rounds.held(range(groups))
     output_rounds.round(joined_rounds.token())
@@ -456,20 +506,19 @@
 
     valid_length = jnp.sum(jnp.where(jnp.arange(lengths.shape[0]) == group_index // 2, lengths, 0))
     attend_meta = jnp.concatenate([jnp.stack([parity, valid_length]), block_order]).astype(jnp.int32)
-    sent_rows = attend(attend_meta, queries, own_pair, far_pair, rows_here, 1)
+    next_rows = attend(attend_meta, queries, own_pair, far_pair, rows_here, 1)
     queries[0] = after(queries[0], output_rounds.token())
-    output_rounds.round(sent_rows)
-    kept_rows = attend(attend_meta, queries, own_pair, far_pair, rows_here, 0)
-
-    order = [0, 1, 2, 4, 5, 3, 6, 7] if groups == 8 else list(range(groups))
-    cut = groups * 5 // 8
-    output_shards = output_rounds.held(order)
-    terms = []
-    for part in (output_shards[:cut], output_shards[cut:]):
-        both, _ = scatter_sum(*output_part(kept_rows, sent_rows, rows_here, part))
-        terms += both
-    finish_meta = jnp.stack([meta[2 + i] for i in order])
-    hidden, normed_second = finish(finish_meta, hidden_in, norm_experts, terms, output_here.shape[1])
+    output_rounds.round(next_rows)
+    last_rows = attend(attend_meta, queries, own_pair, far_pair, rows_here, 0)
+
+    output_shards = output_rounds.held(range(groups))
+    next_rows = after(next_rows, last_rows)
+    output_meta = held_groups(place, side).astype(jnp.int32)
+    kept, sent = output_part(plan, output_meta, next_rows, rows_here, output_shards)
+    next_sum = sum_terms([kept, from_xor(sent, "expert", 1)])
+    kept, sent = output_part(plan, output_meta, last_rows, rows_here, output_shards)
+    terms = scatter_rest([kept, from_xor(sent, "expert", 1)], next_sum)
+    hidden, normed_second = finish(hidden_in, norm_experts, terms)
 
     logits = jnp.dot(normed_second, router, preferred_element_type=jnp.float32)
     route_table = routes[:, :, None] == jnp.arange(logits.shape[1])[None, None, :]

time: 226 us -> 219 us (0.969)
  other arithmetic: 25.9 us -> 14.4 us
  starting transfers between devices: 31.5 us -> 39.5 us
  local copies, waits for them, and re-layouts: 16.6 us -> 9.74 us
  Pallas kernels: 43.9 us -> 46.4 us
    ppermute x22 -> x21, waiting for transfers between devices: 79.2 us -> 85.9 us  [from_xor(): return lax.ppermute(block, axis, [(i, i ^ mask) for i in range(count)])]
    another operation x6 -> x5, local copies, waits for them, and re-layouts: 5.66 us -> 0.28 us
    ppermute x22 -> x21, starting transfers between devices: 18.4 us -> 23.7 us  [from_xor(): return lax.ppermute(block, axis, [(i, i ^ mask) for i in range(count)])]
    another operation x5 -> x3, other arithmetic: 6.5 us -> 1.26 us
    ppermute x10, waiting for transfers between devices: 17.8 us -> 12.8 us  [along(): lax.ppermute(block, 'group', [(2 * a + s, 2 * b + s) for a, b in moves fo...]
    ppermute x10, starting transfers between devices: 13.1 us -> 15.8 us  [along(): lax.ppermute(block, 'group', [(2 * a + s, 2 * b + s) for a, b in moves fo...]
    pallas_call x5 -> x6, Pallas kernels: 28 us -> 30.3 us  [the longest x2 15.7 us: attend(): pl.pallas_call(functools.partial(attend_kernel, tile, block_of), grid_spe...]
    unnamed x66 -> x50, local copies, waits for them, and re-layouts: 9.65 us -> 7.8 us
  transfers between devices with their start and end apart: 32 -> 31, of which waited for: 16 -> 17; matrix products, arithmetic and copies ran while one was open for 12% -> 7% of each run, Pallas kernels for 16% -> 15%
where the time goes in v4:
time: 219 us; the launch traced here: 218 us
  waiting for transfers between devices  98.7 us (45%)
  Pallas kernels  46.4 us (21%)
  starting transfers between devices  39.5 us (18%)
  other arithmetic  14.4 us (7%)
  local copies, waits for them, and re-layouts  9.74 us (4%)
  matrix products  7.96 us (4%)
    ppermute x21, waiting for transfers between devices, from_xor(): return lax.ppermute(block, axis, [(i, i ^ mask) for i in range(count)])  85.9 us
    ppermute x21, starting transfers between devices, from_xor(): return lax.ppermute(block, axis, [(i, i ^ mask) for i in range(count)])  23.7 us
    pallas_call x2, Pallas kernels, project(): pl.pallas_call(functools.partial(kernel, count), grid_spec=pltpu.Prefetch...  16.1 us
    ppermute x10, starting transfers between devices, along(): lax.ppermute(block, 'group', [(2 * a + s, 2 * b + s) for a, b in moves fo...  15.8 us
    pallas_call x2, Pallas kernels, attend(): pl.pallas_call(functools.partial(attend_kernel, tile, block_of), grid_spe...  15.7 us
    ppermute x10, waiting for transfers between devices, along(): lax.ppermute(block, 'group', [(2 * a + s, 2 * b + s) for a, b in moves fo...  12.8 us
    pallas_call x2, Pallas kernels, output_part(): pl.pallas_call(functools.partial(output_kernel, plan), grid_spec=pltpu.Pr...  9.29 us
    unnamed x50, local copies, waits for them, and re-layouts  7.8 us
  transfers between devices with their start and end apart: 31, of which 17 were waited for; matrix products, arithmetic and copies ran while one was open for 7% of the time, Pallas kernels for 15%

profile of v4, /device:TPU:0, one launch (start us, length us, event | category | flops | bytes accessed | tf_op | source)
XLA Modules:
  0.0 217.9 jit_solution(4199843409100841886)
XLA Ops:
  0.7 1.7 copy-done.3
  3.6 1.5 shard_map.167.rest_7_
  5.1 3.0 %collective-permute-start = (bf16[256,1280]{1,0:T(8,128)(2,1)}, bf16[256,1280]{1,0:T(8,128)(2,1)}, u32[]{:S(2)}, u32[]{:S(2)}) collective-permute-start(bf16[256,1280]{1,0:T(8,128)(2,1)} %shard_map.167.rest_7_), channel_id=1, source_target_pairs={{0,8},{4,12},{8,0},{12,4},{16,24},{20,28},{24,16},{28,20},{1,9},{5... | collective-permute-start | bytes 1966088 | tf_op jit(solution)/shard_map/ppermute | solution.py:54
  8.1 1.5 collective-permute-start.1
  9.6 1.5 collective-permute-start.2
  12.7 1.5 collective-permute-start.3
  14.3 2.1 convert_element_type.56
  17.4 5.7 %collective-permute-done.rest_8_ = bf16[256,1280]{1,0:T(8,128)(2,1)} collective-permute-done((bf16[256,1280]{1,0:T(8,128)(2,1)}, bf16[256,1280]{1,0:T(8,128)(2,1)}, u32[]{:S(2)}, u32[]{:S(2)}) %collective-permute-start) | collective-permute-done | bytes 655392 | tf_op jit(solution)/shard_map/ppermute | solution.py:54
  23.1 3.0 %collective-permute-done.2.rest_11_ = bf16[256,1280]{1,0:T(8,128)(2,1)} collective-permute-done((bf16[256,1280]{1,0:T(8,128)(2,1)}, bf16[256,1280]{1,0:T(8,128)(2,1)}, u32[]{:S(2)}, u32[]{:S(2)}) %collective-permute-start.2) | collective-permute-done | bytes 655392 | tf_op jit(solution)/shard_map/ppermute | solution.py:36
  26.1 1.5 collective-permute-start.6
  28.3 1.3 collective-permute-start.8
  29.8 11.8 %collective-permute-done.6.rest_12_ = bf16[256,1280]{1,0:T(8,128)(2,1)S(1)} collective-permute-done((bf16[256,1280]{1,0:T(8,128)(2,1)}, bf16[256,1280]{1,0:T(8,128)(2,1)S(1)}, u32[]{:S(2)}, u32[]{:S(2)}) %collective-permute-start.6) | collective-permute-done | bytes 655392 | tf_op jit(solution)/shard_map/ppermute | solution.py:36
  42.5 1.5 collective-permute-start.13
  43.9 3.6 %collective-permute-done.8 = bf16[256,1280]{1,0:T(8,128)(2,1)S(1)} collective-permute-done((bf16[256,1280]{1,0:T(8,128)(2,1)}, bf16[256,1280]{1,0:T(8,128)(2,1)S(1)}, u32[]{:S(2)}, u32[]{:S(2)}) %collective-permute-start.8) | collective-permute-done | bytes 655392 | tf_op jit(solution)/shard_map/ppermute | solution.py:54
  48.3 1.3 collective-permute-start.10
  49.7 7.8 %collective-permute-done.13 = bf16[1024,256]{1,0:T(8,128)(2,1)S(1)} collective-permute-done((bf16[1024,256]{1,0:T(8,128)(2,1)}, bf16[1024,256]{1,0:T(8,128)(2,1)S(1)}, u32[]{:S(2)}, u32[]{:S(2)}) %collective-permute-start.13) | collective-permute-done | bytes 524320 | tf_op jit(solution)/shard_map/ppermute | solution.py:36
  58.6 3.0 %collective-permute-start.14 = (bf16[1280,256]{1,0:T(8,128)(2,1)}, bf16[1280,256]{1,0:T(8,128)(2,1)}, u32[]{:S(2)}, u32[]{:S(2)}) collective-permute-start(bf16[1280,256]{1,0:T(8,128)(2,1)} %pad_maximum_fusion.2.rest_0_), channel_id=1, source_target_pairs={{0,8},{4,12},{8,0},{12,4},{16,24},{20,28},{24,16},{28,20},{1,9},{5... | collective-permute-start | bytes 1966088 | tf_op jit(solution)/shard_map/ppermute | solution.py:54
  61.6 6.6 %collective-permute-done.9.rest_13_ = bf16[256,1280]{1,0:T(8,128)(2,1)S(1)} collective-permute-done((bf16[256,1280]{1,0:T(8,128)(2,1)S(1)}, bf16[256,1280]{1,0:T(8,128)(2,1)S(1)}, u32[]{:S(2)}, u32[]{:S(2)}) %collective-permute-start.9) | collective-permute-done | bytes 655392 | tf_op jit(solution)/shard_map/ppermute | solution.py:36
  69.1 1.5 collective-permute-start.15
  71.6 1.5 collective-permute-start.11
  73.8 1.9 fusion.19
  76.8 1.4 collective-permute-done.14.rest_1_
  78.1 7.2 %collective-permute-done.11.rest_14_ = bf16[256,1280]{1,0:T(8,128)(2,1)} collective-permute-done((bf16[256,1280]{1,0:T(8,128)(2,1)}, bf16[256,1280]{1,0:T(8,128)(2,1)}, u32[]{:S(2)}, u32[]{:S(2)}) %collective-permute-start.11) | collective-permute-done | bytes 655392 | tf_op jit(solution)/shard_map/ppermute | solution.py:36
  85.4 4.5 %shard_map.168.own = bf16[2,1024,128]{2,1,0:T(8,128)(2,1)S(1)} custom-call(s32[14]{0:T(128)S(1)} %concatenate.44.meta, bf16[256,2048]{1,0:T(8,128)(2,1)} %fusion.10.rest_0_, bf16[256,2048]{1,0:T(8,128)(2,1)} %collective-permute-done.3.rest_1_, bf16[256,2048]{1,0:T(8,128)(2,1)} %collective-permute-done.4.rest_2_, ...), custom_call_target="tpu_custom_call" | custom-call | flops 4294967296 | bytes 4194304 | tf_op jit(solution)/shard_map/pallas_call | solution.py:226
  89.9 1.6 collective-permute-start.12
  93.8 1.3 collective-permute-start.18
  95.0 11.7 %shard_map.169.rest_0_ = bf16[8,1024,128]{2,1,0:T(8,128)(2,1)S(1)} custom-call(s32[14]{0:T(128)S(1)} %concatenate.44.meta, bf16[256,2048]{1,0:T(8,128)(2,1)} %fusion.10.rest_0_, bf16[256,2048]{1,0:T(8,128)(2,1)} %collective-permute-done.3.rest_1_, bf16[256,2048]{1,0:T(8,128)(2,1)} %collective-permute-done.4.rest_2_, ...), custom_call_target="tpu_custom_call" | custom-call | flops 17179869184 | bytes 4194304 | tf_op jit(solution)/shard_map/pallas_call | solution.py:226
  106.7 2.0 collective-permute-done.16.rest_5_
  108.7 1.9 collective-permute-done.18
  110.7 1.6 collective-permute-start.19
  112.3 1.5 collective-permute-start.20
  113.8 12.0 %shard_map.171.rows = bf16[512,1024]{1,0:T(8,128)(2,1)S(1)} custom-call(s32[6]{0:T(128)S(1)} %pad_add_fusion.1.meta, bf16[2,1024,128]{2,1,0:T(8,128)(2,1)S(1)} %shard_map.168.own, bf16[2,1024,128]{2,1,0:T(8,128)(2,1)S(1)} %collective-permute-done.12.far, bf16[8,1024,128]{2,1,0:T(8,128)(2,1)S(1)} %shard_map.169.rest_0_), custom_call_target="tpu_custom_call" | custom-call | flops 8589934592 | bytes 524288 | tf_op jit(solution)/shard_map/pallas_call | solution.py:326
  126.6 3.8 %shard_map.170.rows = bf16[512,1024]{1,0:T(8,128)(2,1)S(1)} custom-call(s32[6]{0:T(128)S(1)} %pad_add_fusion.1.meta, bf16[2,1024,128]{2,1,0:T(8,128)(2,1)S(1)} %shard_map.168.own, bf16[2,1024,128]{2,1,0:T(8,128)(2,1)S(1)} %collective-permute-done.12.far, bf16[8,1024,128]{2,1,0:T(8,128)(2,1)S(1)} %shard_map.169.rest_0_), custom_call_target="tpu_custom_call" | custom-call | flops 8589934592 | bytes 524288 | tf_op jit(solution)/shard_map/pallas_call | solution.py:326
  130.4 3.5 %collective-permute-done.21.rest_7_ = bf16[768,256]{1,0:T(8,128)(2,1)S(1)} collective-permute-done((bf16[768,256]{1,0:T(8,128)(2,1)S(1)}, bf16[768,256]{1,0:T(8,128)(2,1)S(1)}, u32[]{:S(2)}, u32[]{:S(2)}) %collective-permute-start.21) | collective-permute-done | bytes 393248 | tf_op jit(solution)/shard_map/ppermute | solution.py:36
  133.9 4.2 %shard_map.173 = (bf16[1,256,2048]{2,1,0:T(8,128)(2,1)S(1)}, bf16[1,256,2048]{2,1,0:T(8,128)(2,1)S(1)}) custom-call(s32[8]{0:T(128)S(1)} %pad_add_fusion.meta, bf16[512,1024]{1,0:T(8,128)(2,1)S(1)} %shard_map.171.rows, bf16[1280,256]{1,0:T(8,128)(2,1)} %pad_maximum_fusion.2.rest_0_, bf16[1280,256]{1,0:T(8,128)(2,1)} %collective-permute-done.14.rest_1_, ...), custom_call_target="tpu_custom_call" | custom-call | tf_op jit(solution)/shard_map/pallas_call | solution.py:371
  138.1 5.1 %shard_map.172 = (bf16[1,256,2048]{2,1,0:T(8,128)(2,1)S(1)}, bf16[1,256,2048]{2,1,0:T(8,128)(2,1)}) custom-call(s32[8]{0:T(128)S(1)} %pad_add_fusion.meta, bf16[512,1024]{1,0:T(8,128)(2,1)S(1)} %shard_map.170.rows, bf16[1280,256]{1,0:T(8,128)(2,1)} %pad_maximum_fusion.2.rest_0_, bf16[1280,256]{1,0:T(8,128)(2,1)} %collective-permute-done.14.rest_1_, ...), custom_call_target="tpu_custom_call" | custom-call | tf_op jit(solution)/shard_map/pallas_call | solution.py:371
  143.8 1.4 add_convert_fusion
  145.1 6.3 %collective-permute-start.24 = (bf16[1,256,2048]{2,1,0:T(8,128)(2,1)}, bf16[1,256,2048]{2,1,0:T(8,128)(2,1)}, u32[]{:S(2)}, u32[]{:S(2)}) collective-permute-start(bf16[1,256,2048]{2,1,0:T(8,128)(2,1)} %add_convert_fusion), channel_id=1, source_target_pairs={{0,2},{1,3},{2,0},{3,1},{4,6},{5,7},{6,4},{7,5},{8,10},{9,11},{10,... | collective-permute-start | bytes 3145736 | tf_op jit(solution)/shard_map/ppermute | solution.py:36
  153.6 21.5 %collective-permute-done.24 = bf16[1,256,2048]{2,1,0:T(8,128)(2,1)} collective-permute-done((bf16[1,256,2048]{2,1,0:T(8,128)(2,1)}, bf16[1,256,2048]{2,1,0:T(8,128)(2,1)}, u32[]{:S(2)}, u32[]{:S(2)}) %collective-permute-start.24) | collective-permute-done | bytes 1048608 | tf_op jit(solution)/shard_map/ppermute | solution.py:36
  177.5 3.8 %shard_map.174 = (bf16[256,2048]{1,0:T(8,128)(2,1)}, bf16[256,2048]{1,0:T(8,128)(2,1)S(1)}) custom-call(bf16[256,2048]{1,0:T(8,128)(2,1)S(1)} %copy-done.2, f32[1,2048]{1,0:T(1,128)S(1)} %bitcast.54, bf16[256,2048]{1,0:T(8,128)(2,1)S(1)} %bitcast.53, bf16[256,2048]{1,0:T(8,128)(2,1)} %bitcast.7.rest_1_, bf16[256,2048]{1,0:T(8,128)(2,1)} %bitcast.8.rest_2_), custom_call_target="tpu_custom_call" | custom-call | tf_op jit(solution)/shard_map/pallas_call | solution.py:399
  182.5 1.3 collective-permute-start.26
  184.5 5.7 %collective-permute-done.27 = bf16[64,2048]{1,0:T(8,128)(2,1)S(1)} collective-permute-done((bf16[64,2048]{1,0:T(8,128)(2,1)S(1)}, bf16[64,2048]{1,0:T(8,128)(2,1)S(1)}, u32[]{:S(2)}, u32[]{:S(2)}) %collective-permute-start.27) | collective-permute-done | bytes 262176 | tf_op jit(solution)/shard_map/ppermute | solution.py:36
  190.2 5.9 %collective-permute-done.25 = bf16[64,2048]{1,0:T(8,128)(2,1)S(1)} collective-permute-done((bf16[64,2048]{1,0:T(8,128)(2,1)S(1)}, bf16[64,2048]{1,0:T(8,128)(2,1)S(1)}, u32[]{:S(2)}, u32[]{:S(2)}) %collective-permute-start.25) | collective-permute-done | bytes 262176 | tf_op jit(solution)/shard_map/ppermute | solution.py:36
  196.3 4.6 %fusion = f32[256,1536]{1,0:T(8,128)S(1)} fusion(bf16[256,2048]{1,0:T(8,128)(2,1)S(1)} %bitcast.56, bf16[1,2048,1536]{2,1,0:T(8,128)(2,1)} %param.26), kind=kOutput, calls=%fused_computation | convolution fusion | flops 1610612736 | bytes 8912896 | tf_op jit(solution)/shard_map/dot_general | solution.py:543
  202.7 1.5 collective-permute-start.28
  205.4 5.3 %collective-permute-done.30 = bf16[64,2048]{1,0:T(8,128)(2,1)S(1)} collective-permute-done((bf16[64,2048]{1,0:T(8,128)(2,1)S(1)}, bf16[64,2048]{1,0:T(8,128)(2,1)S(1)}, u32[]{:S(2)}, u32[]{:S(2)}) %collective-permute-start.30) | collective-permute-done | bytes 262176 | tf_op jit(solution)/shard_map/ppermute | solution.py:36
  210.7 5.6 %collective-permute-done.28 = bf16[64,2048]{1,0:T(8,128)(2,1)S(1)} collective-permute-done((bf16[64,2048]{1,0:T(8,128)(2,1)S(1)}, bf16[64,2048]{1,0:T(8,128)(2,1)S(1)}, u32[]{:S(2)}, u32[]{:S(2)}) %collective-permute-start.28) | collective-permute-done | bytes 262176 | tf_op jit(solution)/shard_map/ppermute | solution.py:36
  216.4 1.5 fusion.4
  (138 shorter events, 24.6 us)
Async XLA Ops:
  0.6 200.3 %copy-start = (bf16[1,768,2048]{2,1,0:T(8,128)(2,1)S(1)}, bf16[1,768,2048]{2,1,0:T(8,128)(2,1)}, u32[]{:S(2)}) copy-start(bf16[1,768,2048]{2,1,0:T(8,128)(2,1)} %param.27) | copy-start | bytes 9437188
  0.6 10.8 %copy-start.18 = (f32[2048]{0:T(1024)S(1)}, f32[2048]{0:T(1024)}, u32[]{:S(2)}) copy-start(f32[2048]{0:T(1024)} %param.17) | copy-start | bytes 24580
  0.7 10.4 %copy-start.1 = (bf16[256,2048]{1,0:T(8,128)(2,1)S(1)}, bf16[256,2048]{1,0:T(8,128)(2,1)}, u32[]{:S(2)}) copy-start(bf16[256,2048]{1,0:T(8,128)(2,1)} %states.1) | copy-start | bytes 3145732
  5.1 9.2 %copy-start.24 = (s32[4]{0:T(128)S(1)}, s32[4]{0:T(128)}, u32[]{:S(2)}) copy-start(s32[4]{0:T(128)} %constant.109.clone) | copy-start | bytes 52
  5.1 18.1 %collective-permute-start = (bf16[256,1280]{1,0:T(8,128)(2,1)}, bf16[256,1280]{1,0:T(8,128)(2,1)}, u32[]{:S(2)}, u32[]{:S(2)}) collective-permute-start(bf16[256,1280]{1,0:T(8,128)(2,1)} %shard_map.167.rest_7_), channel_id=1, source_target_pairs={{0,8},{4,12},{8,0},{12,4},{16,24},{20,28},{24,16},{28,20},{1,9},{5... | collective-permute-start | bytes 1966088 | tf_op jit(solution)/shard_map/ppermute | solution.py:54
  8.1 15.0 %collective-permute-start.1 = (bf16[256,1280]{1,0:T(8,128)(2,1)}, bf16[256,1280]{1,0:T(8,128)(2,1)}, u32[]{:S(2)}, u32[]{:S(2)}) collective-permute-start(bf16[256,1280]{1,0:T(8,128)(2,1)} %shard_map.167.rest_7_), channel_id=1, source_target_pairs={{8,16},{12,20},{16,8},{20,12},{9,17},{13,21},{17,9},{21,13},{10,18... | collective-permute-start | bytes 1966088 | tf_op jit(solution)/shard_map/ppermute | solution.py:54
  9.6 16.5 %collective-permute-start.2 = (bf16[256,1280]{1,0:T(8,128)(2,1)}, bf16[256,1280]{1,0:T(8,128)(2,1)}, u32[]{:S(2)}, u32[]{:S(2)}) collective-permute-start(bf16[256,1280]{1,0:T(8,128)(2,1)} %shard_map.167.rest_7_), channel_id=1, source_target_pairs={{0,4},{4,0},{8,12},{12,8},{16,20},{20,16},{24,28},{28,24},{1,5},{5... | collective-permute-start | bytes 1966088 | tf_op jit(solution)/shard_map/ppermute | solution.py:36
  11.4 5.0 %copy-start.21 = (s32[4,4]{1,0:T(4,128)S(1)}, s32[4,4]{1,0:T(4,128)}, u32[]{:S(2)}) copy-start(s32[4,4]{1,0:T(4,128)} %constant.110.clone) | copy-start | bytes 196
  11.4 5.3 %copy-start.22 = (s32[4]{0:T(128)S(1)}, s32[4]{0:T(128)}, u32[]{:S(2)}) copy-start(s32[4]{0:T(128)} %param.24) | copy-start | bytes 52
  11.4 5.9 %copy-start.20 = (f32[128]{0:T(128)S(1)}, f32[128]{0:T(128)}, u32[]{:S(2)}) copy-start(f32[128]{0:T(128)} %param.23) | copy-start | bytes 1540
  11.4 18.3 %copy-start.23 = (f32[128]{0:T(128)S(1)}, f32[128]{0:T(128)}, u32[]{:S(2)}) copy-start(f32[128]{0:T(128)} %param.22) | copy-start | bytes 1540
  12.7 36.9 %collective-permute-start.3 = (bf16[256,2048]{1,0:T(8,128)(2,1)}, bf16[256,2048]{1,0:T(8,128)(2,1)}, u32[]{:S(2)}, u32[]{:S(2)}) collective-permute-start(bf16[256,2048]{1,0:T(8,128)(2,1)} %fusion.10.rest_0_), channel_id=1, source_target_pairs={{0,2},{1,3},{2,0},{3,1},{4,6},{5,7},{6,4},{7,5},{8,10},{9,11},{10,... | collective-permute-start | bytes 3145736 | tf_op jit(solution)/shard_map/ppermute | solution.py:36
  14.2 71.1 %collective-permute-start.4 = (bf16[256,2048]{1,0:T(8,128)(2,1)}, bf16[256,2048]{1,0:T(8,128)(2,1)}, u32[]{:S(2)}, u32[]{:S(2)}) collective-permute-start(bf16[256,2048]{1,0:T(8,128)(2,1)} %fusion.10.rest_0_), channel_id=1, source_target_pairs={{0,1},{1,0},{2,3},{3,2},{4,5},{5,4},{6,7},{7,6},{8,9},{9,8},{10,11... | collective-permute-start | bytes 3145736 | tf_op jit(solution)/shard_map/ppermute | solution.py:36
  16.6 40.9 %copy-start.14 = (bf16[1024,256]{1,0:T(8,128)(2,1)S(1)}, bf16[1024,256]{1,0:T(8,128)(2,1)}, u32[]{:S(2)}) copy-start(bf16[1024,256]{1,0:T(8,128)(2,1)} %convert_element_type.56) | copy-start | bytes 1572868
  26.1 15.5 %collective-permute-start.6 = (bf16[256,1280]{1,0:T(8,128)(2,1)}, bf16[256,1280]{1,0:T(8,128)(2,1)S(1)}, u32[]{:S(2)}, u32[]{:S(2)}) collective-permute-start(bf16[256,1280]{1,0:T(8,128)(2,1)} %collective-permute-done.rest_8_), channel_id=1, source_target_pairs={{0,4},{4,0},{8,12},{12,8},{16,20},{20,16},{24,28},{28,24},{1,5},{5... | collective-permute-start | bytes 1966088 | tf_op jit(solution)/shard_map/ppermute | solution.py:36
  27.6 16.4 %collective-permute-start.7 = (bf16[256,1280]{1,0:T(8,128)(2,1)}, bf16[256,1280]{1,0:T(8,128)(2,1)S(1)}, u32[]{:S(2)}, u32[]{:S(2)}) collective-permute-start(bf16[256,1280]{1,0:T(8,128)(2,1)} %collective-permute-done.rest_8_), channel_id=1, source_target_pairs={{8,16},{12,20},{16,8},{20,12},{9,17},{13,21},{17,9},{21,13},{10,18... | collective-permute-start | bytes 1966088 | tf_op jit(solution)/shard_map/ppermute | solution.py:54
  28.3 19.3 %collective-permute-start.8 = (bf16[256,1280]{1,0:T(8,128)(2,1)}, bf16[256,1280]{1,0:T(8,128)(2,1)S(1)}, u32[]{:S(2)}, u32[]{:S(2)}) collective-permute-start(bf16[256,1280]{1,0:T(8,128)(2,1)} %collective-permute-done.1), channel_id=1, source_target_pairs={{8,0},{12,4},{16,24},{20,28},{9,1},{13,5},{17,25},{21,29},{10,2},{... | collective-permute-start | bytes 1966088 | tf_op jit(solution)/shard_map/ppermute | solution.py:54
  42.5 15.1 %collective-permute-start.13 = (bf16[1024,256]{1,0:T(8,128)(2,1)}, bf16[1024,256]{1,0:T(8,128)(2,1)S(1)}, u32[]{:S(2)}, u32[]{:S(2)}) collective-permute-start(bf16[1024,256]{1,0:T(8,128)(2,1)} %convert_element_type.56), channel_id=1, source_target_pairs={{0,4},{4,0},{8,12},{12,8},{16,20},{20,16},{24,28},{28,24},{1,5},{5... | collective-permute-start | bytes 1572872 | tf_op jit(solution)/shard_map/ppermute | solution.py:36
  47.7 23.9 %copy-start.7 = (bf16[256,1280]{1,0:T(8,128)(2,1)}, bf16[256,1280]{1,0:T(8,128)(2,1)S(1)}, u32[]{:S(2)}) copy-start(bf16[256,1280]{1,0:T(8,128)(2,1)S(1)} %broadcast_select_fusion.3.rest_9_) | copy-start | bytes 1966084
  47.7 20.6 %collective-permute-start.9 = (bf16[256,1280]{1,0:T(8,128)(2,1)S(1)}, bf16[256,1280]{1,0:T(8,128)(2,1)S(1)}, u32[]{:S(2)}, u32[]{:S(2)}) collective-permute-start(bf16[256,1280]{1,0:T(8,128)(2,1)S(1)} %broadcast_select_fusion.3.rest_9_), channel_id=1, source_target_pairs={{0,4},{4,0},{8,12},{12,8},{16,20},{20,16},{24,28},{28,24},{1,5},{5... | collective-permute-start | bytes 1966088 | tf_op jit(solution)/shard_map/ppermute | solution.py:36
  48.3 22.3 %collective-permute-start.10 = (bf16[256,1280]{1,0:T(8,128)(2,1)S(1)}, bf16[256,1280]{1,0:T(8,128)(2,1)S(1)}, u32[]{:S(2)}, u32[]{:S(2)}) collective-permute-start(bf16[256,1280]{1,0:T(8,128)(2,1)S(1)} %collective-permute-done.7), channel_id=1, source_target_pairs={{8,0},{12,4},{16,24},{20,28},{9,1},{13,5},{17,25},{21,29},{10,2},{... | collective-permute-start | bytes 1966088 | tf_op jit(solution)/shard_map/ppermute | solution.py:54
  49.7 35.7 %collective-permute-start.5 = (bf16[256,2048]{1,0:T(8,128)(2,1)}, bf16[256,2048]{1,0:T(8,128)(2,1)}, u32[]{:S(2)}, u32[]{:S(2)}) collective-permute-start(bf16[256,2048]{1,0:T(8,128)(2,1)} %collective-permute-done.3.rest_1_), channel_id=1, source_target_pairs={{0,1},{1,0},{2,3},{3,2},{4,5},{5,4},{6,7},{7,6},{8,9},{9,8},{10,11... | collective-permute-start | bytes 3145736 | tf_op jit(solution)/shard_map/ppermute | solution.py:36
  57.5 14.1 %copy-start.15 = (bf16[1024,256]{1,0:T(8,128)(2,1)}, bf16[1024,256]{1,0:T(8,128)(2,1)S(1)}, u32[]{:S(2)}) copy-start(bf16[1024,256]{1,0:T(8,128)(2,1)S(1)} %collective-permute-done.13) | copy-start | bytes 1572868
  58.6 19.5 %collective-permute-start.14 = (bf16[1280,256]{1,0:T(8,128)(2,1)}, bf16[1280,256]{1,0:T(8,128)(2,1)}, u32[]{:S(2)}, u32[]{:S(2)}) collective-permute-start(bf16[1280,256]{1,0:T(8,128)(2,1)} %pad_maximum_fusion.2.rest_0_), channel_id=1, source_target_pairs={{0,8},{4,12},{8,0},{12,4},{16,24},{20,28},{24,16},{28,20},{1,9},{5... | collective-permute-start | bytes 1966088 | tf_op jit(solution)/shard_map/ppermute | solution.py:54
  69.1 9.0 %collective-permute-start.15 = (bf16[1280,256]{1,0:T(8,128)(2,1)}, bf16[1280,256]{1,0:T(8,128)(2,1)}, u32[]{:S(2)}, u32[]{:S(2)}) collective-permute-start(bf16[1280,256]{1,0:T(8,128)(2,1)} %pad_maximum_fusion.2.rest_0_), channel_id=1, source_target_pairs={{8,16},{12,20},{16,8},{20,12},{9,17},{13,21},{17,9},{21,13},{10,18... | collective-permute-start | bytes 1966088 | tf_op jit(solution)/shard_map/ppermute | solution.py:54
  71.6 13.8 %collective-permute-start.11 = (bf16[256,1280]{1,0:T(8,128)(2,1)}, bf16[256,1280]{1,0:T(8,128)(2,1)}, u32[]{:S(2)}, u32[]{:S(2)}) collective-permute-start(bf16[256,1280]{1,0:T(8,128)(2,1)} %broadcast_select_fusion.2.rest_10_), channel_id=1, source_target_pairs={{0,4},{4,0},{8,12},{12,8},{16,20},{20,16},{24,28},{28,24},{1,5},{5... | collective-permute-start | bytes 1966088 | tf_op jit(solution)/shard_map/ppermute | solution.py:36
  75.7 9.7 %copy-start.8 = (bf16[256,1280]{1,0:T(8,128)(2,1)S(1)}, bf16[256,1280]{1,0:T(8,128)(2,1)}, u32[]{:S(2)}) copy-start(bf16[256,1280]{1,0:T(8,128)(2,1)} %copy-done.7) | copy-start | bytes 1966084
  75.7 9.7 %copy-start.11 = (bf16[256,1280]{1,0:T(8,128)(2,1)S(1)}, bf16[256,1280]{1,0:T(8,128)(2,1)}, u32[]{:S(2)}) copy-start(bf16[256,1280]{1,0:T(8,128)(2,1)} %copy-done.10) | copy-start | bytes 1966084
  75.7 9.7 %copy-start.13 = (bf16[256,1280]{1,0:T(8,128)(2,1)S(1)}, bf16[256,1280]{1,0:T(8,128)(2,1)}, u32[]{:S(2)}) copy-start(bf16[256,1280]{1,0:T(8,128)(2,1)} %copy-done.12) | copy-start | bytes 1966084
  89.9 20.8 %collective-permute-start.12 = (bf16[2,1024,128]{2,1,0:T(8,128)(2,1)S(1)}, bf16[2,1024,128]{2,1,0:T(8,128)(2,1)S(1)}, u32[]{:S(2)}, u32[]{:S(2)}) collective-permute-start(bf16[2,1024,128]{2,1,0:T(8,128)(2,1)S(1)} %shard_map.168.own), channel_id=1, source_target_pairs={{0,4},{4,0},{8,12},{12,8},{16,20},{20,16},{24,28},{28,24},{1,5},{5... | collective-permute-start | bytes 1572872 | tf_op jit(solution)/shard_map/ppermute | solution.py:36
  92.4 16.3 %collective-permute-start.17 = (bf16[1280,256]{1,0:T(8,128)(2,1)}, bf16[1280,256]{1,0:T(8,128)(2,1)S(1)}, u32[]{:S(2)}, u32[]{:S(2)}) collective-permute-start(bf16[1280,256]{1,0:T(8,128)(2,1)} %collective-permute-done.14.rest_1_), channel_id=1, source_target_pairs={{8,16},{12,20},{16,8},{20,12},{9,17},{13,21},{17,9},{21,13},{10,18... | collective-permute-start | bytes 1966088 | tf_op jit(solution)/shard_map/ppermute | solution.py:54
  93.2 15.6 %collective-permute-start.16 = (bf16[768,256]{1,0:T(8,128)(2,1)S(1)}, bf16[768,256]{1,0:T(8,128)(2,1)S(1)}, u32[]{:S(2)}, u32[]{:S(2)}) collective-permute-start(bf16[768,256]{1,0:T(8,128)(2,1)S(1)} %slice.90), channel_id=1, source_target_pairs={{0,4},{4,0},{8,12},{12,8},{16,20},{20,16},{24,28},{28,24},{1,5},{5... | collective-permute-start | bytes 1179656 | tf_op jit(solution)/shard_map/ppermute | solution.py:36
  93.8 16.9 %collective-permute-start.18 = (bf16[1280,256]{1,0:T(8,128)(2,1)}, bf16[1280,256]{1,0:T(8,128)(2,1)S(1)}, u32[]{:S(2)}, u32[]{:S(2)}) collective-permute-start(bf16[1280,256]{1,0:T(8,128)(2,1)} %collective-permute-done.15), channel_id=1, source_target_pairs={{8,0},{12,4},{16,24},{20,28},{9,1},{13,5},{17,25},{21,29},{10,2},{... | collective-permute-start | bytes 1966088 | tf_op jit(solution)/shard_map/ppermute | solution.py:54
  110.7 15.0 %collective-permute-start.19 = (bf16[768,256]{1,0:T(8,128)(2,1)S(1)}, bf16[768,256]{1,0:T(8,128)(2,1)S(1)}, u32[]{:S(2)}, u32[]{:S(2)}) collective-permute-start(bf16[768,256]{1,0:T(8,128)(2,1)S(1)} %slice.108), channel_id=1, source_target_pairs={{0,4},{4,0},{8,12},{12,8},{16,20},{20,16},{24,28},{28,24},{1,5},{5... | collective-permute-start | bytes 1179656 | tf_op jit(solution)/shard_map/ppermute | solution.py:36
  112.3 13.6 %collective-permute-start.20 = (bf16[1280,256]{1,0:T(8,128)(2,1)S(1)}, bf16[1280,256]{1,0:T(8,128)(2,1)S(1)}, u32[]{:S(2)}, u32[]{:S(2)}) collective-permute-start(bf16[1280,256]{1,0:T(8,128)(2,1)S(1)} %collective-permute-done.17), channel_id=1, source_target_pairs={{8,0},{12,4},{16,24},{20,28},{9,1},{13,5},{17,25},{21,29},{10,2},{... | collective-permute-start | bytes 1966088 | tf_op jit(solution)/shard_map/ppermute | solution.py:54
  126.0 7.8 %collective-permute-start.21 = (bf16[768,256]{1,0:T(8,128)(2,1)S(1)}, bf16[768,256]{1,0:T(8,128)(2,1)S(1)}, u32[]{:S(2)}, u32[]{:S(2)}) collective-permute-start(bf16[768,256]{1,0:T(8,128)(2,1)S(1)} %slice.109), channel_id=1, source_target_pairs={{0,4},{4,0},{8,12},{12,8},{16,20},{20,16},{24,28},{28,24},{1,5},{5... | collective-permute-start | bytes 1179656 | tf_op jit(solution)/shard_map/ppermute | solution.py:36
  138.0 5.7 %collective-permute-start.23 = (bf16[1,256,2048]{2,1,0:T(8,128)(2,1)S(1)}, bf16[1,256,2048]{2,1,0:T(8,128)(2,1)S(1)}, u32[]{:S(2)}, u32[]{:S(2)}) collective-permute-start(bf16[1,256,2048]{2,1,0:T(8,128)(2,1)S(1)} %get-tuple-element.82), channel_id=1, source_target_pairs={{0,1},{1,0},{2,3},{3,2},{4,5},{5,4},{6,7},{7,6},{8,9},{9,8},{10,11... | collective-permute-start | bytes 3145736 | tf_op jit(solution)/shard_map/ppermute | solution.py:36
  143.3 8.2 %copy-start.19 = (s32[256,8]{0,1:T(8,128)S(1)}, s32[256,8]{0,1:T(8,128)}, u32[]{:S(2)}) copy-start(s32[256,8]{0,1:T(8,128)} %param.28) | copy-start | bytes 24580
  143.3 31.8 %copy-start.9 = (f32[2048]{0:T(1024)S(1)}, f32[2048]{0:T(1024)}, u32[]{:S(2)}) copy-start(f32[2048]{0:T(1024)} %param.18) | copy-start | bytes 24580
  143.3 10.3 %collective-permute-start.22 = (bf16[1,256,2048]{2,1,0:T(8,128)(2,1)}, bf16[1,256,2048]{2,1,0:T(8,128)(2,1)}, u32[]{:S(2)}, u32[]{:S(2)}) collective-permute-start(bf16[1,256,2048]{2,1,0:T(8,128)(2,1)} %get-tuple-element.79), channel_id=1, source_target_pairs={{0,1},{1,0},{2,3},{3,2},{4,5},{5,4},{6,7},{7,6},{8,9},{9,8},{10,11... | collective-permute-start | bytes 3145736 | tf_op jit(solution)/shard_map/ppermute | solution.py:36
  145.1 29.9 %collective-permute-start.24 = (bf16[1,256,2048]{2,1,0:T(8,128)(2,1)}, bf16[1,256,2048]{2,1,0:T(8,128)(2,1)}, u32[]{:S(2)}, u32[]{:S(2)}) collective-permute-start(bf16[1,256,2048]{2,1,0:T(8,128)(2,1)} %add_convert_fusion), channel_id=1, source_target_pairs={{0,2},{1,3},{2,0},{3,1},{4,6},{5,7},{6,4},{7,5},{8,10},{9,11},{10,... | collective-permute-start | bytes 3145736 | tf_op jit(solution)/shard_map/ppermute | solution.py:36
  181.3 2.7 %copy-start.17 = (bf16[2048,128]{1,0:T(8,128)(2,1)S(1)}, bf16[2048,128]{1,0:T(8,128)(2,1)}, u32[]{:S(2)}) copy-start(bf16[2048,128]{1,0:T(8,128)(2,1)} %param.25) | copy-start | bytes 1572868
  181.9 8.4 %collective-permute-start.27 = (bf16[64,2048]{1,0:T(8,128)(2,1)S(1)}, bf16[64,2048]{1,0:T(8,128)(2,1)S(1)}, u32[]{:S(2)}, u32[]{:S(2)}) collective-permute-start(bf16[64,2048]{1,0:T(8,128)(2,1)S(1)} %get-tuple-element.91), channel_id=1, source_target_pairs={{0,3},{1,2},{2,1},{3,0},{4,7},{5,6},{6,5},{7,4},{8,11},{9,10},{10,... | collective-permute-start | bytes 786440 | tf_op jit(solution)/shard_map/ppermute | solution.py:36
  182.5 7.8 %collective-permute-start.26 = (bf16[64,2048]{1,0:T(8,128)(2,1)S(1)}, bf16[64,2048]{1,0:T(8,128)(2,1)S(1)}, u32[]{:S(2)}, u32[]{:S(2)}) collective-permute-start(bf16[64,2048]{1,0:T(8,128)(2,1)S(1)} %get-tuple-element.92), channel_id=1, source_target_pairs={{0,1},{1,0},{2,3},{3,2},{4,5},{5,4},{6,7},{7,6},{8,9},{9,8},{10,11... | collective-permute-start | bytes 786440 | tf_op jit(solution)/shard_map/ppermute | solution.py:36
  183.8 12.4 %collective-permute-start.25 = (bf16[64,2048]{1,0:T(8,128)(2,1)S(1)}, bf16[64,2048]{1,0:T(8,128)(2,1)S(1)}, u32[]{:S(2)}, u32[]{:S(2)}) collective-permute-start(bf16[64,2048]{1,0:T(8,128)(2,1)S(1)} %get-tuple-element.93), channel_id=1, source_target_pairs={{0,2},{1,3},{2,0},{3,1},{4,6},{5,7},{6,4},{7,5},{8,10},{9,11},{10,... | collective-permute-start | bytes 786440 | tf_op jit(solution)/shard_map/ppermute | solution.py:36
  202.0 8.7 %collective-permute-start.30 = (bf16[64,2048]{1,0:T(8,128)(2,1)S(1)}, bf16[64,2048]{1,0:T(8,128)(2,1)S(1)}, u32[]{:S(2)}, u32[]{:S(2)}) collective-permute-start(bf16[64,2048]{1,0:T(8,128)(2,1)S(1)} %get-tuple-element.87), channel_id=1, source_target_pairs={{0,3},{1,2},{2,1},{3,0},{4,7},{5,6},{6,5},{7,4},{8,11},{9,10},{10,... | collective-permute-start | bytes 786440 | tf_op jit(solution)/shard_map/ppermute | solution.py:36
  202.6 8.1 %collective-permute-start.29 = (bf16[64,2048]{1,0:T(8,128)(2,1)S(1)}, bf16[64,2048]{1,0:T(8,128)(2,1)S(1)}, u32[]{:S(2)}, u32[]{:S(2)}) collective-permute-start(bf16[64,2048]{1,0:T(8,128)(2,1)S(1)} %get-tuple-element.88), channel_id=1, source_target_pairs={{0,1},{1,0},{2,3},{3,2},{4,5},{5,4},{6,7},{7,6},{8,9},{9,8},{10,11... | collective-permute-start | bytes 786440 | tf_op jit(solution)/shard_map/ppermute | solution.py:36
  202.7 13.6 %collective-permute-start.28 = (bf16[64,2048]{1,0:T(8,128)(2,1)S(1)}, bf16[64,2048]{1,0:T(8,128)(2,1)S(1)}, u32[]{:S(2)}, u32[]{:S(2)}) collective-permute-start(bf16[64,2048]{1,0:T(8,128)(2,1)S(1)} %get-tuple-element.89), channel_id=1, source_target_pairs={{0,2},{1,3},{2,0},{3,1},{4,6},{5,7},{6,4},{7,5},{8,10},{9,11},{10,... | collective-permute-start | bytes 786440 | tf_op jit(solution)/shard_map/ppermute | solution.py:36
  (8 other events, 10.0 us)

commit v5 on v4

--- a/solution.py
+++ b/solution.py
@@ -320,7 +320,7 @@
     steps = row_count // tile // 2
 
     def block_of(step):
-        return step + steps // 2 * (part + (step >= steps // 2))
+        return step + (steps // 2 if part else steps * (step >= steps // 2))
 
     whole = pl.BlockSpec((2, row_count, dim), lambda i, meta: (0, 0, 0))
     return pl.pallas_call(
@@ -345,23 +345,22 @@
     )(meta, own, far, *queries)
 
 
-def output_kernel(plan, meta, rows, *rest):
+def output_kernel(plan, meta, kept_rows, sent_rows, *rest):
     *shards, kept, sent = rest
     columns = shards[0].shape[1]
-    half = rows.shape[0] // 2
     for index, pieces in enumerate(plan):
         here = pl.ds(pl.multiple_of(meta[index] * columns, columns), columns)
-        for part, out in enumerate((kept, sent)):
+        for rows, out in ((kept_rows, kept), (sent_rows, sent)):
             product = 0.0
             for shard, start, size, depth in pieces:
-                left = rows[part * half : (part + 1) * half, depth : depth + size]
+                left = rows[:, depth : depth + size]
                 right = shards[shard][start : start + size, :]
                 product += jnp.dot(left, right, preferred_element_type=jnp.float32)
             out[:, :, here] = product.astype(jnp.bfloat16).reshape(*out.shape[:2], columns)
 
 
-def output_part(plan, meta, rows, tile, shards):
-    count, depth = rows.shape
+def output_part(plan, meta, kept_rows, sent_rows, tile, shards):
+    count, depth = kept_rows.shape
     width = len(plan) * shards[0].shape[1]
 
     def whole(shape):
@@ -373,13 +372,14 @@
         grid_spec=pltpu.PrefetchScalarGridSpec(
             num_scalar_prefetch=1,
             grid=(1,),
-            in_specs=[whole((count, depth))] + [whole(shard.shape) for shard in shards],
+            in_specs=[pl.BlockSpec((count // 2, depth), lambda n, meta, half=half: (half, 0)) for half in range(2)]
+            + [whole(shard.shape) for shard in shards],
             out_specs=[whole(out)] * 2,
         ),
         out_shape=[jax.ShapeDtypeStruct(out, jnp.bfloat16)] * 2,
         compiler_params=pltpu.CompilerParams(vmem_limit_bytes=VMEM_LIMIT),
-        cost_estimate=FREE,
-    )(meta, rows, *shards)
+        cost_estimate=pl.CostEstimate(flops=6 * count * width * depth, bytes_accessed=4 * count * width, transcendentals=0),
+    )(meta, kept_rows, sent_rows, *shards)
 
 
 def finish_kernel(states, gain, *rest):
@@ -506,17 +506,16 @@
 
     valid_length = jnp.sum(jnp.where(jnp.arange(lengths.shape[0]) == group_index // 2, lengths, 0))
     attend_meta = jnp.concatenate([jnp.stack([parity, valid_length]), block_order]).astype(jnp.int32)
-    next_rows = attend(attend_meta, queries, own_pair, far_pair, rows_here, 1)
+    outer_rows = attend(attend_meta, queries, own_pair, far_pair, rows_here, 0)
     queries[0] = after(queries[0], output_rounds.token())
-    output_rounds.round(next_rows)
-    last_rows = attend(attend_meta, queries, own_pair, far_pair, rows_here, 0)
+    output_rounds.round(outer_rows)
+    inner_rows = attend(attend_meta, queries, own_pair, far_pair, rows_here, 1)
 
     output_shards = output_rounds.held(range(groups))
-    next_rows = after(next_rows, last_rows)
     output_meta = held_groups(place, side).astype(jnp.int32)
-    kept, sent = output_part(plan, output_meta, next_rows, rows_here, output_shards)
+    kept, sent = output_part(plan, output_meta, inner_rows, outer_rows, rows_here, output_shards)
     next_sum = sum_terms([kept, from_xor(sent, "expert", 1)])
-    kept, sent = output_part(plan, output_meta, last_rows, rows_here, output_shards)
+    kept, sent = output_part(plan, output_meta, outer_rows, inner_rows, rows_here, output_shards)
     terms = scatter_rest([kept, from_xor(sent, "expert", 1)], next_sum)
     hidden, normed_second = finish(hidden_in, norm_experts, terms)
 
@@ -532,24 +531,30 @@
         .reshape(experts_axis, capacity, model_width)
     )
 
-    def exchange(slots):
-        return jnp.stack([slots[0]] + [from_xor(slots[j], "expert", masks[j]) for j in range(1, experts_axis)])
-
     gateup_here = expert_gateup[0]
     down_here = expert_down[0]
     hidden_units = down_here.shape[0]
-    slot_items = exchange(outgoing)
-    flattened = slot_items.reshape(-1, slot_items.shape[-1])
-    gate_up = jnp.dot(flattened, gateup_here, preferred_element_type=jnp.float32)
-    active = (jax.nn.silu(gate_up[:, :hidden_units]) * gate_up[:, hidden_units:]).astype(
-        jnp.bfloat16
+
+    def expert(slots):
+        gate_up = jnp.dot(slots, gateup_here, preferred_element_type=jnp.float32)
+        active = (jax.nn.silu(gate_up[:, :hidden_units]) * gate_up[:, hidden_units:]).astype(jnp.bfloat16)
+        return jnp.dot(active, down_here, preferred_element_type=jnp.float32).astype(jnp.bfloat16)
+
+    far = [j for j in range(experts_axis) if masks[j] >= experts_axis // 2]
+    first, second = far[: len(far) // 2], far[len(far) // 2 :]
+    near = [j for j in range(1, experts_axis) if j not in far]
+    results = {}
+    arrived = {j: from_xor(outgoing[j], "expert", masks[j]) for j in first}
+    held = after(outgoing, *arrived.values())
+    arrived.update({j: from_xor(held[j], "expert", masks[j]) for j in second + near})
+    arrived[0] = outgoing[0]
+    for part in (first, second + near + [0]):
+        done = expert(jnp.concatenate([arrived[j] for j in part], axis=0))
+        for index, j in enumerate(part):
+            results[j] = done[index * capacity : (index + 1) * capacity]
+    returned = jnp.stack(
+        [results[0]] + [from_xor(results[j], "expert", masks[j]) for j in range(1, experts_axis)]
     )
-    result = (
-        jnp.dot(active, down_here, preferred_element_type=jnp.float32)
-        .astype(jnp.bfloat16)
-        .reshape(slot_items.shape)
-    )
-    returned = exchange(result)
     combined = jnp.dot(
         jnp.transpose(select), returned.reshape(-1, model_width), preferred_element_type=jnp.float32
     )

time: 219 us -> 207 us (0.945)
  waiting for transfers between devices: 98.7 us -> 89.7 us
  starting transfers between devices: 39.5 us -> 36.2 us
    ppermute x21, waiting for transfers between devices: 85.9 us -> 72.6 us  [from_xor(): return lax.ppermute(block, axis, [(i, i ^ mask) for i in range(count)])]
    ppermute x10, waiting for transfers between devices: 12.8 us -> 17.1 us  [along(): lax.ppermute(block, 'group', [(2 * a + s, 2 * b + s) for a, b in moves fo...]
    ppermute x21, starting transfers between devices: 23.7 us -> 20.4 us  [from_xor(): return lax.ppermute(block, axis, [(i, i ^ mask) for i in range(count)])]
    dot_general x2 -> x4, matrix products: 5.62 us -> 6.88 us  [the longest x2 5.35 us: expert(): gate_up = jnp.dot(slots, gateup_here, preferred_element_type=jnp.float32)]
    unnamed x50 -> x54, local copies, waits for them, and re-layouts: 7.8 us -> 7.78 us
  transfers between devices with their start and end apart: 31 -> 31, of which waited for: 17 -> 16; matrix products, arithmetic and copies ran while one was open for 7% -> 11% of each run, Pallas kernels for 15% -> 16%
where the time goes in v5:
time: 207 us
  waiting for transfers between devices  89.7 us (43%)
  Pallas kernels  46.5 us (22%)
  starting transfers between devices  36.2 us (17%)
  other arithmetic  14.1 us (7%)
  local copies, waits for them, and re-layouts  9.7 us (5%)
  matrix products  9.21 us (4%)
    ppermute x21, waiting for transfers between devices, from_xor(): return lax.ppermute(block, axis, [(i, i ^ mask) for i in range(count)])  72.6 us
    ppermute x21, starting transfers between devices, from_xor(): return lax.ppermute(block, axis, [(i, i ^ mask) for i in range(count)])  20.4 us
    ppermute x10, waiting for transfers between devices, along(): lax.ppermute(block, 'group', [(2 * a + s, 2 * b + s) for a, b in moves fo...  17.1 us
    pallas_call x2, Pallas kernels, project(): pl.pallas_call(functools.partial(kernel, count), grid_spec=pltpu.Prefetch...  16.2 us
    ppermute x10, starting transfers between devices, along(): lax.ppermute(block, 'group', [(2 * a + s, 2 * b + s) for a, b in moves fo...  15.8 us
    pallas_call x2, Pallas kernels, attend(): pl.pallas_call(functools.partial(attend_kernel, tile, block_of), grid_spe...  15.7 us
    pallas_call x2, Pallas kernels, output_part(): pl.pallas_call(functools.partial(output_kernel, plan), grid_spec=pltpu.Pr...  9.29 us
    unnamed x54, local copies, waits for them, and re-layouts  7.78 us
  transfers between devices with their start and end apart: 31, of which 16 were waited for; matrix products, arithmetic and copies ran while one was open for 11% of the time, Pallas kernels for 16%

profile of v5, /device:TPU:0, one launch (start us, length us, event | category | flops | bytes accessed | tf_op | source)
XLA Modules:
  0.0 206.6 jit_solution(10271344743697918161)
XLA Ops:
  0.7 1.7 copy-done.3
  3.6 1.5 shard_map.167.rest_7_
  5.1 3.0 %collective-permute-start = (bf16[256,1280]{1,0:T(8,128)(2,1)}, bf16[256,1280]{1,0:T(8,128)(2,1)}, u32[]{:S(2)}, u32[]{:S(2)}) collective-permute-start(bf16[256,1280]{1,0:T(8,128)(2,1)} %shard_map.167.rest_7_), channel_id=1, source_target_pairs={{0,8},{4,12},{8,0},{12,4},{16,24},{20,28},{24,16},{28,20},{1,9},{5... | collective-permute-start | bytes 1966088 | tf_op jit(solution)/shard_map/ppermute | solution.py:54
  8.1 1.5 collective-permute-start.1
  9.6 1.5 collective-permute-start.2
  12.7 1.5 collective-permute-start.3
  14.3 2.1 %convert_element_type.62 = bf16[1024,256]{1,0:T(8,128)(2,1)} convert(f32[1024,256]{1,0:T(8,128)} %param.21) | non-fusion elementwise | flops 262144 | bytes 1572864 | tf_op jit(solution)/shard_map/convert_element_type | solution.py:437
  17.4 5.8 %collective-permute-done.rest_8_ = bf16[256,1280]{1,0:T(8,128)(2,1)} collective-permute-done((bf16[256,1280]{1,0:T(8,128)(2,1)}, bf16[256,1280]{1,0:T(8,128)(2,1)}, u32[]{:S(2)}, u32[]{:S(2)}) %collective-permute-start) | collective-permute-done | bytes 655392 | tf_op jit(solution)/shard_map/ppermute | solution.py:54
  23.1 3.0 %collective-permute-done.2.rest_11_ = bf16[256,1280]{1,0:T(8,128)(2,1)} collective-permute-done((bf16[256,1280]{1,0:T(8,128)(2,1)}, bf16[256,1280]{1,0:T(8,128)(2,1)}, u32[]{:S(2)}, u32[]{:S(2)}) %collective-permute-start.2) | collective-permute-done | bytes 655392 | tf_op jit(solution)/shard_map/ppermute | solution.py:36
  26.1 1.5 collective-permute-start.6
  28.3 1.3 collective-permute-start.8
  29.8 11.8 %collective-permute-done.6.rest_12_ = bf16[256,1280]{1,0:T(8,128)(2,1)S(1)} collective-permute-done((bf16[256,1280]{1,0:T(8,128)(2,1)}, bf16[256,1280]{1,0:T(8,128)(2,1)S(1)}, u32[]{:S(2)}, u32[]{:S(2)}) %collective-permute-start.6) | collective-permute-done | bytes 655392 | tf_op jit(solution)/shard_map/ppermute | solution.py:36
  42.4 1.5 collective-permute-start.13
  43.9 3.7 %collective-permute-done.8 = bf16[256,1280]{1,0:T(8,128)(2,1)S(1)} collective-permute-done((bf16[256,1280]{1,0:T(8,128)(2,1)}, bf16[256,1280]{1,0:T(8,128)(2,1)S(1)}, u32[]{:S(2)}, u32[]{:S(2)}) %collective-permute-start.8) | collective-permute-done | bytes 655392 | tf_op jit(solution)/shard_map/ppermute | solution.py:54
  49.7 7.8 %collective-permute-done.13 = bf16[1024,256]{1,0:T(8,128)(2,1)S(1)} collective-permute-done((bf16[1024,256]{1,0:T(8,128)(2,1)}, bf16[1024,256]{1,0:T(8,128)(2,1)S(1)}, u32[]{:S(2)}, u32[]{:S(2)}) %collective-permute-start.13) | collective-permute-done | bytes 524320 | tf_op jit(solution)/shard_map/ppermute | solution.py:36
  58.6 3.0 %collective-permute-start.14 = (bf16[1280,256]{1,0:T(8,128)(2,1)}, bf16[1280,256]{1,0:T(8,128)(2,1)}, u32[]{:S(2)}, u32[]{:S(2)}) collective-permute-start(bf16[1280,256]{1,0:T(8,128)(2,1)} %pad_maximum_fusion.1.rest_0_), channel_id=1, source_target_pairs={{0,8},{4,12},{8,0},{12,4},{16,24},{20,28},{24,16},{28,20},{1,9},{5... | collective-permute-start | bytes 1966088 | tf_op jit(solution)/shard_map/ppermute | solution.py:54
  61.6 6.6 %collective-permute-done.9.rest_13_ = bf16[256,1280]{1,0:T(8,128)(2,1)S(1)} collective-permute-done((bf16[256,1280]{1,0:T(8,128)(2,1)S(1)}, bf16[256,1280]{1,0:T(8,128)(2,1)S(1)}, u32[]{:S(2)}, u32[]{:S(2)}) %collective-permute-start.9) | collective-permute-done | bytes 655392 | tf_op jit(solution)/shard_map/ppermute | solution.py:36
  69.1 1.5 collective-permute-start.15
  71.5 1.5 collective-permute-start.11
  73.7 1.9 fusion.32
  76.7 1.5 collective-permute-done.14.rest_1_
  78.1 7.2 %collective-permute-done.11.rest_14_ = bf16[256,1280]{1,0:T(8,128)(2,1)} collective-permute-done((bf16[256,1280]{1,0:T(8,128)(2,1)}, bf16[256,1280]{1,0:T(8,128)(2,1)}, u32[]{:S(2)}, u32[]{:S(2)}) %collective-permute-start.11) | collective-permute-done | bytes 655392 | tf_op jit(solution)/shard_map/ppermute | solution.py:36
  85.3 4.5 %shard_map.168.own = bf16[2,1024,128]{2,1,0:T(8,128)(2,1)S(1)} custom-call(s32[14]{0:T(128)S(1)} %concatenate.47.meta, bf16[256,2048]{1,0:T(8,128)(2,1)} %fusion.17.rest_0_, bf16[256,2048]{1,0:T(8,128)(2,1)} %collective-permute-done.3.rest_1_, bf16[256,2048]{1,0:T(8,128)(2,1)} %collective-permute-done.4.rest_2_, ...), custom_call_target="tpu_custom_call" | custom-call | flops 4294967296 | bytes 4194304 | tf_op jit(solution)/shard_map/pallas_call | solution.py:226
  89.8 1.6 collective-permute-start.12
  95.0 11.7 %shard_map.169.rest_0_ = bf16[8,1024,128]{2,1,0:T(8,128)(2,1)S(1)} custom-call(s32[14]{0:T(128)S(1)} %concatenate.47.meta, bf16[256,2048]{1,0:T(8,128)(2,1)} %fusion.17.rest_0_, bf16[256,2048]{1,0:T(8,128)(2,1)} %collective-permute-done.3.rest_1_, bf16[256,2048]{1,0:T(8,128)(2,1)} %collective-permute-done.4.rest_2_, ...), custom_call_target="tpu_custom_call" | custom-call | flops 17179869184 | bytes 4194304 | tf_op jit(solution)/shard_map/pallas_call | solution.py:226
  106.7 2.0 collective-permute-done.16.rest_5_
  108.7 1.9 collective-permute-done.18
  110.7 1.6 collective-permute-start.19
  112.3 1.5 collective-permute-start.20
  113.7 7.9 %shard_map.170.kept_rows.sent_rows = bf16[512,1024]{1,0:T(8,128)(2,1)S(1)} custom-call(s32[6]{0:T(128)S(1)} %pad_add_fusion.1.meta, bf16[2,1024,128]{2,1,0:T(8,128)(2,1)S(1)} %shard_map.168.own, bf16[2,1024,128]{2,1,0:T(8,128)(2,1)S(1)} %collective-permute-done.12.far, bf16[8,1024,128]{2,1,0:T(8,128)(2,1)S(1)} %shard_map.169.rest_0_), custom_call_target="tpu_custom_call" | custom-call | flops 8589934592 | bytes 524288 | tf_op jit(solution)/shard_map/pallas_call | solution.py:326
  121.6 4.3 %collective-permute-done.20 = bf16[1280,256]{1,0:T(8,128)(2,1)S(1)} collective-permute-done((bf16[1280,256]{1,0:T(8,128)(2,1)S(1)}, bf16[1280,256]{1,0:T(8,128)(2,1)S(1)}, u32[]{:S(2)}, u32[]{:S(2)}) %collective-permute-start.20) | collective-permute-done | bytes 655392 | tf_op jit(solution)/shard_map/ppermute | solution.py:54
  126.6 7.9 %shard_map.171.sent_rows.kept_rows = bf16[512,1024]{1,0:T(8,128)(2,1)S(1)} custom-call(s32[6]{0:T(128)S(1)} %pad_add_fusion.1.meta, bf16[2,1024,128]{2,1,0:T(8,128)(2,1)S(1)} %shard_map.168.own, bf16[2,1024,128]{2,1,0:T(8,128)(2,1)S(1)} %collective-permute-done.12.far, bf16[8,1024,128]{2,1,0:T(8,128)(2,1)S(1)} %shard_map.169.rest_0_), custom_call_target="tpu_custom_call" | custom-call | flops 8589934592 | bytes 524288 | tf_op jit(solution)/shard_map/pallas_call | solution.py:326
  134.5 4.2 %shard_map.173 = (bf16[1,256,2048]{2,1,0:T(8,128)(2,1)S(1)}, bf16[1,256,2048]{2,1,0:T(8,128)(2,1)S(1)}) custom-call(s32[8]{0:T(128)S(1)} %pad_add_fusion.meta, bf16[512,1024]{1,0:T(8,128)(2,1)S(1)} %shard_map.171.sent_rows.kept_rows, bf16[512,1024]{1,0:T(8,128)(2,1)S(1)} %shard_map.170.kept_rows.sent_rows, bf16[1280,256]{1,0:T(8,128)(2,1)} %pad_maximum_fusion.1.rest_0_, ...), custom_call_target="tpu_custom_call" | custom-call | flops 6442450944 | bytes 4194304 | tf_op jit(solution)/shard_map/pallas_call | solution.py:370
  138.8 5.1 %shard_map.172 = (bf16[1,256,2048]{2,1,0:T(8,128)(2,1)S(1)}, bf16[1,256,2048]{2,1,0:T(8,128)(2,1)}) custom-call(s32[8]{0:T(128)S(1)} %pad_add_fusion.meta, bf16[512,1024]{1,0:T(8,128)(2,1)S(1)} %shard_map.170.kept_rows.sent_rows, bf16[512,1024]{1,0:T(8,128)(2,1)S(1)} %shard_map.171.sent_rows.kept_rows, bf16[1280,256]{1,0:T(8,128)(2,1)} %pad_maximum_fusion.1.rest_0_, ...), custom_call_target="tpu_custom_call" | custom-call | flops 6442450944 | bytes 4194304 | tf_op jit(solution)/shard_map/pallas_call | solution.py:370
  144.4 1.4 add_convert_fusion
  145.8 1.5 collective-permute-start.24
  149.4 21.7 %collective-permute-done.24 = bf16[1,256,2048]{2,1,0:T(8,128)(2,1)} collective-permute-done((bf16[1,256,2048]{2,1,0:T(8,128)(2,1)}, bf16[1,256,2048]{2,1,0:T(8,128)(2,1)}, u32[]{:S(2)}, u32[]{:S(2)}) %collective-permute-start.24) | collective-permute-done | bytes 1048608 | tf_op jit(solution)/shard_map/ppermute | solution.py:36
  173.6 3.8 %shard_map.174 = (bf16[256,2048]{1,0:T(8,128)(2,1)}, bf16[256,2048]{1,0:T(8,128)(2,1)S(1)}) custom-call(bf16[256,2048]{1,0:T(8,128)(2,1)S(1)} %copy-done.2, f32[1,2048]{1,0:T(1,128)S(1)} %bitcast.59, bf16[256,2048]{1,0:T(8,128)(2,1)S(1)} %bitcast.58, bf16[256,2048]{1,0:T(8,128)(2,1)} %bitcast.7.rest_1_, bf16[256,2048]{1,0:T(8,128)(2,1)} %bitcast.8.rest_2_), custom_call_target="tpu_custom_call" | custom-call | tf_op jit(solution)/shard_map/pallas_call | solution.py:399
  177.9 1.6 collective-permute-start.25
  179.9 5.4 %collective-permute-done.25 = bf16[64,2048]{1,0:T(8,128)(2,1)S(1)} collective-permute-done((bf16[64,2048]{1,0:T(8,128)(2,1)S(1)}, bf16[64,2048]{1,0:T(8,128)(2,1)S(1)}, u32[]{:S(2)}, u32[]{:S(2)}) %collective-permute-start.25) | collective-permute-done | bytes 262176 | tf_op jit(solution)/shard_map/ppermute | solution.py:36
  185.5 1.6 collective-permute-start.26
  187.1 4.0 %fusion = f32[64,1536]{1,0:T(8,128)S(1)} fusion(bf16[64,2048]{1,0:T(8,128)(2,1)S(1)} %collective-permute-done.25, bf16[1,2048,1536]{2,1,0:T(8,128)(2,1)} %param.26), kind=kOutput, calls=%fused_computation | convolution fusion | flops 402653184 | bytes 6946816 | tf_op jit(solution)/shard_map/dot_general | solution.py:539
  192.4 1.4 collective-permute-done.26
  193.8 1.4 fusion.2
  196.1 2.0 collective-permute-start.30
  199.3 1.6 collective-permute-done.28
  200.9 4.1 %collective-permute-done.30 = bf16[64,2048]{1,0:T(8,128)(2,1)S(1)} collective-permute-done((bf16[64,2048]{1,0:T(8,128)(2,1)S(1)}, bf16[64,2048]{1,0:T(8,128)(2,1)S(1)}, u32[]{:S(2)}, u32[]{:S(2)}) %collective-permute-start.30) | collective-permute-done | bytes 262176 | tf_op jit(solution)/shard_map/ppermute | solution.py:36
  205.1 1.5 fusion.8
  (145 shorter events, 26.3 us)
Async XLA Ops:
  0.6 190.5 %copy-start = (bf16[1,768,2048]{2,1,0:T(8,128)(2,1)S(1)}, bf16[1,768,2048]{2,1,0:T(8,128)(2,1)}, u32[]{:S(2)}) copy-start(bf16[1,768,2048]{2,1,0:T(8,128)(2,1)} %param.27) | copy-start | bytes 9437188
  0.6 10.8 %copy-start.18 = (f32[2048]{0:T(1024)S(1)}, f32[2048]{0:T(1024)}, u32[]{:S(2)}) copy-start(f32[2048]{0:T(1024)} %param.17) | copy-start | bytes 24580
  0.7 10.4 %copy-start.1 = (bf16[256,2048]{1,0:T(8,128)(2,1)S(1)}, bf16[256,2048]{1,0:T(8,128)(2,1)}, u32[]{:S(2)}) copy-start(bf16[256,2048]{1,0:T(8,128)(2,1)} %states.1) | copy-start | bytes 3145732
  5.1 9.2 %copy-start.24 = (s32[4]{0:T(128)S(1)}, s32[4]{0:T(128)}, u32[]{:S(2)}) copy-start(s32[4]{0:T(128)} %constant.111.clone) | copy-start | bytes 52
  5.1 18.1 %collective-permute-start = (bf16[256,1280]{1,0:T(8,128)(2,1)}, bf16[256,1280]{1,0:T(8,128)(2,1)}, u32[]{:S(2)}, u32[]{:S(2)}) collective-permute-start(bf16[256,1280]{1,0:T(8,128)(2,1)} %shard_map.167.rest_7_), channel_id=1, source_target_pairs={{0,8},{4,12},{8,0},{12,4},{16,24},{20,28},{24,16},{28,20},{1,9},{5... | collective-permute-start | bytes 1966088 | tf_op jit(solution)/shard_map/ppermute | solution.py:54
  8.1 15.0 %collective-permute-start.1 = (bf16[256,1280]{1,0:T(8,128)(2,1)}, bf16[256,1280]{1,0:T(8,128)(2,1)}, u32[]{:S(2)}, u32[]{:S(2)}) collective-permute-start(bf16[256,1280]{1,0:T(8,128)(2,1)} %shard_map.167.rest_7_), channel_id=1, source_target_pairs={{8,16},{12,20},{16,8},{20,12},{9,17},{13,21},{17,9},{21,13},{10,18... | collective-permute-start | bytes 1966088 | tf_op jit(solution)/shard_map/ppermute | solution.py:54
  9.6 16.5 %collective-permute-start.2 = (bf16[256,1280]{1,0:T(8,128)(2,1)}, bf16[256,1280]{1,0:T(8,128)(2,1)}, u32[]{:S(2)}, u32[]{:S(2)}) collective-permute-start(bf16[256,1280]{1,0:T(8,128)(2,1)} %shard_map.167.rest_7_), channel_id=1, source_target_pairs={{0,4},{4,0},{8,12},{12,8},{16,20},{20,16},{24,28},{28,24},{1,5},{5... | collective-permute-start | bytes 1966088 | tf_op jit(solution)/shard_map/ppermute | solution.py:36
  11.4 5.0 %copy-start.21 = (s32[4,4]{1,0:T(4,128)S(1)}, s32[4,4]{1,0:T(4,128)}, u32[]{:S(2)}) copy-start(s32[4,4]{1,0:T(4,128)} %constant.112.clone) | copy-start | bytes 196
  11.4 5.3 %copy-start.22 = (s32[4]{0:T(128)S(1)}, s32[4]{0:T(128)}, u32[]{:S(2)}) copy-start(s32[4]{0:T(128)} %param.24) | copy-start | bytes 52
  11.4 5.9 %copy-start.20 = (f32[128]{0:T(128)S(1)}, f32[128]{0:T(128)}, u32[]{:S(2)}) copy-start(f32[128]{0:T(128)} %param.23) | copy-start | bytes 1540
  11.4 18.3 %copy-start.23 = (f32[128]{0:T(128)S(1)}, f32[128]{0:T(128)}, u32[]{:S(2)}) copy-start(f32[128]{0:T(128)} %param.22) | copy-start | bytes 1540
  12.7 36.9 %collective-permute-start.3 = (bf16[256,2048]{1,0:T(8,128)(2,1)}, bf16[256,2048]{1,0:T(8,128)(2,1)}, u32[]{:S(2)}, u32[]{:S(2)}) collective-permute-start(bf16[256,2048]{1,0:T(8,128)(2,1)} %fusion.17.rest_0_), channel_id=1, source_target_pairs={{0,2},{1,3},{2,0},{3,1},{4,6},{5,7},{6,4},{7,5},{8,10},{9,11},{10,... | collective-permute-start | bytes 3145736 | tf_op jit(solution)/shard_map/ppermute | solution.py:36
  14.2 71.1 %collective-permute-start.4 = (bf16[256,2048]{1,0:T(8,128)(2,1)}, bf16[256,2048]{1,0:T(8,128)(2,1)}, u32[]{:S(2)}, u32[]{:S(2)}) collective-permute-start(bf16[256,2048]{1,0:T(8,128)(2,1)} %fusion.17.rest_0_), channel_id=1, source_target_pairs={{0,1},{1,0},{2,3},{3,2},{4,5},{5,4},{6,7},{7,6},{8,9},{9,8},{10,11... | collective-permute-start | bytes 3145736 | tf_op jit(solution)/shard_map/ppermute | solution.py:36
  16.6 40.9 %copy-start.14 = (bf16[1024,256]{1,0:T(8,128)(2,1)S(1)}, bf16[1024,256]{1,0:T(8,128)(2,1)}, u32[]{:S(2)}) copy-start(bf16[1024,256]{1,0:T(8,128)(2,1)} %convert_element_type.62) | copy-start | bytes 1572868
  26.1 15.5 %collective-permute-start.6 = (bf16[256,1280]{1,0:T(8,128)(2,1)}, bf16[256,1280]{1,0:T(8,128)(2,1)S(1)}, u32[]{:S(2)}, u32[]{:S(2)}) collective-permute-start(bf16[256,1280]{1,0:T(8,128)(2,1)} %collective-permute-done.rest_8_), channel_id=1, source_target_pairs={{0,4},{4,0},{8,12},{12,8},{16,20},{20,16},{24,28},{28,24},{1,5},{5... | collective-permute-start | bytes 1966088 | tf_op jit(solution)/shard_map/ppermute | solution.py:36
  27.6 16.3 %collective-permute-start.7 = (bf16[256,1280]{1,0:T(8,128)(2,1)}, bf16[256,1280]{1,0:T(8,128)(2,1)S(1)}, u32[]{:S(2)}, u32[]{:S(2)}) collective-permute-start(bf16[256,1280]{1,0:T(8,128)(2,1)} %collective-permute-done.rest_8_), channel_id=1, source_target_pairs={{8,16},{12,20},{16,8},{20,12},{9,17},{13,21},{17,9},{21,13},{10,18... | collective-permute-start | bytes 1966088 | tf_op jit(solution)/shard_map/ppermute | solution.py:54
  28.3 19.3 %collective-permute-start.8 = (bf16[256,1280]{1,0:T(8,128)(2,1)}, bf16[256,1280]{1,0:T(8,128)(2,1)S(1)}, u32[]{:S(2)}, u32[]{:S(2)}) collective-permute-start(bf16[256,1280]{1,0:T(8,128)(2,1)} %collective-permute-done.1), channel_id=1, source_target_pairs={{8,0},{12,4},{16,24},{20,28},{9,1},{13,5},{17,25},{21,29},{10,2},{... | collective-permute-start | bytes 1966088 | tf_op jit(solution)/shard_map/ppermute | solution.py:54
  42.4 15.1 %collective-permute-start.13 = (bf16[1024,256]{1,0:T(8,128)(2,1)}, bf16[1024,256]{1,0:T(8,128)(2,1)S(1)}, u32[]{:S(2)}, u32[]{:S(2)}) collective-permute-start(bf16[1024,256]{1,0:T(8,128)(2,1)} %convert_element_type.62), channel_id=1, source_target_pairs={{0,4},{4,0},{8,12},{12,8},{16,20},{20,16},{24,28},{28,24},{1,5},{5... | collective-permute-start | bytes 1572872 | tf_op jit(solution)/shard_map/ppermute | solution.py:36
  47.7 23.9 %copy-start.7 = (bf16[256,1280]{1,0:T(8,128)(2,1)}, bf16[256,1280]{1,0:T(8,128)(2,1)S(1)}, u32[]{:S(2)}) copy-start(bf16[256,1280]{1,0:T(8,128)(2,1)S(1)} %broadcast_select_fusion.3.rest_9_) | copy-start | bytes 1966084
  47.7 20.6 %collective-permute-start.9 = (bf16[256,1280]{1,0:T(8,128)(2,1)S(1)}, bf16[256,1280]{1,0:T(8,128)(2,1)S(1)}, u32[]{:S(2)}, u32[]{:S(2)}) collective-permute-start(bf16[256,1280]{1,0:T(8,128)(2,1)S(1)} %broadcast_select_fusion.3.rest_9_), channel_id=1, source_target_pairs={{0,4},{4,0},{8,12},{12,8},{16,20},{20,16},{24,28},{28,24},{1,5},{5... | collective-permute-start | bytes 1966088 | tf_op jit(solution)/shard_map/ppermute | solution.py:36
  48.3 22.3 %collective-permute-start.10 = (bf16[256,1280]{1,0:T(8,128)(2,1)S(1)}, bf16[256,1280]{1,0:T(8,128)(2,1)S(1)}, u32[]{:S(2)}, u32[]{:S(2)}) collective-permute-start(bf16[256,1280]{1,0:T(8,128)(2,1)S(1)} %collective-permute-done.7), channel_id=1, source_target_pairs={{8,0},{12,4},{16,24},{20,28},{9,1},{13,5},{17,25},{21,29},{10,2},{... | collective-permute-start | bytes 1966088 | tf_op jit(solution)/shard_map/ppermute | solution.py:54
  49.7 35.6 %collective-permute-start.5 = (bf16[256,2048]{1,0:T(8,128)(2,1)}, bf16[256,2048]{1,0:T(8,128)(2,1)}, u32[]{:S(2)}, u32[]{:S(2)}) collective-permute-start(bf16[256,2048]{1,0:T(8,128)(2,1)} %collective-permute-done.3.rest_1_), channel_id=1, source_target_pairs={{0,1},{1,0},{2,3},{3,2},{4,5},{5,4},{6,7},{7,6},{8,9},{9,8},{10,11... | collective-permute-start | bytes 3145736 | tf_op jit(solution)/shard_map/ppermute | solution.py:36
  57.5 14.0 %copy-start.15 = (bf16[1024,256]{1,0:T(8,128)(2,1)}, bf16[1024,256]{1,0:T(8,128)(2,1)S(1)}, u32[]{:S(2)}) copy-start(bf16[1024,256]{1,0:T(8,128)(2,1)S(1)} %collective-permute-done.13) | copy-start | bytes 1572868
  58.6 19.6 %collective-permute-start.14 = (bf16[1280,256]{1,0:T(8,128)(2,1)}, bf16[1280,256]{1,0:T(8,128)(2,1)}, u32[]{:S(2)}, u32[]{:S(2)}) collective-permute-start(bf16[1280,256]{1,0:T(8,128)(2,1)} %pad_maximum_fusion.1.rest_0_), channel_id=1, source_target_pairs={{0,8},{4,12},{8,0},{12,4},{16,24},{20,28},{24,16},{28,20},{1,9},{5... | collective-permute-start | bytes 1966088 | tf_op jit(solution)/shard_map/ppermute | solution.py:54
  69.1 9.0 %collective-permute-start.15 = (bf16[1280,256]{1,0:T(8,128)(2,1)}, bf16[1280,256]{1,0:T(8,128)(2,1)}, u32[]{:S(2)}, u32[]{:S(2)}) collective-permute-start(bf16[1280,256]{1,0:T(8,128)(2,1)} %pad_maximum_fusion.1.rest_0_), channel_id=1, source_target_pairs={{8,16},{12,20},{16,8},{20,12},{9,17},{13,21},{17,9},{21,13},{10,18... | collective-permute-start | bytes 1966088 | tf_op jit(solution)/shard_map/ppermute | solution.py:54
  71.5 13.8 %collective-permute-start.11 = (bf16[256,1280]{1,0:T(8,128)(2,1)}, bf16[256,1280]{1,0:T(8,128)(2,1)}, u32[]{:S(2)}, u32[]{:S(2)}) collective-permute-start(bf16[256,1280]{1,0:T(8,128)(2,1)} %broadcast_select_fusion.2.rest_10_), channel_id=1, source_target_pairs={{0,4},{4,0},{8,12},{12,8},{16,20},{20,16},{24,28},{28,24},{1,5},{5... | collective-permute-start | bytes 1966088 | tf_op jit(solution)/shard_map/ppermute | solution.py:36
  75.6 9.7 %copy-start.8 = (bf16[256,1280]{1,0:T(8,128)(2,1)S(1)}, bf16[256,1280]{1,0:T(8,128)(2,1)}, u32[]{:S(2)}) copy-start(bf16[256,1280]{1,0:T(8,128)(2,1)} %copy-done.7) | copy-start | bytes 1966084
  75.6 9.7 %copy-start.11 = (bf16[256,1280]{1,0:T(8,128)(2,1)S(1)}, bf16[256,1280]{1,0:T(8,128)(2,1)}, u32[]{:S(2)}) copy-start(bf16[256,1280]{1,0:T(8,128)(2,1)} %copy-done.10) | copy-start | bytes 1966084
  75.6 9.7 %copy-start.13 = (bf16[256,1280]{1,0:T(8,128)(2,1)S(1)}, bf16[256,1280]{1,0:T(8,128)(2,1)}, u32[]{:S(2)}) copy-start(bf16[256,1280]{1,0:T(8,128)(2,1)} %copy-done.12) | copy-start | bytes 1966084
  89.8 20.8 %collective-permute-start.12 = (bf16[2,1024,128]{2,1,0:T(8,128)(2,1)S(1)}, bf16[2,1024,128]{2,1,0:T(8,128)(2,1)S(1)}, u32[]{:S(2)}, u32[]{:S(2)}) collective-permute-start(bf16[2,1024,128]{2,1,0:T(8,128)(2,1)S(1)} %shard_map.168.own), channel_id=1, source_target_pairs={{0,4},{4,0},{8,12},{12,8},{16,20},{20,16},{24,28},{28,24},{1,5},{5... | collective-permute-start | bytes 1572872 | tf_op jit(solution)/shard_map/ppermute | solution.py:36
  92.4 16.3 %collective-permute-start.17 = (bf16[1280,256]{1,0:T(8,128)(2,1)}, bf16[1280,256]{1,0:T(8,128)(2,1)S(1)}, u32[]{:S(2)}, u32[]{:S(2)}) collective-permute-start(bf16[1280,256]{1,0:T(8,128)(2,1)} %collective-permute-done.14.rest_1_), channel_id=1, source_target_pairs={{8,16},{12,20},{16,8},{20,12},{9,17},{13,21},{17,9},{21,13},{10,18... | collective-permute-start | bytes 1966088 | tf_op jit(solution)/shard_map/ppermute | solution.py:54
  93.1 15.6 %collective-permute-start.16 = (bf16[768,256]{1,0:T(8,128)(2,1)S(1)}, bf16[768,256]{1,0:T(8,128)(2,1)S(1)}, u32[]{:S(2)}, u32[]{:S(2)}) collective-permute-start(bf16[768,256]{1,0:T(8,128)(2,1)S(1)} %slice.83), channel_id=1, source_target_pairs={{0,4},{4,0},{8,12},{12,8},{16,20},{20,16},{24,28},{28,24},{1,5},{5... | collective-permute-start | bytes 1179656 | tf_op jit(solution)/shard_map/ppermute | solution.py:36
  93.7 16.9 %collective-permute-start.18 = (bf16[1280,256]{1,0:T(8,128)(2,1)}, bf16[1280,256]{1,0:T(8,128)(2,1)S(1)}, u32[]{:S(2)}, u32[]{:S(2)}) collective-permute-start(bf16[1280,256]{1,0:T(8,128)(2,1)} %collective-permute-done.15), channel_id=1, source_target_pairs={{8,0},{12,4},{16,24},{20,28},{9,1},{13,5},{17,25},{21,29},{10,2},{... | collective-permute-start | bytes 1966088 | tf_op jit(solution)/shard_map/ppermute | solution.py:54
  110.7 10.9 %collective-permute-start.19 = (bf16[768,256]{1,0:T(8,128)(2,1)S(1)}, bf16[768,256]{1,0:T(8,128)(2,1)S(1)}, u32[]{:S(2)}, u32[]{:S(2)}) collective-permute-start(bf16[768,256]{1,0:T(8,128)(2,1)S(1)} %slice.100), channel_id=1, source_target_pairs={{0,4},{4,0},{8,12},{12,8},{16,20},{20,16},{24,28},{28,24},{1,5},{5... | collective-permute-start | bytes 1179656 | tf_op jit(solution)/shard_map/ppermute | solution.py:36
  112.3 13.7 %collective-permute-start.20 = (bf16[1280,256]{1,0:T(8,128)(2,1)S(1)}, bf16[1280,256]{1,0:T(8,128)(2,1)S(1)}, u32[]{:S(2)}, u32[]{:S(2)}) collective-permute-start(bf16[1280,256]{1,0:T(8,128)(2,1)S(1)} %collective-permute-done.17), channel_id=1, source_target_pairs={{8,0},{12,4},{16,24},{20,28},{9,1},{13,5},{17,25},{21,29},{10,2},{... | collective-permute-start | bytes 1966088 | tf_op jit(solution)/shard_map/ppermute | solution.py:54
  126.0 8.5 %collective-permute-start.21 = (bf16[768,256]{1,0:T(8,128)(2,1)S(1)}, bf16[768,256]{1,0:T(8,128)(2,1)S(1)}, u32[]{:S(2)}, u32[]{:S(2)}) collective-permute-start(bf16[768,256]{1,0:T(8,128)(2,1)S(1)} %slice.101), channel_id=1, source_target_pairs={{0,4},{4,0},{8,12},{12,8},{16,20},{20,16},{24,28},{28,24},{1,5},{5... | collective-permute-start | bytes 1179656 | tf_op jit(solution)/shard_map/ppermute | solution.py:36
  138.7 5.7 %collective-permute-start.23 = (bf16[1,256,2048]{2,1,0:T(8,128)(2,1)S(1)}, bf16[1,256,2048]{2,1,0:T(8,128)(2,1)S(1)}, u32[]{:S(2)}, u32[]{:S(2)}) collective-permute-start(bf16[1,256,2048]{2,1,0:T(8,128)(2,1)S(1)} %get-tuple-element.81), channel_id=1, source_target_pairs={{0,1},{1,0},{2,3},{3,2},{4,5},{5,4},{6,7},{7,6},{8,9},{9,8},{10,11... | collective-permute-start | bytes 3145736 | tf_op jit(solution)/shard_map/ppermute | solution.py:36
  143.9 27.3 %copy-start.9 = (f32[2048]{0:T(1024)S(1)}, f32[2048]{0:T(1024)}, u32[]{:S(2)}) copy-start(f32[2048]{0:T(1024)} %param.18) | copy-start | bytes 24580
  143.9 5.5 %collective-permute-start.22 = (bf16[1,256,2048]{2,1,0:T(8,128)(2,1)}, bf16[1,256,2048]{2,1,0:T(8,128)(2,1)}, u32[]{:S(2)}, u32[]{:S(2)}) collective-permute-start(bf16[1,256,2048]{2,1,0:T(8,128)(2,1)} %get-tuple-element.79), channel_id=1, source_target_pairs={{0,1},{1,0},{2,3},{3,2},{4,5},{5,4},{6,7},{7,6},{8,9},{9,8},{10,11... | collective-permute-start | bytes 3145736 | tf_op jit(solution)/shard_map/ppermute | solution.py:36
  145.8 25.4 %collective-permute-start.24 = (bf16[1,256,2048]{2,1,0:T(8,128)(2,1)}, bf16[1,256,2048]{2,1,0:T(8,128)(2,1)}, u32[]{:S(2)}, u32[]{:S(2)}) collective-permute-start(bf16[1,256,2048]{2,1,0:T(8,128)(2,1)} %add_convert_fusion), channel_id=1, source_target_pairs={{0,2},{1,3},{2,0},{3,1},{4,6},{5,7},{6,4},{7,5},{8,10},{9,11},{10,... | collective-permute-start | bytes 3145736 | tf_op jit(solution)/shard_map/ppermute | solution.py:36
  177.9 7.4 %collective-permute-start.25 = (bf16[64,2048]{1,0:T(8,128)(2,1)S(1)}, bf16[64,2048]{1,0:T(8,128)(2,1)S(1)}, u32[]{:S(2)}, u32[]{:S(2)}) collective-permute-start(bf16[64,2048]{1,0:T(8,128)(2,1)S(1)} %get-tuple-element.88), channel_id=1, source_target_pairs={{0,2},{1,3},{2,0},{3,1},{4,6},{5,7},{6,4},{7,5},{8,10},{9,11},{10,... | collective-permute-start | bytes 786440 | tf_op jit(solution)/shard_map/ppermute | solution.py:36
  179.5 14.3 %slice-start = ((s8[6291456]{0:T(1024)(128)(4,1)}), s8[4194304]{0:T(1024)(128)(4,1)S(1)}, s32[]{:S(2)}) async-start(s8[6291456]{0:T(1024)(128)(4,1)} %bitcast.60), calls=%async_computation | async-start | bytes 8388608
  185.4 7.0 %collective-permute-start.27 = (bf16[64,2048]{1,0:T(8,128)(2,1)S(1)}, bf16[64,2048]{1,0:T(8,128)(2,1)S(1)}, u32[]{:S(2)}, u32[]{:S(2)}) collective-permute-start(bf16[64,2048]{1,0:T(8,128)(2,1)S(1)} %get-tuple-element.87), channel_id=1, source_target_pairs={{0,1},{1,0},{2,3},{3,2},{4,5},{5,4},{6,7},{7,6},{8,9},{9,8},{10,11... | collective-permute-start | bytes 786440 | tf_op jit(solution)/shard_map/ppermute | solution.py:36
  185.5 8.3 %slice-start.1 = ((s8[6291456]{0:T(1024)(128)(4,1)}), s8[2097152]{0:T(1024)(128)(4,1)S(1)}, s32[]{:S(2)}) async-start(s8[6291456]{0:T(1024)(128)(4,1)} %bitcast.60), calls=%async_computation.1 | async-start | bytes 4194304
  185.5 8.3 %collective-permute-start.26 = (bf16[64,2048]{1,0:T(8,128)(2,1)S(1)}, bf16[64,2048]{1,0:T(8,128)(2,1)S(1)}, u32[]{:S(2)}, u32[]{:S(2)}) collective-permute-start(bf16[64,2048]{1,0:T(8,128)(2,1)S(1)} %get-tuple-element.86), channel_id=1, source_target_pairs={{0,3},{1,2},{2,1},{3,0},{4,7},{5,6},{6,5},{7,4},{8,11},{9,10},{10,... | collective-permute-start | bytes 786440 | tf_op jit(solution)/shard_map/ppermute | solution.py:36
  191.8 9.1 %collective-permute-start.28 = (bf16[64,2048]{1,0:T(8,128)(2,1)S(1)}, bf16[64,2048]{1,0:T(8,128)(2,1)S(1)}, u32[]{:S(2)}, u32[]{:S(2)}) collective-permute-start(bf16[64,2048]{1,0:T(8,128)(2,1)S(1)} %fusion.12), channel_id=1, source_target_pairs={{0,2},{1,3},{2,0},{3,1},{4,6},{5,7},{6,4},{7,5},{8,10},{9,11},{10,... | collective-permute-start | bytes 786440 | tf_op jit(solution)/shard_map/ppermute | solution.py:36
  196.1 8.9 %collective-permute-start.30 = (bf16[64,2048]{1,0:T(8,128)(2,1)S(1)}, bf16[64,2048]{1,0:T(8,128)(2,1)S(1)}, u32[]{:S(2)}, u32[]{:S(2)}) collective-permute-start(bf16[64,2048]{1,0:T(8,128)(2,1)S(1)} %get-tuple-element.93), channel_id=1, source_target_pairs={{0,3},{1,2},{2,1},{3,0},{4,7},{5,6},{6,5},{7,4},{8,11},{9,10},{10,... | collective-permute-start | bytes 786440 | tf_op jit(solution)/shard_map/ppermute | solution.py:36
  198.1 6.9 %collective-permute-start.29 = (bf16[64,2048]{1,0:T(8,128)(2,1)S(1)}, bf16[64,2048]{1,0:T(8,128)(2,1)S(1)}, u32[]{:S(2)}, u32[]{:S(2)}) collective-permute-start(bf16[64,2048]{1,0:T(8,128)(2,1)S(1)} %get-tuple-element.94), channel_id=1, source_target_pairs={{0,1},{1,0},{2,3},{3,2},{4,5},{5,4},{6,7},{7,6},{8,9},{9,8},{10,11... | collective-permute-start | bytes 786440 | tf_op jit(solution)/shard_map/ppermute | solution.py:36
  (10 other events, 15.4 us)

commit v6 on v5

--- a/solution.py
+++ b/solution.py
@@ -462,7 +462,7 @@
         plan = [((k, 0, depth, 0),) for k in range(groups)]
     joined_rounds.round()
     shards = joined_rounds.held(range(groups))
-    output_rounds.round(joined_rounds.token())
+    output_rounds.round()
 
     masks = doubling_masks(experts_axis)
     block_order = jnp.bitwise_xor(group_member, jnp.array(masks, jnp.int32))
@@ -499,10 +499,9 @@
     blocks[0] = after(blocks[0], select)
     own_pair = project(key_kernel, 0, 1, meta, blocks, shards, *key_tables, mixer)
     far_pair = cross(own_pair)
-    rows_now = [after(blocks[0], own_pair)] + blocks[1:]
+    rows_now = [after(blocks[0], own_pair, output_rounds.token())] + blocks[1:]
+    output_rounds.round(own_pair)
     queries = [project(query_kernel, 1, heads // 2, meta, rows_now, shards, *query_tables, mixer)]
-    queries[0] = after(queries[0], output_rounds.token())
-    output_rounds.round(queries[0], far_pair)
 
     valid_length = jnp.sum(jnp.where(jnp.arange(lengths.shape[0]) == group_index // 2, lengths, 0))
     attend_meta = jnp.concatenate([jnp.stack([parity, valid_length]), block_order]).astype(jnp.int32)

time: 207 us -> 206 us (level); the launches traced: 207 us -> 203 us
  waiting for transfers between devices: 89.7 us -> 85.7 us
  starting transfers between devices: 36.2 us -> 33.2 us
  local copies, waits for them, and re-layouts: 9.7 us -> 12.5 us
    ppermute x21, waiting for transfers between devices: 72.6 us -> 60.1 us  [from_xor(): return lax.ppermute(block, axis, [(i, i ^ mask) for i in range(count)])]
    ppermute x10, waiting for transfers between devices: 17.1 us -> 25.6 us  [along(): lax.ppermute(block, 'group', [(2 * a + s, 2 * b + s) for a, b in moves fo...]
    ppermute x21, starting transfers between devices: 20.4 us -> 18.3 us  [from_xor(): return lax.ppermute(block, axis, [(i, i ^ mask) for i in range(count)])]
    unnamed x54 -> x60, local copies, waits for them, and re-layouts: 7.78 us -> 8.54 us
  transfers between devices with their start and end apart: 31 -> 31, of which waited for: 16 -> 16; matrix products, arithmetic and copies ran while one was open for 11% -> 13% of each run, Pallas kernels for 16% -> 16%
where the time goes in v6:
time: 206 us; the launch traced here: 203 us
  waiting for transfers between devices  85.7 us (42%)
  Pallas kernels  46.3 us (22%)
  starting transfers between devices  33.2 us (16%)
  other arithmetic  14.5 us (7%)
  local copies, waits for them, and re-layouts  12.5 us (6%)
  matrix products  9.2 us (4%)
    ppermute x21, waiting for transfers between devices, from_xor(): return lax.ppermute(block, axis, [(i, i ^ mask) for i in range(count)])  60.1 us
    ppermute x10, waiting for transfers between devices, along(): lax.ppermute(block, 'group', [(2 * a + s, 2 * b + s) for a, b in moves fo...  25.6 us
    ppermute x21, starting transfers between devices, from_xor(): return lax.ppermute(block, axis, [(i, i ^ mask) for i in range(count)])  18.3 us
    pallas_call x2, Pallas kernels, project(): pl.pallas_call(functools.partial(kernel, count), grid_spec=pltpu.Prefetch...  16.2 us
    pallas_call x2, Pallas kernels, attend(): pl.pallas_call(functools.partial(attend_kernel, tile, block_of), grid_spe...  15.9 us
    ppermute x10, starting transfers between devices, along(): lax.ppermute(block, 'group', [(2 * a + s, 2 * b + s) for a, b in moves fo...  14.9 us
    pallas_call x2, Pallas kernels, output_part(): pl.pallas_call(functools.partial(output_kernel, plan), grid_spec=pltpu.Pr...  8.9 us
    unnamed x60, local copies, waits for them, and re-layouts  8.54 us
  transfers between devices with their start and end apart: 31, of which 16 were waited for; matrix products, arithmetic and copies ran while one was open for 13% of the time, Pallas kernels for 16%

profile of v6, /device:TPU:0, one launch (start us, length us, event | category | flops | bytes accessed | tf_op | source)
XLA Modules:
  0.0 202.7 jit_solution(5429618599144492452)
XLA Ops:
  0.7 1.7 copy-done.3
  2.4 1.2 copy-done.4
  3.6 1.5 shard_map.167.rest_7_
  5.1 2.9 %collective-permute-start.2 = (bf16[256,1280]{1,0:T(8,128)(2,1)}, bf16[256,1280]{1,0:T(8,128)(2,1)}, u32[]{:S(2)}, u32[]{:S(2)}) collective-permute-start(bf16[256,1280]{1,0:T(8,128)(2,1)} %shard_map.167.rest_7_), channel_id=1, source_target_pairs={{0,4},{4,0},{8,12},{12,8},{16,20},{20,16},{24,28},{28,24},{1,5},{5... | collective-permute-start | bytes 1966088 | tf_op jit(solution)/shard_map/ppermute | solution.py:36
  8.0 1.5 collective-permute-start.1
  9.5 3.6 %collective-permute-start = (bf16[256,1280]{1,0:T(8,128)(2,1)}, bf16[256,1280]{1,0:T(8,128)(2,1)}, u32[]{:S(2)}, u32[]{:S(2)}) collective-permute-start(bf16[256,1280]{1,0:T(8,128)(2,1)} %shard_map.167.rest_7_), channel_id=1, source_target_pairs={{0,8},{4,12},{8,0},{12,4},{16,24},{20,28},{24,16},{28,20},{1,9},{5... | collective-permute-start | bytes 1966088 | tf_op jit(solution)/shard_map/ppermute | solution.py:54
  13.5 1.3 fusion.17.rest_0_
  14.8 1.5 collective-permute-start.3
  16.3 2.1 %convert_element_type.62 = bf16[1024,256]{1,0:T(8,128)(2,1)} convert(f32[1024,256]{1,0:T(8,128)} %param.21) | non-fusion elementwise | flops 262144 | bytes 1572864 | tf_op jit(solution)/shard_map/convert_element_type | solution.py:437
  18.7 4.4 %collective-permute-done.2.rest_11_ = bf16[256,1280]{1,0:T(8,128)(2,1)} collective-permute-done((bf16[256,1280]{1,0:T(8,128)(2,1)}, bf16[256,1280]{1,0:T(8,128)(2,1)}, u32[]{:S(2)}, u32[]{:S(2)}) %collective-permute-start.2) | collective-permute-done | bytes 655392 | tf_op jit(solution)/shard_map/ppermute | solution.py:36
  23.1 4.6 %collective-permute-done.rest_8_ = bf16[256,1280]{1,0:T(8,128)(2,1)} collective-permute-done((bf16[256,1280]{1,0:T(8,128)(2,1)}, bf16[256,1280]{1,0:T(8,128)(2,1)}, u32[]{:S(2)}, u32[]{:S(2)}) %collective-permute-start) | collective-permute-done | bytes 655392 | tf_op jit(solution)/shard_map/ppermute | solution.py:54
  28.9 1.6 collective-permute-start.6
  30.5 1.3 collective-permute-start.8
  31.9 10.7 %collective-permute-done.13 = bf16[1024,256]{1,0:T(8,128)(2,1)S(1)} collective-permute-done((bf16[1024,256]{1,0:T(8,128)(2,1)}, bf16[1024,256]{1,0:T(8,128)(2,1)S(1)}, u32[]{:S(2)}, u32[]{:S(2)}) %collective-permute-start.13) | collective-permute-done | bytes 524320 | tf_op jit(solution)/shard_map/ppermute | solution.py:36
  44.9 1.5 collective-permute-start.15
  46.4 1.9 collective-permute-done.8
  49.0 5.3 %collective-permute-done.6.rest_12_ = bf16[256,1280]{1,0:T(8,128)(2,1)S(1)} collective-permute-done((bf16[256,1280]{1,0:T(8,128)(2,1)}, bf16[256,1280]{1,0:T(8,128)(2,1)S(1)}, u32[]{:S(2)}, u32[]{:S(2)}) %collective-permute-start.6) | collective-permute-done | bytes 655392 | tf_op jit(solution)/shard_map/ppermute | solution.py:36
  55.9 1.3 collective-permute-start.10
  58.6 7.2 %collective-permute-done.14.rest_1_ = bf16[1280,256]{1,0:T(8,128)(2,1)} collective-permute-done((bf16[1280,256]{1,0:T(8,128)(2,1)S(1)}, bf16[1280,256]{1,0:T(8,128)(2,1)}, u32[]{:S(2)}, u32[]{:S(2)}) %collective-permute-start.14) | collective-permute-done | bytes 655392 | tf_op jit(solution)/shard_map/ppermute | solution.py:54
  66.8 1.5 collective-permute-start.17
  68.3 1.5 collective-permute-done.9.rest_13_
  71.2 4.7 %collective-permute-done.10 = bf16[256,1280]{1,0:T(8,128)(2,1)S(1)} collective-permute-done((bf16[256,1280]{1,0:T(8,128)(2,1)S(1)}, bf16[256,1280]{1,0:T(8,128)(2,1)S(1)}, u32[]{:S(2)}, u32[]{:S(2)}) %collective-permute-start.10) | collective-permute-done | bytes 655392 | tf_op jit(solution)/shard_map/ppermute | solution.py:54
  75.9 1.3 collective-permute-start.18
  80.7 1.9 fusion.32
  83.7 7.3 %collective-permute-done.18 = bf16[1280,256]{1,0:T(8,128)(2,1)} collective-permute-done((bf16[1280,256]{1,0:T(8,128)(2,1)}, bf16[1280,256]{1,0:T(8,128)(2,1)}, u32[]{:S(2)}, u32[]{:S(2)}) %collective-permute-start.18) | collective-permute-done | bytes 655392 | tf_op jit(solution)/shard_map/ppermute | solution.py:54
  91.0 1.8 collective-permute-done.11.rest_14_
  92.8 4.5 %shard_map.168.own = bf16[2,1024,128]{2,1,0:T(8,128)(2,1)S(1)} custom-call(s32[14]{0:T(128)S(1)} %concatenate.47.meta, bf16[256,2048]{1,0:T(8,128)(2,1)} %fusion.17.rest_0_, bf16[256,2048]{1,0:T(8,128)(2,1)} %collective-permute-done.3.rest_1_, bf16[256,2048]{1,0:T(8,128)(2,1)} %collective-permute-done.4.rest_2_, ...), custom_call_target="tpu_custom_call" | custom-call | flops 4294967296 | bytes 4194304 | tf_op jit(solution)/shard_map/pallas_call | solution.py:226
  99.4 1.2 collective-permute-start.19
  100.6 1.5 collective-permute-start.20
  102.1 11.7 %shard_map.169.rest_0_ = bf16[8,1024,128]{2,1,0:T(8,128)(2,1)S(1)} custom-call(s32[14]{0:T(128)S(1)} %concatenate.47.meta, bf16[256,2048]{1,0:T(8,128)(2,1)} %fusion.17.rest_0_, bf16[256,2048]{1,0:T(8,128)(2,1)} %collective-permute-done.3.rest_1_, bf16[256,2048]{1,0:T(8,128)(2,1)} %collective-permute-done.4.rest_2_, ...), custom_call_target="tpu_custom_call" | custom-call | flops 17179869184 | bytes 4194304 | tf_op jit(solution)/shard_map/pallas_call | solution.py:226
  113.8 7.9 %shard_map.170.kept_rows.sent_rows = bf16[512,1024]{1,0:T(8,128)(2,1)S(1)} custom-call(s32[6]{0:T(128)S(1)} %pad_add_fusion.1.meta, bf16[2,1024,128]{2,1,0:T(8,128)(2,1)S(1)} %shard_map.168.own, bf16[2,1024,128]{2,1,0:T(8,128)(2,1)S(1)} %collective-permute-done.12.far, bf16[8,1024,128]{2,1,0:T(8,128)(2,1)S(1)} %shard_map.169.rest_0_), custom_call_target="tpu_custom_call" | custom-call | flops 8589934592 | bytes 524288 | tf_op jit(solution)/shard_map/pallas_call | solution.py:326
  122.8 8.1 %shard_map.171.sent_rows.kept_rows = bf16[512,1024]{1,0:T(8,128)(2,1)S(1)} custom-call(s32[6]{0:T(128)S(1)} %pad_add_fusion.1.meta, bf16[2,1024,128]{2,1,0:T(8,128)(2,1)S(1)} %shard_map.168.own, bf16[2,1024,128]{2,1,0:T(8,128)(2,1)S(1)} %collective-permute-done.12.far, bf16[8,1024,128]{2,1,0:T(8,128)(2,1)S(1)} %shard_map.169.rest_0_), custom_call_target="tpu_custom_call" | custom-call | flops 8589934592 | bytes 524288 | tf_op jit(solution)/shard_map/pallas_call | solution.py:326
  130.9 4.0 %shard_map.173 = (bf16[1,256,2048]{2,1,0:T(8,128)(2,1)S(1)}, bf16[1,256,2048]{2,1,0:T(8,128)(2,1)S(1)}) custom-call(s32[8]{0:T(128)S(1)} %pad_add_fusion.meta, bf16[512,1024]{1,0:T(8,128)(2,1)S(1)} %shard_map.171.sent_rows.kept_rows, bf16[512,1024]{1,0:T(8,128)(2,1)S(1)} %shard_map.170.kept_rows.sent_rows, bf16[1280,256]{1,0:T(8,128)(2,1)S(1)} %copy-done.8, ...), custom_call_target="tpu_custom_call" | custom-call | flops 6442450944 | bytes 4194304 | tf_op jit(solution)/shard_map/pallas_call | solution.py:370
  135.0 4.9 %shard_map.172 = (bf16[1,256,2048]{2,1,0:T(8,128)(2,1)S(1)}, bf16[1,256,2048]{2,1,0:T(8,128)(2,1)}) custom-call(s32[8]{0:T(128)S(1)} %pad_add_fusion.meta, bf16[512,1024]{1,0:T(8,128)(2,1)S(1)} %shard_map.170.kept_rows.sent_rows, bf16[512,1024]{1,0:T(8,128)(2,1)S(1)} %shard_map.171.sent_rows.kept_rows, bf16[1280,256]{1,0:T(8,128)(2,1)S(1)} %copy-done.8, ...), custom_call_target="tpu_custom_call" | custom-call | flops 6442450944 | bytes 4194304 | tf_op jit(solution)/shard_map/pallas_call | solution.py:370
  140.4 1.4 add_convert_fusion
  141.8 1.5 collective-permute-start.24
  145.4 21.7 %collective-permute-done.24 = bf16[1,256,2048]{2,1,0:T(8,128)(2,1)} collective-permute-done((bf16[1,256,2048]{2,1,0:T(8,128)(2,1)}, bf16[1,256,2048]{2,1,0:T(8,128)(2,1)}, u32[]{:S(2)}, u32[]{:S(2)}) %collective-permute-start.24) | collective-permute-done | bytes 1048608 | tf_op jit(solution)/shard_map/ppermute | solution.py:36
  167.2 1.2 copy-done.2
  169.6 3.8 %shard_map.174 = (bf16[256,2048]{1,0:T(8,128)(2,1)}, bf16[256,2048]{1,0:T(8,128)(2,1)S(1)}) custom-call(bf16[256,2048]{1,0:T(8,128)(2,1)S(1)} %copy-done.2, f32[1,2048]{1,0:T(1,128)S(1)} %bitcast.59, bf16[256,2048]{1,0:T(8,128)(2,1)S(1)} %bitcast.58, bf16[256,2048]{1,0:T(8,128)(2,1)} %bitcast.7.rest_1_, bf16[256,2048]{1,0:T(8,128)(2,1)} %bitcast.8.rest_2_), custom_call_target="tpu_custom_call" | custom-call | tf_op jit(solution)/shard_map/pallas_call | solution.py:399
  173.9 1.6 collective-permute-start.25
  176.0 5.4 %collective-permute-done.25 = bf16[64,2048]{1,0:T(8,128)(2,1)S(1)} collective-permute-done((bf16[64,2048]{1,0:T(8,128)(2,1)S(1)}, bf16[64,2048]{1,0:T(8,128)(2,1)S(1)}, u32[]{:S(2)}, u32[]{:S(2)}) %collective-permute-start.25) | collective-permute-done | bytes 262176 | tf_op jit(solution)/shard_map/ppermute | solution.py:36
  181.5 1.6 collective-permute-start.27
  183.1 4.0 %fusion = f32[64,1536]{1,0:T(8,128)S(1)} fusion(bf16[64,2048]{1,0:T(8,128)(2,1)S(1)} %collective-permute-done.25, bf16[1,2048,1536]{2,1,0:T(8,128)(2,1)} %param.26), kind=kOutput, calls=%fused_computation | convolution fusion | flops 402653184 | bytes 6946816 | tf_op jit(solution)/shard_map/dot_general | solution.py:538
  188.4 1.6 collective-permute-done.26
  190.0 1.4 fusion.2
  194.4 2.5 %collective-permute-done.28 = bf16[64,2048]{1,0:T(8,128)(2,1)S(1)} collective-permute-done((bf16[64,2048]{1,0:T(8,128)(2,1)S(1)}, bf16[64,2048]{1,0:T(8,128)(2,1)S(1)}, u32[]{:S(2)}, u32[]{:S(2)}) %collective-permute-start.28) | collective-permute-done | bytes 262176 | tf_op jit(solution)/shard_map/ppermute | solution.py:36
  196.9 4.2 %collective-permute-done.30 = bf16[64,2048]{1,0:T(8,128)(2,1)S(1)} collective-permute-done((bf16[64,2048]{1,0:T(8,128)(2,1)S(1)}, bf16[64,2048]{1,0:T(8,128)(2,1)S(1)}, u32[]{:S(2)}, u32[]{:S(2)}) %collective-permute-start.30) | collective-permute-done | bytes 262176 | tf_op jit(solution)/shard_map/ppermute | solution.py:36
  201.2 1.5 fusion.8
  (151 shorter events, 27.3 us)
Async XLA Ops:
  0.6 186.5 %copy-start = (bf16[1,768,2048]{2,1,0:T(8,128)(2,1)S(1)}, bf16[1,768,2048]{2,1,0:T(8,128)(2,1)}, u32[]{:S(2)}) copy-start(bf16[1,768,2048]{2,1,0:T(8,128)(2,1)} %param.27) | copy-start | bytes 9437188
  0.6 12.8 %copy-start.21 = (f32[2048]{0:T(1024)S(1)}, f32[2048]{0:T(1024)}, u32[]{:S(2)}) copy-start(f32[2048]{0:T(1024)} %param.17) | copy-start | bytes 24580
  0.7 12.5 %copy-start.1 = (bf16[256,2048]{1,0:T(8,128)(2,1)S(1)}, bf16[256,2048]{1,0:T(8,128)(2,1)}, u32[]{:S(2)}) copy-start(bf16[256,2048]{1,0:T(8,128)(2,1)} %states.1) | copy-start | bytes 3145732
  5.1 11.2 %copy-start.27 = (s32[4]{0:T(128)S(1)}, s32[4]{0:T(128)}, u32[]{:S(2)}) copy-start(s32[4]{0:T(128)} %constant.111.clone) | copy-start | bytes 52
  5.1 18.0 %collective-permute-start.2 = (bf16[256,1280]{1,0:T(8,128)(2,1)}, bf16[256,1280]{1,0:T(8,128)(2,1)}, u32[]{:S(2)}, u32[]{:S(2)}) collective-permute-start(bf16[256,1280]{1,0:T(8,128)(2,1)} %shard_map.167.rest_7_), channel_id=1, source_target_pairs={{0,4},{4,0},{8,12},{12,8},{16,20},{20,16},{24,28},{28,24},{1,5},{5... | collective-permute-start | bytes 1966088 | tf_op jit(solution)/shard_map/ppermute | solution.py:36
  8.0 15.0 %collective-permute-start.1 = (bf16[256,1280]{1,0:T(8,128)(2,1)}, bf16[256,1280]{1,0:T(8,128)(2,1)}, u32[]{:S(2)}, u32[]{:S(2)}) collective-permute-start(bf16[256,1280]{1,0:T(8,128)(2,1)} %shard_map.167.rest_7_), channel_id=1, source_target_pairs={{8,16},{12,20},{16,8},{20,12},{9,17},{13,21},{17,9},{21,13},{10,18... | collective-permute-start | bytes 1966088 | tf_op jit(solution)/shard_map/ppermute | solution.py:54
  9.5 18.1 %collective-permute-start = (bf16[256,1280]{1,0:T(8,128)(2,1)}, bf16[256,1280]{1,0:T(8,128)(2,1)}, u32[]{:S(2)}, u32[]{:S(2)}) collective-permute-start(bf16[256,1280]{1,0:T(8,128)(2,1)} %shard_map.167.rest_7_), channel_id=1, source_target_pairs={{0,8},{4,12},{8,0},{12,4},{16,24},{20,28},{24,16},{28,20},{1,9},{5... | collective-permute-start | bytes 1966088 | tf_op jit(solution)/shard_map/ppermute | solution.py:54
  13.4 5.1 %copy-start.25 = (f32[128]{0:T(128)S(1)}, f32[128]{0:T(128)}, u32[]{:S(2)}) copy-start(f32[128]{0:T(128)} %param.22) | copy-start | bytes 1540
  13.4 18.4 %copy-start.23 = (f32[128]{0:T(128)S(1)}, f32[128]{0:T(128)}, u32[]{:S(2)}) copy-start(f32[128]{0:T(128)} %param.23) | copy-start | bytes 1540
  14.8 43.3 %collective-permute-start.3 = (bf16[256,2048]{1,0:T(8,128)(2,1)}, bf16[256,2048]{1,0:T(8,128)(2,1)}, u32[]{:S(2)}, u32[]{:S(2)}) collective-permute-start(bf16[256,2048]{1,0:T(8,128)(2,1)} %fusion.17.rest_0_), channel_id=1, source_target_pairs={{0,2},{1,3},{2,0},{3,1},{4,6},{5,7},{6,4},{7,5},{8,10},{9,11},{10,... | collective-permute-start | bytes 3145736 | tf_op jit(solution)/shard_map/ppermute | solution.py:36
  27.6 15.1 %collective-permute-start.13 = (bf16[1024,256]{1,0:T(8,128)(2,1)}, bf16[1024,256]{1,0:T(8,128)(2,1)S(1)}, u32[]{:S(2)}, u32[]{:S(2)}) collective-permute-start(bf16[1024,256]{1,0:T(8,128)(2,1)} %convert_element_type.62), channel_id=1, source_target_pairs={{0,4},{4,0},{8,12},{12,8},{16,20},{20,16},{24,28},{28,24},{1,5},{5... | collective-permute-start | bytes 1572872 | tf_op jit(solution)/shard_map/ppermute | solution.py:36
  28.2 20.8 %collective-permute-start.7 = (bf16[256,1280]{1,0:T(8,128)(2,1)}, bf16[256,1280]{1,0:T(8,128)(2,1)S(1)}, u32[]{:S(2)}, u32[]{:S(2)}) collective-permute-start(bf16[256,1280]{1,0:T(8,128)(2,1)} %collective-permute-done.rest_8_), channel_id=1, source_target_pairs={{8,16},{12,20},{16,8},{20,12},{9,17},{13,21},{17,9},{21,13},{10,18... | collective-permute-start | bytes 1966088 | tf_op jit(solution)/shard_map/ppermute | solution.py:54
  28.9 25.4 %collective-permute-start.6 = (bf16[256,1280]{1,0:T(8,128)(2,1)}, bf16[256,1280]{1,0:T(8,128)(2,1)S(1)}, u32[]{:S(2)}, u32[]{:S(2)}) collective-permute-start(bf16[256,1280]{1,0:T(8,128)(2,1)} %collective-permute-done.rest_8_), channel_id=1, source_target_pairs={{0,4},{4,0},{8,12},{12,8},{16,20},{20,16},{24,28},{28,24},{1,5},{5... | collective-permute-start | bytes 1966088 | tf_op jit(solution)/shard_map/ppermute | solution.py:36
  30.5 17.7 %collective-permute-start.8 = (bf16[256,1280]{1,0:T(8,128)(2,1)}, bf16[256,1280]{1,0:T(8,128)(2,1)S(1)}, u32[]{:S(2)}, u32[]{:S(2)}) collective-permute-start(bf16[256,1280]{1,0:T(8,128)(2,1)} %collective-permute-done.1), channel_id=1, source_target_pairs={{8,0},{12,4},{16,24},{20,28},{9,1},{13,5},{17,25},{21,29},{10,2},{... | collective-permute-start | bytes 1966088 | tf_op jit(solution)/shard_map/ppermute | solution.py:54
  43.7 13.5 %copy-start.26 = (s32[4]{0:T(128)S(1)}, s32[4]{0:T(128)}, u32[]{:S(2)}) copy-start(s32[4]{0:T(128)} %param.24) | copy-start | bytes 52
  44.9 33.3 %copy-start.7 = (bf16[1280,256]{1,0:T(8,128)(2,1)}, bf16[1280,256]{1,0:T(8,128)(2,1)S(1)}, u32[]{:S(2)}) copy-start(bf16[1280,256]{1,0:T(8,128)(2,1)S(1)} %pad_maximum_fusion.1.rest_0_) | copy-start | bytes 1966084
  44.9 13.3 %collective-permute-start.15 = (bf16[1280,256]{1,0:T(8,128)(2,1)S(1)}, bf16[1280,256]{1,0:T(8,128)(2,1)}, u32[]{:S(2)}, u32[]{:S(2)}) collective-permute-start(bf16[1280,256]{1,0:T(8,128)(2,1)S(1)} %pad_maximum_fusion.1.rest_0_), channel_id=1, source_target_pairs={{8,16},{12,20},{16,8},{20,12},{9,17},{13,21},{17,9},{21,13},{10,18... | collective-permute-start | bytes 1966088 | tf_op jit(solution)/shard_map/ppermute | solution.py:54
  48.2 17.6 %collective-permute-start.14 = (bf16[1280,256]{1,0:T(8,128)(2,1)S(1)}, bf16[1280,256]{1,0:T(8,128)(2,1)}, u32[]{:S(2)}, u32[]{:S(2)}) collective-permute-start(bf16[1280,256]{1,0:T(8,128)(2,1)S(1)} %pad_maximum_fusion.1.rest_0_), channel_id=1, source_target_pairs={{0,8},{4,12},{8,0},{12,4},{16,24},{20,28},{24,16},{28,20},{1,9},{5... | collective-permute-start | bytes 1966088 | tf_op jit(solution)/shard_map/ppermute | solution.py:54
  55.3 23.7 %copy-start.9 = (bf16[256,1280]{1,0:T(8,128)(2,1)}, bf16[256,1280]{1,0:T(8,128)(2,1)S(1)}, u32[]{:S(2)}) copy-start(bf16[256,1280]{1,0:T(8,128)(2,1)S(1)} %broadcast_select_fusion.3.rest_9_) | copy-start | bytes 1966084
  55.3 14.5 %collective-permute-start.9 = (bf16[256,1280]{1,0:T(8,128)(2,1)S(1)}, bf16[256,1280]{1,0:T(8,128)(2,1)S(1)}, u32[]{:S(2)}, u32[]{:S(2)}) collective-permute-start(bf16[256,1280]{1,0:T(8,128)(2,1)S(1)} %broadcast_select_fusion.3.rest_9_), channel_id=1, source_target_pairs={{0,4},{4,0},{8,12},{12,8},{16,20},{20,16},{24,28},{28,24},{1,5},{5... | collective-permute-start | bytes 1966088 | tf_op jit(solution)/shard_map/ppermute | solution.py:36
  55.9 20.0 %collective-permute-start.10 = (bf16[256,1280]{1,0:T(8,128)(2,1)S(1)}, bf16[256,1280]{1,0:T(8,128)(2,1)S(1)}, u32[]{:S(2)}, u32[]{:S(2)}) collective-permute-start(bf16[256,1280]{1,0:T(8,128)(2,1)S(1)} %collective-permute-done.7), channel_id=1, source_target_pairs={{8,0},{12,4},{16,24},{20,28},{9,1},{13,5},{17,25},{21,29},{10,2},{... | collective-permute-start | bytes 1966088 | tf_op jit(solution)/shard_map/ppermute | solution.py:54
  58.0 34.7 %collective-permute-start.4 = (bf16[256,2048]{1,0:T(8,128)(2,1)}, bf16[256,2048]{1,0:T(8,128)(2,1)}, u32[]{:S(2)}, u32[]{:S(2)}) collective-permute-start(bf16[256,2048]{1,0:T(8,128)(2,1)} %fusion.17.rest_0_), channel_id=1, source_target_pairs={{0,1},{1,0},{2,3},{3,2},{4,5},{5,4},{6,7},{7,6},{8,9},{9,8},{10,11... | collective-permute-start | bytes 3145736 | tf_op jit(solution)/shard_map/ppermute | solution.py:36
  58.1 34.6 %collective-permute-start.5 = (bf16[256,2048]{1,0:T(8,128)(2,1)}, bf16[256,2048]{1,0:T(8,128)(2,1)}, u32[]{:S(2)}, u32[]{:S(2)}) collective-permute-start(bf16[256,2048]{1,0:T(8,128)(2,1)} %collective-permute-done.3.rest_1_), channel_id=1, source_target_pairs={{0,1},{1,0},{2,3},{3,2},{4,5},{5,4},{6,7},{7,6},{8,9},{9,8},{10,11... | collective-permute-start | bytes 3145736 | tf_op jit(solution)/shard_map/ppermute | solution.py:36
  66.8 24.2 %collective-permute-start.17 = (bf16[1280,256]{1,0:T(8,128)(2,1)}, bf16[1280,256]{1,0:T(8,128)(2,1)}, u32[]{:S(2)}, u32[]{:S(2)}) collective-permute-start(bf16[1280,256]{1,0:T(8,128)(2,1)} %collective-permute-done.14.rest_1_), channel_id=1, source_target_pairs={{8,16},{12,20},{16,8},{20,12},{9,17},{13,21},{17,9},{21,13},{10,18... | collective-permute-start | bytes 1966088 | tf_op jit(solution)/shard_map/ppermute | solution.py:54
  70.7 8.3 %collective-permute-start.16 = (bf16[768,256]{1,0:T(8,128)(2,1)S(1)}, bf16[768,256]{1,0:T(8,128)(2,1)S(1)}, u32[]{:S(2)}, u32[]{:S(2)}) collective-permute-start(bf16[768,256]{1,0:T(8,128)(2,1)S(1)} %slice.81), channel_id=1, source_target_pairs={{0,4},{4,0},{8,12},{12,8},{16,20},{20,16},{24,28},{28,24},{1,5},{5... | collective-permute-start | bytes 1179656 | tf_op jit(solution)/shard_map/ppermute | solution.py:36
  75.9 15.1 %collective-permute-start.18 = (bf16[1280,256]{1,0:T(8,128)(2,1)}, bf16[1280,256]{1,0:T(8,128)(2,1)}, u32[]{:S(2)}, u32[]{:S(2)}) collective-permute-start(bf16[1280,256]{1,0:T(8,128)(2,1)} %collective-permute-done.15), channel_id=1, source_target_pairs={{8,0},{12,4},{16,24},{20,28},{9,1},{13,5},{17,25},{21,29},{10,2},{... | collective-permute-start | bytes 1966088 | tf_op jit(solution)/shard_map/ppermute | solution.py:54
  79.7 13.0 %collective-permute-start.11 = (bf16[256,1280]{1,0:T(8,128)(2,1)}, bf16[256,1280]{1,0:T(8,128)(2,1)}, u32[]{:S(2)}, u32[]{:S(2)}) collective-permute-start(bf16[256,1280]{1,0:T(8,128)(2,1)} %broadcast_select_fusion.2.rest_10_), channel_id=1, source_target_pairs={{0,4},{4,0},{8,12},{12,8},{16,20},{20,16},{24,28},{28,24},{1,5},{5... | collective-permute-start | bytes 1966088 | tf_op jit(solution)/shard_map/ppermute | solution.py:36
  82.6 10.2 %copy-start.10 = (bf16[256,1280]{1,0:T(8,128)(2,1)S(1)}, bf16[256,1280]{1,0:T(8,128)(2,1)}, u32[]{:S(2)}) copy-start(bf16[256,1280]{1,0:T(8,128)(2,1)} %copy-done.9) | copy-start | bytes 1966084
  82.6 10.2 %copy-start.13 = (bf16[256,1280]{1,0:T(8,128)(2,1)S(1)}, bf16[256,1280]{1,0:T(8,128)(2,1)}, u32[]{:S(2)}) copy-start(bf16[256,1280]{1,0:T(8,128)(2,1)} %copy-done.12) | copy-start | bytes 1966084
  82.6 10.2 %copy-start.15 = (bf16[256,1280]{1,0:T(8,128)(2,1)S(1)}, bf16[256,1280]{1,0:T(8,128)(2,1)}, u32[]{:S(2)}) copy-start(bf16[256,1280]{1,0:T(8,128)(2,1)} %copy-done.14) | copy-start | bytes 1966084
  97.3 16.5 %collective-permute-start.12 = (bf16[2,1024,128]{2,1,0:T(8,128)(2,1)S(1)}, bf16[2,1024,128]{2,1,0:T(8,128)(2,1)S(1)}, u32[]{:S(2)}, u32[]{:S(2)}) collective-permute-start(bf16[2,1024,128]{2,1,0:T(8,128)(2,1)S(1)} %shard_map.168.own), channel_id=1, source_target_pairs={{0,4},{4,0},{8,12},{12,8},{16,20},{20,16},{24,28},{28,24},{1,5},{5... | collective-permute-start | bytes 1572872 | tf_op jit(solution)/shard_map/ppermute | solution.py:36
  99.4 22.3 %collective-permute-start.19 = (bf16[768,256]{1,0:T(8,128)(2,1)S(1)}, bf16[768,256]{1,0:T(8,128)(2,1)S(1)}, u32[]{:S(2)}, u32[]{:S(2)}) collective-permute-start(bf16[768,256]{1,0:T(8,128)(2,1)S(1)} %slice.100), channel_id=1, source_target_pairs={{0,4},{4,0},{8,12},{12,8},{16,20},{20,16},{24,28},{28,24},{1,5},{5... | collective-permute-start | bytes 1179656 | tf_op jit(solution)/shard_map/ppermute | solution.py:36
  100.6 21.1 %collective-permute-start.20 = (bf16[1280,256]{1,0:T(8,128)(2,1)}, bf16[1280,256]{1,0:T(8,128)(2,1)S(1)}, u32[]{:S(2)}, u32[]{:S(2)}) collective-permute-start(bf16[1280,256]{1,0:T(8,128)(2,1)} %collective-permute-done.17), channel_id=1, source_target_pairs={{8,0},{12,4},{16,24},{20,28},{9,1},{13,5},{17,25},{21,29},{10,2},{... | collective-permute-start | bytes 1966088 | tf_op jit(solution)/shard_map/ppermute | solution.py:54
  121.9 9.0 %copy-start.8 = (bf16[1280,256]{1,0:T(8,128)(2,1)S(1)}, bf16[1280,256]{1,0:T(8,128)(2,1)}, u32[]{:S(2)}) copy-start(bf16[1280,256]{1,0:T(8,128)(2,1)} %copy-done.7) | copy-start | bytes 1966084
  121.9 9.0 %copy-start.17 = (bf16[768,256]{1,0:T(8,128)(2,1)S(1)}, bf16[768,256]{1,0:T(8,128)(2,1)}, u32[]{:S(2)}) copy-start(bf16[768,256]{1,0:T(8,128)(2,1)} %copy-done.16) | copy-start | bytes 1179652
  121.9 9.0 %collective-permute-start.21 = (bf16[768,256]{1,0:T(8,128)(2,1)S(1)}, bf16[768,256]{1,0:T(8,128)(2,1)S(1)}, u32[]{:S(2)}, u32[]{:S(2)}) collective-permute-start(bf16[768,256]{1,0:T(8,128)(2,1)S(1)} %slice.101), channel_id=1, source_target_pairs={{0,4},{4,0},{8,12},{12,8},{16,20},{20,16},{24,28},{28,24},{1,5},{5... | collective-permute-start | bytes 1179656 | tf_op jit(solution)/shard_map/ppermute | solution.py:36
  134.9 5.5 %collective-permute-start.23 = (bf16[1,256,2048]{2,1,0:T(8,128)(2,1)S(1)}, bf16[1,256,2048]{2,1,0:T(8,128)(2,1)S(1)}, u32[]{:S(2)}, u32[]{:S(2)}) collective-permute-start(bf16[1,256,2048]{2,1,0:T(8,128)(2,1)S(1)} %get-tuple-element.75), channel_id=1, source_target_pairs={{0,1},{1,0},{2,3},{3,2},{4,5},{5,4},{6,7},{7,6},{8,9},{9,8},{10,11... | collective-permute-start | bytes 3145736 | tf_op jit(solution)/shard_map/ppermute | solution.py:36
  139.9 27.3 %copy-start.11 = (f32[2048]{0:T(1024)S(1)}, f32[2048]{0:T(1024)}, u32[]{:S(2)}) copy-start(f32[2048]{0:T(1024)} %param.18) | copy-start | bytes 24580
  139.9 5.5 %collective-permute-start.22 = (bf16[1,256,2048]{2,1,0:T(8,128)(2,1)}, bf16[1,256,2048]{2,1,0:T(8,128)(2,1)}, u32[]{:S(2)}, u32[]{:S(2)}) collective-permute-start(bf16[1,256,2048]{2,1,0:T(8,128)(2,1)} %get-tuple-element.73), channel_id=1, source_target_pairs={{0,1},{1,0},{2,3},{3,2},{4,5},{5,4},{6,7},{7,6},{8,9},{9,8},{10,11... | collective-permute-start | bytes 3145736 | tf_op jit(solution)/shard_map/ppermute | solution.py:36
  141.8 25.4 %collective-permute-start.24 = (bf16[1,256,2048]{2,1,0:T(8,128)(2,1)}, bf16[1,256,2048]{2,1,0:T(8,128)(2,1)}, u32[]{:S(2)}, u32[]{:S(2)}) collective-permute-start(bf16[1,256,2048]{2,1,0:T(8,128)(2,1)} %add_convert_fusion), channel_id=1, source_target_pairs={{0,2},{1,3},{2,0},{3,1},{4,6},{5,7},{6,4},{7,5},{8,10},{9,11},{10,... | collective-permute-start | bytes 3145736 | tf_op jit(solution)/shard_map/ppermute | solution.py:36
  173.9 7.4 %collective-permute-start.25 = (bf16[64,2048]{1,0:T(8,128)(2,1)S(1)}, bf16[64,2048]{1,0:T(8,128)(2,1)S(1)}, u32[]{:S(2)}, u32[]{:S(2)}) collective-permute-start(bf16[64,2048]{1,0:T(8,128)(2,1)S(1)} %get-tuple-element.82), channel_id=1, source_target_pairs={{0,2},{1,3},{2,0},{3,1},{4,6},{5,7},{6,4},{7,5},{8,10},{9,11},{10,... | collective-permute-start | bytes 786440 | tf_op jit(solution)/shard_map/ppermute | solution.py:36
  175.5 14.5 %slice-start = ((s8[6291456]{0:T(1024)(128)(4,1)}), s8[4194304]{0:T(1024)(128)(4,1)S(1)}, s32[]{:S(2)}) async-start(s8[6291456]{0:T(1024)(128)(4,1)} %bitcast.60), calls=%async_computation | async-start | bytes 8388608
  181.4 8.6 %collective-permute-start.26 = (bf16[64,2048]{1,0:T(8,128)(2,1)S(1)}, bf16[64,2048]{1,0:T(8,128)(2,1)S(1)}, u32[]{:S(2)}, u32[]{:S(2)}) collective-permute-start(bf16[64,2048]{1,0:T(8,128)(2,1)S(1)} %get-tuple-element.80), channel_id=1, source_target_pairs={{0,3},{1,2},{2,1},{3,0},{4,7},{5,6},{6,5},{7,4},{8,11},{9,10},{10,... | collective-permute-start | bytes 786440 | tf_op jit(solution)/shard_map/ppermute | solution.py:36
  181.5 8.5 %slice-start.1 = ((s8[6291456]{0:T(1024)(128)(4,1)}), s8[2097152]{0:T(1024)(128)(4,1)S(1)}, s32[]{:S(2)}) async-start(s8[6291456]{0:T(1024)(128)(4,1)} %bitcast.60), calls=%async_computation.1 | async-start | bytes 4194304
  181.5 8.5 %collective-permute-start.27 = (bf16[64,2048]{1,0:T(8,128)(2,1)S(1)}, bf16[64,2048]{1,0:T(8,128)(2,1)S(1)}, u32[]{:S(2)}, u32[]{:S(2)}) collective-permute-start(bf16[64,2048]{1,0:T(8,128)(2,1)S(1)} %get-tuple-element.81), channel_id=1, source_target_pairs={{0,1},{1,0},{2,3},{3,2},{4,5},{5,4},{6,7},{7,6},{8,9},{9,8},{10,11... | collective-permute-start | bytes 786440 | tf_op jit(solution)/shard_map/ppermute | solution.py:36
  187.8 9.1 %collective-permute-start.28 = (bf16[64,2048]{1,0:T(8,128)(2,1)S(1)}, bf16[64,2048]{1,0:T(8,128)(2,1)S(1)}, u32[]{:S(2)}, u32[]{:S(2)}) collective-permute-start(bf16[64,2048]{1,0:T(8,128)(2,1)S(1)} %fusion.12), channel_id=1, source_target_pairs={{0,2},{1,3},{2,0},{3,1},{4,6},{5,7},{6,4},{7,5},{8,10},{9,11},{10,... | collective-permute-start | bytes 786440 | tf_op jit(solution)/shard_map/ppermute | solution.py:36
  192.4 8.7 %collective-permute-start.30 = (bf16[64,2048]{1,0:T(8,128)(2,1)S(1)}, bf16[64,2048]{1,0:T(8,128)(2,1)S(1)}, u32[]{:S(2)}, u32[]{:S(2)}) collective-permute-start(bf16[64,2048]{1,0:T(8,128)(2,1)S(1)} %get-tuple-element.87), channel_id=1, source_target_pairs={{0,3},{1,2},{2,1},{3,0},{4,7},{5,6},{6,5},{7,4},{8,11},{9,10},{10,... | collective-permute-start | bytes 786440 | tf_op jit(solution)/shard_map/ppermute | solution.py:36
  192.4 8.7 %collective-permute-start.29 = (bf16[64,2048]{1,0:T(8,128)(2,1)S(1)}, bf16[64,2048]{1,0:T(8,128)(2,1)S(1)}, u32[]{:S(2)}, u32[]{:S(2)}) collective-permute-start(bf16[64,2048]{1,0:T(8,128)(2,1)S(1)} %get-tuple-element.88), channel_id=1, source_target_pairs={{0,1},{1,0},{2,3},{3,2},{4,5},{5,4},{6,7},{7,6},{8,9},{9,8},{10,11... | collective-permute-start | bytes 786440 | tf_op jit(solution)/shard_map/ppermute | solution.py:36
  (13 other events, 23.3 us)
